TPU v7x, 256 devices: a whole 4x4x8 slice. The times are simulated.
256 devices in a mesh: dcn: 2 (over core), gx: 8 (over z_lo, y), gy: 4 (over z_hi), gz: 4 (over x).
Axes of the slice: x: 4, y: 4, z: 8 (z_hi: 4, z_lo: 2; z = z_hi * 2 + z_lo), core: 2. Of those that a mesh axis runs over, the one named last changes fastest.
Arguments:
- tokens: bfloat16 [512, 8192], P(('dcn', 'gx', 'gz'), 'gy'), may hold values from -6 to 6
- gate_weight: bfloat16 [28672, 8192], P(('dcn', 'gx', 'gz'), 'gy'), may hold values from -0.0625 to 0.0625
- up_weight: bfloat16 [28672, 8192], P(('dcn', 'gx', 'gz'), 'gy'), may hold values from -0.0625 to 0.0625
- down_weight: bfloat16 [28672, 8192], P(('dcn', 'gx', 'gz'), 'gy'), may hold values from -0.03125 to 0.03125
- out_grad: bfloat16 [512, 8192], P(('dcn', 'gx', 'gz'), 'gy'), may hold values from -6 to 6
Outputs:
- output: bfloat16 [512, 8192], P(('dcn', 'gx', 'gz'), 'gy')
- tokens_grad: bfloat16 [512, 8192], P(('dcn', 'gx', 'gz'), 'gy')
- gate_grad: bfloat16 [28672, 8192], P(('dcn', 'gx', 'gz'), 'gy')
- up_grad: bfloat16 [28672, 8192], P(('dcn', 'gx', 'gz'), 'gy')
- down_grad: bfloat16 [28672, 8192], P(('dcn', 'gx', 'gz'), 'gy')
All inputs are finite; a program needn't handle non-finite values.
Results may differ from a plain program's by a relative error of at most 0.0054.
Values may be sent and summed in bfloat16 or wider, within the bound.
No kernel may reach another device: no remote copies, remote signals or barrier semaphores. Data moves between devices by JAX's collectives and lax.ppermute only.
A program may use at most 128 MiB of HBM per device.

v0:
```python
import math

import jax
import jax.numpy as jnp
from jax import lax
from jax.sharding import PartitionSpec as P


def by_features(left, right):
    return lax.dot_general(
        left, right, (((1,), (1,)), ((), ())), preferred_element_type=jnp.float32
    )


def by_tokens(left, right):
    return lax.dot_general(
        left, right, (((0,), (0,)), ((), ())), preferred_element_type=jnp.float32
    )


def per_device(tokens, gate_weight, up_weight, down_weight, out_grad):
    shard_rows = tokens.shape[0]
    token_count = shard_rows * lax.axis_size("dcn") * lax.axis_size("gx") * lax.axis_size("gz")
    factor = 1.0 / math.sqrt(token_count)
    token_rows, grad_rows = (
        lax.all_gather(tokens, ("gx", "gz"), axis=0, tiled=True),
        lax.all_gather(out_grad, ("gx", "gz"), axis=0, tiled=True),
    )
    w_gate, w_up, w_down = (
        lax.all_gather(gate_weight, "dcn", axis=0, tiled=True),
        lax.all_gather(up_weight, "dcn", axis=0, tiled=True),
        lax.all_gather(down_weight, "dcn", axis=0, tiled=True),
    )
    gate_part = by_features(token_rows, w_gate)
    up_part = by_features(token_rows, w_up)
    gate_total, up_total = (
        lax.psum_scatter(gate_part, "gy", scatter_dimension=0, tiled=True),
        lax.psum_scatter(up_part, "gy", scatter_dimension=0, tiled=True),
    )
    sigmoid_gate = jax.nn.sigmoid(gate_total)
    hidden = (gate_total * sigmoid_gate * up_total).astype(jnp.bfloat16)
    hidden_all = lax.all_gather(hidden, "gy", axis=0, tiled=True)
    output = lax.psum_scatter(
        jnp.dot(hidden_all, w_down, preferred_element_type=jnp.float32),
        ("gx", "gz"),
        scatter_dimension=0,
        tiled=True,
    )
    output = output.astype(jnp.bfloat16)
    hgrad_part = by_features(grad_rows, w_down)
    hidden_grad = lax.psum_scatter(hgrad_part, "gy", scatter_dimension=0, tiled=True)
    gate_delta = (
        hidden_grad * up_total * sigmoid_gate * (1.0 + gate_total * (1.0 - sigmoid_gate))
    ).astype(jnp.bfloat16)
    up_delta = (hidden_grad * gate_total * sigmoid_gate).astype(jnp.bfloat16)
    gate_rows, up_rows = (
        lax.all_gather(gate_delta, "gy", axis=0, tiled=True),
        lax.all_gather(up_delta, "gy", axis=0, tiled=True),
    )
    tokens_grad = lax.psum_scatter(
        jnp.dot(gate_rows, w_gate, preferred_element_type=jnp.float32)
        + jnp.dot(up_rows, w_up, preferred_element_type=jnp.float32),
        ("gx", "gz"),
        scatter_dimension=0,
        tiled=True,
    )
    tokens_grad = tokens_grad.astype(jnp.bfloat16)
    gate_grad = by_tokens(gate_rows, token_rows)
    up_grad = by_tokens(up_rows, token_rows)
    down_grad = by_tokens(hidden_all, grad_rows)
    gate_grad, up_grad, down_grad = (
        lax.psum_scatter(gate_grad, "dcn", scatter_dimension=0, tiled=True),
        lax.psum_scatter(up_grad, "dcn", scatter_dimension=0, tiled=True),
        lax.psum_scatter(down_grad, "dcn", scatter_dimension=0, tiled=True),
    )
    return (
        output,
        tokens_grad,
        (gate_grad * factor).astype(jnp.bfloat16),
        (up_grad * factor).astype(jnp.bfloat16),
        (down_grad * factor).astype(jnp.bfloat16),
    )


def solution(mesh):
    placed = (
        P(("dcn", "gx", "gz"), "gy"),
        P(("dcn", "gx", "gz"), "gy"),
        P(("dcn", "gx", "gz"), "gy"),
        P(("dcn", "gx", "gz"), "gy"),
        P(("dcn", "gx", "gz"), "gy"),
    )
    return jax.shard_map(
        per_device,
        mesh=mesh,
        in_specs=placed,
        out_specs=(
            P(("dcn", "gx", "gz"), "gy"),
            P(("dcn", "gx", "gz"), "gy"),
            P(("dcn", "gx", "gz"), "gy"),
            P(("dcn", "gx", "gz"), "gy"),
            P(("dcn", "gx", "gz"), "gy"),
        ),
        check_vma=False,
    )
```

profile of v0, /device:TPU:1, one launch (start us, length us, event | category | flops | bytes accessed | tf_op | source)
XLA Modules:
  0.0 922.6 jit_solution(7216687863876340269)
XLA Ops:
  7.2 0.7 all-gather.14.cloned.1.call-update
  7.9 0.0 all-gather.12.cloned.1.call-start
  7.9 0.7 all-gather.12.cloned.1.call-update
  8.6 0.0 all-gather.6.cloned.1.call-start
  8.7 0.7 all-gather.6.cloned.1.call-update
  9.4 0.0 all-gather.8.cloned.1.call-start
  9.4 0.5 all-gather.8.cloned.1.call-update
  10.0 0.5 all-gather.10.cloned.1.call-update
  10.5 0.0 reduce-scatter.15.cloned.1.call-start
  10.6 135.1 %all-gather.14.cloned.1.call-done = bf16[256,2048]{1,0:T(8,128)(2,1)} async-done(((bf16[8,2048]{1,0:T(8,128)(2,1)}), bf16[256,2048]{1,0:T(8,128)(2,1)}) %all-gather.14.cloned.1.call-update) | async-done | bytes 1048592 | tf_op jit(solution)/shard_map/all_gather | solution.py:27
  145.6 42.6 %all-gather.12.cloned.1.call-done = bf16[896,2048]{1,0:T(8,128)(2,1)} async-done(((bf16[448,2048]{1,0:T(8,128)(2,1)}), bf16[896,2048]{1,0:T(8,128)(2,1)}) %all-gather.12.cloned.1.call-update) | async-done | bytes 3670032 | tf_op jit(solution)/shard_map/all_gather | solution.py:32
  188.2 4.6 fusion.3
  192.8 0.0 reduce-scatter.9.cloned.1.call-start
  192.9 129.8 %all-gather.6.cloned.1.call-done = bf16[256,2048]{1,0:T(8,128)(2,1)} async-done(((bf16[8,2048]{1,0:T(8,128)(2,1)}), bf16[256,2048]{1,0:T(8,128)(2,1)}) %all-gather.6.cloned.1.call-update) | async-done | bytes 1048592 | tf_op jit(solution)/shard_map/all_gather | solution.py:26
  322.6 42.4 %all-gather.8.cloned.1.call-done = bf16[896,2048]{1,0:T(8,128)(2,1)} async-done(((bf16[448,2048]{1,0:T(8,128)(2,1)}), bf16[896,2048]{1,0:T(8,128)(2,1)}) %all-gather.8.cloned.1.call-update) | async-done | bytes 3670032 | tf_op jit(solution)/shard_map/all_gather | solution.py:30
  365.1 4.6 fusion
  369.7 0.0 reduce-scatter.11.cloned.1.call-start
  369.7 16.6 %all-gather.10.cloned.1.call-done = bf16[896,2048]{1,0:T(8,128)(2,1)} async-done(((bf16[448,2048]{1,0:T(8,128)(2,1)}), bf16[896,2048]{1,0:T(8,128)(2,1)}) %all-gather.10.cloned.1.call-update) | async-done | bytes 3670032 | tf_op jit(solution)/shard_map/all_gather | solution.py:31
  386.3 4.2 fusion.1
  390.5 0.0 reduce-scatter.13.cloned.1.call-start
  390.6 30.3 %reduce-scatter.15.cloned.1.call-done = f32[64,896]{1,0:T(8,128)} async-done(((f32[256,896]{1,0:T(8,128)}), f32[64,896]{1,0:T(8,128)}) %reduce-scatter.15.cloned.1.call-update) | async-done | bytes 229392 | tf_op jit(solution)/shard_map/reduce_scatter | solution.py:51
  420.9 34.7 %reduce-scatter.9.cloned.1.call-done = f32[64,896]{1,0:T(8,128)} async-done(((f32[256,896]{1,0:T(8,128)}), f32[64,896]{1,0:T(8,128)}) %reduce-scatter.9.cloned.1.call-update) | async-done | bytes 229392 | tf_op jit(solution)/shard_map/reduce_scatter | solution.py:37
  455.6 34.2 %reduce-scatter.11.cloned.1.call-done = f32[64,896]{1,0:T(8,128)} async-done(((f32[256,896]{1,0:T(8,128)}), f32[64,896]{1,0:T(8,128)}) %reduce-scatter.11.cloned.1.call-update) | async-done | bytes 229392 | tf_op jit(solution)/shard_map/reduce_scatter | solution.py:38
  489.8 1.3 multiply_convert_fusion.3
  491.1 12.2 %all_gather.27 = bf16[256,896]{1,0:T(8,128)(2,1)S(1)} all-gather(bf16[64,896]{1,0:T(8,128)(2,1)S(1)} %get-tuple-element.7), channel_id=1, replica_groups=mesh['dcn'=2,'gx'=8,'gy'=4,'gz'=4] {'gy'}, dimensions={0}, use_global_device_ids=true | all-gather | bytes 573440 | tf_op jit(solution)/shard_map/all_gather | solution.py:42
  503.3 4.6 fusion.2
  507.9 0.0 reduce-scatter.17.cloned.1.call-start
  507.9 13.2 %all_gather.30 = bf16[256,896]{1,0:T(8,128)(2,1)S(1)} all-gather(bf16[64,896]{1,0:T(8,128)(2,1)S(1)} %get-tuple-element.6), channel_id=1, replica_groups=mesh['dcn'=2,'gx'=8,'gy'=4,'gz'=4] {'gy'}, dimensions={0}, use_global_device_ids=true | all-gather | bytes 573440 | tf_op jit(solution)/shard_map/all_gather | solution.py:57
  521.1 16.0 %all_gather.31 = bf16[256,896]{1,0:T(8,128)(2,1)S(1)} all-gather(bf16[64,896]{1,0:T(8,128)(2,1)S(1)} %get-tuple-element.5), channel_id=1, replica_groups=mesh['dcn'=2,'gx'=8,'gy'=4,'gz'=4] {'gy'}, dimensions={0}, use_global_device_ids=true | all-gather | bytes 573440 | tf_op jit(solution)/shard_map/all_gather | solution.py:58
  537.1 3.3 fusion.4
  540.4 2.7 convolution_add_fusion
  543.2 0.0 reduce-scatter.19.cloned.1.call-start
  543.2 4.1 fusion.5
  547.3 0.0 reduce-scatter.21.cloned.1.call-start
  547.4 4.2 fusion.6
  551.6 0.0 reduce-scatter.23.cloned.1.call-start
  551.6 1.1 copy-done.2
  552.8 4.1 fusion.7
  556.9 97.6 %reduce-scatter.13.cloned.1.call-done = f32[8,2048]{1,0:T(8,128)} async-done(((f32[256,2048]{1,0:T(8,128)}), f32[8,2048]{1,0:T(8,128)}) %reduce-scatter.13.cloned.1.call-update) | async-done | bytes 65552 | tf_op jit(solution)/shard_map/reduce_scatter | solution.py:43
  654.5 1.5 convert_element_type.25
  655.9 162.9 %reduce-scatter.17.cloned.1.call-done = f32[8,2048]{1,0:T(8,128)} async-done(((f32[256,2048]{1,0:T(8,128)}), f32[8,2048]{1,0:T(8,128)}) %reduce-scatter.17.cloned.1.call-update) | async-done | bytes 65552 | tf_op jit(solution)/shard_map/reduce_scatter | solution.py:60
  818.8 1.5 convert_element_type.28
  820.3 42.1 %reduce-scatter.19.cloned.1.call-done = f32[448,2048]{1,0:T(8,128)} async-done(((f32[896,2048]{1,0:T(8,128)}), f32[448,2048]{1,0:T(8,128)}) %reduce-scatter.19.cloned.1.call-update) | async-done | bytes 3670032 | tf_op jit(solution)/shard_map/reduce_scatter | solution.py:72
  862.4 3.6 multiply_convert_fusion.2
  866.0 21.4 %reduce-scatter.21.cloned.1.call-done = f32[448,2048]{1,0:T(8,128)} async-done(((f32[896,2048]{1,0:T(8,128)}), f32[448,2048]{1,0:T(8,128)}) %reduce-scatter.21.cloned.1.call-update) | async-done | bytes 3670032 | tf_op jit(solution)/shard_map/reduce_scatter | solution.py:73
  887.5 3.6 multiply_convert_fusion.1
  891.1 21.4 %reduce-scatter.23.cloned.1.call-done = f32[448,2048]{1,0:T(8,128)} async-done(((f32[896,2048]{1,0:T(8,128)}), f32[448,2048]{1,0:T(8,128)}) %reduce-scatter.23.cloned.1.call-update) | async-done | bytes 3670032 | tf_op jit(solution)/shard_map/reduce_scatter | solution.py:74
  912.5 3.6 multiply_convert_fusion
  (15 shorter events, 0.2 us)
Async XLA Ops:
  7.2 138.5 %all-gather.14.cloned.1.call-start = ((), (), s32[]{:S(2)}) async-start(), calls=%async_computation.15 | async-start | bytes 1081344 | tf_op jit(solution)/shard_map/all_gather | solution.py:27
  7.9 180.3 %all-gather.12.cloned.1.call-start = ((), (), s32[]{:S(2)}) async-start(), calls=%async_computation.13 | async-start | bytes 5505024 | tf_op jit(solution)/shard_map/all_gather | solution.py:32
  8.6 314.0 %all-gather.6.cloned.1.call-start = ((), (), s32[]{:S(2)}) async-start(), calls=%async_computation.8 | async-start | bytes 1081344 | tf_op jit(solution)/shard_map/all_gather | solution.py:26
  9.4 355.7 %all-gather.8.cloned.1.call-start = ((), (), s32[]{:S(2)}) async-start(), calls=%async_computation.9 | async-start | bytes 5505024 | tf_op jit(solution)/shard_map/all_gather | solution.py:30
  10.0 376.3 %all-gather.10.cloned.1.call-start = ((), (), s32[]{:S(2)}) async-start(), calls=%async_computation.11 | async-start | bytes 5505024 | tf_op jit(solution)/shard_map/all_gather | solution.py:31
  10.5 410.4 %reduce-scatter.15.cloned.1.call-start = ((), (), s32[]{:S(2)}) async-start(), calls=%async_computation.16 | async-start | bytes 1146880 | tf_op jit(solution)/shard_map/reduce_scatter | solution.py:51
  192.8 262.8 %reduce-scatter.9.cloned.1.call-start = ((), (), s32[]{:S(2)}) async-start(), calls=%async_computation.10 | async-start | bytes 1146880 | tf_op jit(solution)/shard_map/reduce_scatter | solution.py:37
  322.6 63.6 %copy-start = (bf16[256,2048]{1,0:T(8,128)(2,1)S(1)}, bf16[256,2048]{1,0:T(8,128)(2,1)}, u32[]{:S(2)}) copy-start(bf16[256,2048]{1,0:T(8,128)(2,1)} %all-gather.6.cloned.1.call-done) | copy-start | bytes 3145732
  369.7 120.1 %reduce-scatter.11.cloned.1.call-start = ((), (), s32[]{:S(2)}) async-start(), calls=%async_computation.12 | async-start | bytes 1146880 | tf_op jit(solution)/shard_map/reduce_scatter | solution.py:38
  390.5 263.9 %reduce-scatter.13.cloned.1.call-start = ((), (), s32[]{:S(2)}) async-start(), calls=%async_computation.14 | async-start | bytes 2162688 | tf_op jit(solution)/shard_map/reduce_scatter | solution.py:43
  507.9 310.9 %reduce-scatter.17.cloned.1.call-start = ((), (), s32[]{:S(2)}) async-start(), calls=%async_computation.17 | async-start | bytes 2162688 | tf_op jit(solution)/shard_map/reduce_scatter | solution.py:60
  507.9 32.5 %copy-start.1 = (bf16[896,2048]{1,0:T(8,128)(2,1)S(1)}, bf16[896,2048]{1,0:T(8,128)(2,1)}, u32[]{:S(2)}) copy-start(bf16[896,2048]{1,0:T(8,128)(2,1)} %all-gather.10.cloned.1.call-done) | copy-start | bytes 11010052
  543.2 319.3 %reduce-scatter.19.cloned.1.call-start = ((), (), s32[]{:S(2)}) async-start(), calls=%async_computation.18 | async-start | bytes 11010048 | tf_op jit(solution)/shard_map/reduce_scatter | solution.py:72
  547.3 340.1 %reduce-scatter.21.cloned.1.call-start = ((), (), s32[]{:S(2)}) async-start(), calls=%async_computation.19 | async-start | bytes 11010048 | tf_op jit(solution)/shard_map/reduce_scatter | solution.py:73
  551.5 1.2 copy-start.2
  551.6 360.9 %reduce-scatter.23.cloned.1.call-start = ((), (), s32[]{:S(2)}) async-start(), calls=%async_computation.20 | async-start | bytes 11010048 | tf_op jit(solution)/shard_map/reduce_scatter | solution.py:74
Sparse Core Ops, SparseCore 0:
  9.8 135.8 all-gather.13
  147.4 40.7 all-gather.11
  190.0 132.5 all-gather.5
  324.3 40.7 all-gather.7
  366.7 19.5 all-gather.9
  389.3 31.6 reduce-scatter.14
  424.1 31.4 reduce-scatter.8
  458.7 30.9 reduce-scatter.10
  508.0 146.4 reduce-scatter.12
  657.0 161.7 reduce-scatter.16
  821.4 40.9 reduce-scatter.18
  865.0 22.4 reduce-scatter.20
  890.0 22.3 reduce-scatter.22
where the time goes:
time: 923 us
  waiting for transfers between devices  814 us (88%)
  blocking collectives  41.4 us (4%)
  matrix products  36.3 us (4%)
  other arithmetic  15 us (2%)
  between operations  13.9 us (2%)
    reduce_scatter x1, waiting for transfers between devices, per_device(): lax.psum_scatter(jnp.dot(gate_rows, w_gate, preferred_element_type=jnp.fl...  163 us
    all_gather x1, waiting for transfers between devices, per_device(): lax.all_gather(out_grad, ('gx', 'gz'), axis=0, tiled=True)  135 us
    all_gather x1, waiting for transfers between devices, per_device(): lax.all_gather(tokens, ('gx', 'gz'), axis=0, tiled=True)  130 us
    reduce_scatter x1, waiting for transfers between devices, per_device(): lax.psum_scatter(jnp.dot(hidden_all, w_down, preferred_element_type=jnp.f...  97.6 us
    all_gather x1, waiting for transfers between devices, per_device(): lax.all_gather(down_weight, 'dcn', axis=0, tiled=True)  42.6 us
    all_gather x1, waiting for transfers between devices, per_device(): lax.all_gather(gate_weight, 'dcn', axis=0, tiled=True)  42.4 us
    reduce_scatter x1, waiting for transfers between devices, per_device(): lax.psum_scatter(gate_grad, 'dcn', scatter_dimension=0, tiled=True)  42.1 us
    reduce_scatter x1, waiting for transfers between devices, per_device(): lax.psum_scatter(gate_part, 'gy', scatter_dimension=0, tiled=True)  34.7 us
  transfers between devices with their start and end apart: 13, of which 13 were waited for; matrix products, arithmetic and copies ran while one was open for 5% of the time, Pallas kernels for 0%

commit v1 on v0

v1 whole, which is shorter than its diff:
```python
import math

import jax
import jax.numpy as jnp
from jax import lax
from jax.experimental import pallas as pl
from jax.experimental.pallas import tpu as pltpu
from jax.sharding import PartitionSpec as P

BF16, F32 = jnp.bfloat16, jnp.float32
PLANE = ("gx", "gz")
WIDTH = 512
SMEM = pl.BlockSpec(memory_space=pltpu.SMEM)
VMEM = pl.BlockSpec(memory_space=pltpu.VMEM)
PARAMS = pltpu.CompilerParams(vmem_limit_bytes=40 * 1024 * 1024)


def by_features(left, right):
    return lax.dot_general(left, right, (((1,), (1,)), ((), ())), preferred_element_type=F32)


def cost(flops, moved):
    return pl.CostEstimate(flops=int(flops), bytes_accessed=int(moved), transcendentals=0)


def shifted(x, axis, by):
    n = lax.axis_size(axis)
    return lax.ppermute(x, axis, [(i, (i + by) % n) for i in range(n)])


def partial_sums(me, own, other, weights):
    count, ways = len(weights), 4
    units, width = weights[0].shape
    rows = own.shape[0]
    block = 2 * rows // ways

    def kernel(me_ref, own_ref, other_ref, *refs):
        w_refs, o_refs, held = refs[:count], refs[count : count + ways], refs[-1]
        for k in range(count):
            for half, t_ref in enumerate((own_ref, other_ref)):
                sums = by_features(w_refs[k][...], t_ref[...])
                held[2 * half, k] = sums[:, :block]
                held[2 * half + 1, k] = sums[:, block:]
        for s in range(ways):
            o_refs[s][...] = held[lax.rem(me_ref[0] + s, ways)].astype(o_refs[s].dtype)

    shape = (count, units, block)
    return pl.pallas_call(
        kernel,
        in_specs=[SMEM] + [VMEM] * (2 + count),
        out_specs=[VMEM] * ways,
        out_shape=[jax.ShapeDtypeStruct(shape, F32 if s == 0 else BF16) for s in range(ways)],
        scratch_shapes=[pltpu.VMEM((ways,) + shape, F32)],
        compiler_params=PARAMS,
        cost_estimate=cost(4 * count * units * width * rows, 2 * width * (2 * rows + count * units)),
        name="partial_sums",
    )(me, own, other, *weights)


def row_sums(me, blocks, weights):
    count, ways = len(weights), 4
    units, width = weights[0].shape
    block = blocks[0].shape[-1]

    def kernel(me_ref, *refs):
        b_refs, w_refs = refs[:ways], refs[ways : ways + count]
        own_ref, other_ref, held = refs[ways + count :]

        @pl.when(pl.program_id(0) == 0)
        def _():
            for s in range(ways):
                at = pl.multiple_of(lax.rem(me_ref[0] + s, ways) * block, block)
                for k in range(count):
                    held[pl.ds(at, block), k * units : (k + 1) * units] = b_refs[s][k].T

        total = 0.0
        for k in range(count):
            total += jnp.dot(
                held[:, k * units : (k + 1) * units], w_refs[k][...], preferred_element_type=F32
            )
        own_ref[...] = total[: 2 * block]
        other_ref[...] = total[2 * block :].astype(BF16)

    columns = pl.BlockSpec((units, WIDTH), lambda i: (0, i))
    rows = pl.BlockSpec((2 * block, WIDTH), lambda i: (0, i))
    return pl.pallas_call(
        kernel,
        grid=(width // WIDTH,),
        in_specs=[SMEM] + [VMEM] * ways + [columns] * count,
        out_specs=[rows, rows],
        out_shape=[
            jax.ShapeDtypeStruct((2 * block, width), F32),
            jax.ShapeDtypeStruct((2 * block, width), BF16),
        ],
        scratch_shapes=[pltpu.VMEM((ways * block, count * units), BF16)],
        compiler_params=PARAMS,
        cost_estimate=cost(2 * ways * block * count * units * width, 2 * width * (count * units + 6 * block)),
        name="row_sums",
    )(me, *blocks, *weights)


def weight_grads(me, blocks, own, other, factor):
    ways = 4
    count, units, block = blocks[0].shape
    width = own.shape[1]

    def kernel(me_ref, *refs):
        b_refs, (own_ref, other_ref) = refs[:ways], refs[ways : ways + 2]
        o_refs, held = refs[ways + 2 : -1], refs[-1]

        @pl.when(pl.program_id(0) == 0)
        def _():
            for s in range(ways):
                at = pl.multiple_of(lax.rem(me_ref[0] + s, ways) * block, block)
                for k in range(count):
                    held[k, :, pl.ds(at, block)] = b_refs[s][k]

        for k in range(count):
            total = jnp.dot(held[k, :, : 2 * block], own_ref[...], preferred_element_type=F32)
            total += jnp.dot(held[k, :, 2 * block :], other_ref[...], preferred_element_type=F32)
            o_refs[k][...] = (total * factor).astype(BF16)

    rows = pl.BlockSpec((2 * block, WIDTH), lambda i: (0, i))
    columns = pl.BlockSpec((units, WIDTH), lambda i: (0, i))
    return pl.pallas_call(
        kernel,
        grid=(width // WIDTH,),
        in_specs=[SMEM] + [VMEM] * ways + [rows, rows],
        out_specs=[columns] * count,
        out_shape=[jax.ShapeDtypeStruct((units, width), BF16)] * count,
        scratch_shapes=[pltpu.VMEM((count, units, ways * block), BF16)],
        compiler_params=PARAMS,
        cost_estimate=cost(2 * ways * block * count * units * width, 2 * width * (count * units + 4 * block)),
        name="weight_grads",
    )(me, *blocks, own, other)


def gathered(x):
    n = lax.axis_size("gx") * lax.axis_size("gz")
    rows, width = x.shape
    spread = jnp.broadcast_to(x[None], (n, rows, width))
    own = lax.all_to_all(spread, PLANE, 0, 0, tiled=True).reshape(n * rows, width)
    return own, shifted(own, "dcn", 1)


def scattered(own, other):
    n = lax.axis_size("gx") * lax.axis_size("gz")
    rows, width = own.shape
    both = (own + shifted(other, "dcn", 1).astype(F32)).astype(BF16)
    parts = lax.all_to_all(both.reshape(n, rows // n, width), PLANE, 0, 0, tiled=True)
    return jnp.sum(parts.astype(F32), axis=0).astype(BF16)


def exchanged(parts):
    return [parts[0]] + [shifted(parts[s], "gy", s) for s in (1, 2, 3)]


def spread(block):
    return [block] + [shifted(block, "gy", -s) for s in (1, 2, 3)]


def summed(parts):
    total = parts[0]
    for part in parts[1:]:
        total = total + part.astype(F32)
    return total


def per_device(tokens, gate_weight, up_weight, down_weight, out_grad):
    token_count = tokens.shape[0] * lax.axis_size("dcn") * lax.axis_size("gx") * lax.axis_size("gz")
    factor = 1.0 / math.sqrt(token_count)
    me = lax.axis_index("gy").astype(jnp.int32).reshape(1)

    token_rows = gathered(tokens)
    gate_up_parts = partial_sums(me, *token_rows, (gate_weight, up_weight))
    gate_up_parts = exchanged(gate_up_parts)

    out_grad, _ = lax.optimization_barrier((out_grad, token_rows[1]))
    grad_rows = gathered(out_grad)
    hgrad_parts = exchanged(partial_sums(me, *grad_rows, (down_weight,)))

    gate_total, up_total = summed(gate_up_parts)
    sigmoid_gate = jax.nn.sigmoid(gate_total)
    hidden = (gate_total * sigmoid_gate * up_total).astype(BF16)
    hidden_all = spread(hidden[None])

    hidden_grad = summed(hgrad_parts)[0]
    gate_delta = (
        hidden_grad * up_total * sigmoid_gate * (1.0 + gate_total * (1.0 - sigmoid_gate))
    ).astype(BF16)
    up_delta = (hidden_grad * gate_total * sigmoid_gate).astype(BF16)
    deltas_all = spread(jnp.stack([gate_delta, up_delta]))

    output = scattered(*row_sums(me, hidden_all, (down_weight,)))
    (down_grad,) = weight_grads(me, hidden_all, *grad_rows, factor)
    tokens_grad = scattered(*row_sums(me, deltas_all, (gate_weight, up_weight)))
    gate_grad, up_grad = weight_grads(me, deltas_all, *token_rows, factor)
    return output, tokens_grad, gate_grad, up_grad, down_grad


def solution(mesh):
    placed = P(("dcn", "gx", "gz"), "gy")
    return jax.shard_map(
        per_device,
        mesh=mesh,
        in_specs=(placed,) * 5,
        out_specs=(placed,) * 5,
        check_vma=False,
    )
```

time: 923 us -> 200 us (0.22)
  waiting for transfers between devices: 814 us -> 58 us
  starting transfers between devices: 0.52 us -> 59 us
  matrix products: 36.3 us -> 0 us
  Pallas kernels: 0 us -> 16.9 us
  between operations: 13.9 us -> 0.81 us
  local copies, waits for them, and re-layouts: 1.16 us -> 11.9 us
    reduce_scatter x8 -> x0, waiting for transfers between devices: 445 us -> none  [the longest x1 163 us: per_device(): lax.psum_scatter(jnp.dot(gate_rows, w_gate, preferred_element_type=jnp.fl...]
    all_gather x5 -> x0, waiting for transfers between devices: 366 us -> none  [the longest x1 135 us: per_device(): lax.all_gather(out_grad, ('gx', 'gz'), axis=0, tiled=True)]
    ppermute x0 -> x16, waiting for transfers between devices: none -> 54.6 us  [shifted(): return lax.ppermute(x, axis, [(i, (i + by) % n) for i in range(n)])]
    all_to_all x0 -> x2, blocking collectives: none -> 43.6 us  [gathered(): lax.all_to_all(spread, PLANE, 0, 0, tiled=True).reshape(n * rows, width)]
    all_gather x3 -> x0, blocking collectives: 41.4 us -> none  [the longest x1 16 us: per_device(): lax.all_gather(up_delta, 'gy', axis=0, tiled=True)]
    ppermute x0 -> x16, starting transfers between devices: none -> 39.3 us  [shifted(): return lax.ppermute(x, axis, [(i, (i + by) % n) for i in range(n)])]
    dot_general x9 -> x0, matrix products: 36.3 us -> none  [the longest x3 13.4 us: by_features(): lax.dot_general(left, right, (((1,), (1,)), ((), ())), preferred_element_...]
    all_to_all x0 -> x2, starting transfers between devices: none -> 19.7 us  [scattered(): lax.all_to_all(both.reshape(n, rows // n, width), PLANE, 0, 0, tiled=True)]
  transfers between devices with their start and end apart: 13 -> 18, of which waited for: 13 -> 12; matrix products, arithmetic and copies ran while one was open for 5% -> 2% of each run, Pallas kernels for 0% -> 7%
where the time goes in v1:
time: 200 us; the launch traced here: 199 us
  starting transfers between devices  59 us (30%)
  waiting for transfers between devices  58 us (29%)
  blocking collectives  43.6 us (22%)
  Pallas kernels  16.9 us (8%)
  local copies, waits for them, and re-layouts  11.9 us (6%)
  other arithmetic  8.46 us (4%)
    ppermute x16, waiting for transfers between devices, shifted(): return lax.ppermute(x, axis, [(i, (i + by) % n) for i in range(n)])  54.6 us
    all_to_all x2, blocking collectives, gathered(): lax.all_to_all(spread, PLANE, 0, 0, tiled=True).reshape(n * rows, width)  43.6 us
    ppermute x16, starting transfers between devices, shifted(): return lax.ppermute(x, axis, [(i, (i + by) % n) for i in range(n)])  39.3 us
    all_to_all x2, starting transfers between devices, scattered(): lax.all_to_all(both.reshape(n, rows // n, width), PLANE, 0, 0, tiled=True)  19.7 us
    unnamed x42, local copies, waits for them, and re-layouts  10.9 us
    pallas_call x2, Pallas kernels, weight_grads(): pl.pallas_call(kernel, grid=(width // WIDTH,), in_specs=[SMEM] + [VMEM] *...  6.98 us
    pallas_call x2, Pallas kernels, row_sums(): pl.pallas_call(kernel, grid=(width // WIDTH,), in_specs=[SMEM] + [VMEM] *...  6.28 us
    reduce_sum x2, other arithmetic, scattered(): return jnp.sum(parts.astype(F32), axis=0).astype(BF16)  4 us
  transfers between devices with their start and end apart: 18, of which 12 were waited for; matrix products, arithmetic and copies ran while one was open for 2% of the time, Pallas kernels for 7%

profile of v1, /device:TPU:1, one launch (start us, length us, event | category | flops | bytes accessed | tf_op | source)
XLA Modules:
  0.0 198.7 jit_solution(8948021803637768774)
XLA Ops:
  1.5 23.9 %all_to_all.20 = bf16[32,8,2048]{2,1,0:T(8,128)(2,1)S(1)} all-to-all(bf16[32,8,2048]{2,1,0:T(8,128)(2,1)S(1)} %broadcast_in_dim.4), channel_id=1, replica_groups=mesh['dcn'=2,'gx'=8,'gy'=4,'gz'=4] {'gx','gz'}, dimensions={0} | all-to-all | bytes 2097152 | tf_op jit(solution)/shard_map/all_to_all | solution.py:142
  25.4 2.6 %collective-permute-start = (bf16[256,2048]{1,0:T(8,128)(2,1)S(1)}, bf16[256,2048]{1,0:T(8,128)(2,1)S(1)}, u32[]{:S(2)}, u32[]{:S(2)}) collective-permute-start(bf16[256,2048]{1,0:T(8,128)(2,1)S(1)} %bitcast.10), channel_id=1, source_target_pairs={{0,128},{128,0},{1,129},{129,1},{2,130},{130,2},{3,131},{131,3},{4... | collective-permute-start | bytes 3145736 | tf_op jit(solution)/shard_map/ppermute | solution.py:28
  28.0 2.3 %collective-permute-done.other_ref.refs_5_ = bf16[256,2048]{1,0:T(8,128)(2,1)S(1)} collective-permute-done((bf16[256,2048]{1,0:T(8,128)(2,1)S(1)}, bf16[256,2048]{1,0:T(8,128)(2,1)S(1)}, u32[]{:S(2)}, u32[]{:S(2)}) %collective-permute-start) | collective-permute-done | bytes 1048608 | tf_op jit(solution)/shard_map/ppermute | solution.py:28
  30.3 1.0 copy-done.11
  31.4 19.8 %all_to_all.21 = bf16[32,8,2048]{2,1,0:T(8,128)(2,1)S(1)} all-to-all(bf16[32,8,2048]{2,1,0:T(8,128)(2,1)S(1)} %broadcast_in_dim.5), channel_id=1, replica_groups=mesh['dcn'=2,'gx'=8,'gy'=4,'gz'=4] {'gx','gz'}, dimensions={0} | all-to-all | bytes 2097152 | tf_op jit(solution)/shard_map/all_to_all | solution.py:142
  51.2 2.3 %collective-permute-start.8 = (bf16[256,2048]{1,0:T(8,128)(2,1)S(1)}, bf16[256,2048]{1,0:T(8,128)(2,1)S(1)}, u32[]{:S(2)}, u32[]{:S(2)}) collective-permute-start(bf16[256,2048]{1,0:T(8,128)(2,1)S(1)} %bitcast.7), channel_id=1, source_target_pairs={{0,128},{128,0},{1,129},{129,1},{2,130},{130,2},{3,131},{131,3},{4... | collective-permute-start | bytes 3145736 | tf_op jit(solution)/shard_map/ppermute | solution.py:28
  53.4 1.5 copy-done.7
  54.9 1.5 copy-done.9
  56.4 1.2 copy-done.12
  57.6 2.4 %partial_sums.2 = (f32[2,448,128]{2,1,0:T(8,128)S(1)}, bf16[2,448,128]{2,1,0:T(8,128)(2,1)S(1)}, bf16[2,448,128]{2,1,0:T(8,128)(2,1)S(1)}, bf16[2,448,128]{2,1,0:T(8,128)(2,1)S(1)}) custom-call(s32[1]{0:T(128)} %bitcast.me_ref, bf16[256,2048]{1,0:T(8,128)(2,1)S(1)} %bitcast.11, bf16[256,2048]{1,0:T(8,128)(2,1)S(1)} %copy-done.12, ...), custom_call_target="tpu_custom_call" | custom-call | flops 1879048192 | bytes 5767168 | tf_op jit(solution)/shard_map/partial_sums/pallas_call | solution.py:48
  60.0 5.2 %collective-permute-start.3 = (bf16[2,448,128]{2,1,0:T(8,128)(2,1)S(1)}, bf16[2,448,128]{2,1,0:T(8,128)(2,1)S(1)}, u32[]{:S(2)}, u32[]{:S(2)}) collective-permute-start(bf16[2,448,128]{2,1,0:T(8,128)(2,1)S(1)} %get-tuple-element.23), channel_id=1, source_target_pairs={{0,12},{4,0},{8,4},{12,8},{1,13},{5,1},{9,5},{13,9},{2,14},{6,2},{... | collective-permute-start | bytes 688136 | tf_op jit(solution)/shard_map/ppermute | solution.py:28
  65.3 1.1 collective-permute-start.2
  66.4 2.1 %collective-permute-start.1 = (bf16[2,448,128]{2,1,0:T(8,128)(2,1)S(1)}, bf16[2,448,128]{2,1,0:T(8,128)(2,1)S(1)}, u32[]{:S(2)}, u32[]{:S(2)}) collective-permute-start(bf16[2,448,128]{2,1,0:T(8,128)(2,1)S(1)} %get-tuple-element.21), channel_id=1, source_target_pairs={{0,4},{4,8},{8,12},{12,0},{1,5},{5,9},{9,13},{13,1},{2,6},{6,10},{... | collective-permute-start | bytes 688136 | tf_op jit(solution)/shard_map/ppermute | solution.py:28
  68.5 1.3 partial_sums.3
  69.8 1.6 collective-permute-start.11
  71.3 4.2 %collective-permute-start.10 = (bf16[1,448,128]{2,1,0:T(8,128)(2,1)S(1)}, bf16[1,448,128]{2,1,0:T(8,128)(2,1)S(1)}, u32[]{:S(2)}, u32[]{:S(2)}) collective-permute-start(bf16[1,448,128]{2,1,0:T(8,128)(2,1)S(1)} %get-tuple-element.29), channel_id=1, source_target_pairs={{0,8},{4,12},{8,0},{12,4},{1,9},{5,13},{9,1},{13,5},{2,10},{6,14},... | collective-permute-start | bytes 344072 | tf_op jit(solution)/shard_map/ppermute | solution.py:28
  75.6 5.1 %collective-permute-done.2 = bf16[2,448,128]{2,1,0:T(8,128)(2,1)S(1)} collective-permute-done((bf16[2,448,128]{2,1,0:T(8,128)(2,1)S(1)}, bf16[2,448,128]{2,1,0:T(8,128)(2,1)S(1)}, u32[]{:S(2)}, u32[]{:S(2)}) %collective-permute-start.2) | collective-permute-done | bytes 229408 | tf_op jit(solution)/shard_map/ppermute | solution.py:28
  80.7 1.5 collective-permute-done.1
  82.3 8.3 %collective-permute-done.10 = bf16[1,448,128]{2,1,0:T(8,128)(2,1)S(1)} collective-permute-done((bf16[1,448,128]{2,1,0:T(8,128)(2,1)S(1)}, bf16[1,448,128]{2,1,0:T(8,128)(2,1)S(1)}, u32[]{:S(2)}, u32[]{:S(2)}) %collective-permute-start.10) | collective-permute-done | bytes 114720 | tf_op jit(solution)/shard_map/ppermute | solution.py:28
  91.4 3.1 %collective-permute-start.4 = (bf16[1,448,128]{2,1,0:T(8,128)(2,1)S(1)}, bf16[1,448,128]{2,1,0:T(8,128)(2,1)S(1)}, u32[]{:S(2)}, u32[]{:S(2)}) collective-permute-start(bf16[1,448,128]{2,1,0:T(8,128)(2,1)S(1)} %get-tuple-element.37.refs_0_), channel_id=1, source_target_pairs={{0,12},{4,0},{8,4},{12,8},{1,13},{5,1},{9,5},{13,9},{2,14},{6,2},{... | collective-permute-start | bytes 344072 | tf_op jit(solution)/shard_map/ppermute | solution.py:28
  94.5 3.6 %collective-permute-start.5 = (bf16[1,448,128]{2,1,0:T(8,128)(2,1)S(1)}, bf16[1,448,128]{2,1,0:T(8,128)(2,1)S(1)}, u32[]{:S(2)}, u32[]{:S(2)}) collective-permute-start(bf16[1,448,128]{2,1,0:T(8,128)(2,1)S(1)} %get-tuple-element.37.refs_0_), channel_id=1, source_target_pairs={{0,8},{4,12},{8,0},{12,4},{1,9},{5,13},{9,1},{13,5},{2,10},{6,14},... | collective-permute-start | bytes 344072 | tf_op jit(solution)/shard_map/ppermute | solution.py:28
  98.1 1.1 collective-permute-start.6
  99.2 4.0 %collective-permute-done.5.refs_2_ = bf16[1,448,128]{2,1,0:T(8,128)(2,1)S(1)} collective-permute-done((bf16[1,448,128]{2,1,0:T(8,128)(2,1)S(1)}, bf16[1,448,128]{2,1,0:T(8,128)(2,1)S(1)}, u32[]{:S(2)}, u32[]{:S(2)}) %collective-permute-start.5) | collective-permute-done | bytes 114720 | tf_op jit(solution)/shard_map/ppermute | solution.py:28
  103.2 2.8 %collective-permute-done.6.refs_3_ = bf16[1,448,128]{2,1,0:T(8,128)(2,1)S(1)} collective-permute-done((bf16[1,448,128]{2,1,0:T(8,128)(2,1)S(1)}, bf16[1,448,128]{2,1,0:T(8,128)(2,1)S(1)}, u32[]{:S(2)}, u32[]{:S(2)}) %collective-permute-start.6) | collective-permute-done | bytes 114720 | tf_op jit(solution)/shard_map/ppermute | solution.py:28
  106.0 2.3 %row_sums.2 = (f32[256,2048]{1,0:T(8,128)S(1)}, bf16[256,2048]{1,0:T(8,128)(2,1)S(1)}) custom-call(s32[1]{0:T(128)} %bitcast.me_ref, bf16[1,448,128]{2,1,0:T(8,128)(2,1)S(1)} %get-tuple-element.37.refs_0_, bf16[1,448,128]{2,1,0:T(8,128)(2,1)S(1)} %collective-permute-done.4.refs_1_, bf16[1,448,128]{2,1,0:T(8,128)(2,1)S(1)} %collective-permute-done.5.refs_2_, ...), custom_call_target="tpu_custom_call" | custom-call | flops 939524096 | bytes 4980736 | tf_op jit(solution)/shard_map/row_sums/pallas_call | solution.py:86
  108.3 5.2 %collective-permute-start.7 = (bf16[256,2048]{1,0:T(8,128)(2,1)S(1)}, bf16[256,2048]{1,0:T(8,128)(2,1)S(1)}, u32[]{:S(2)}, u32[]{:S(2)}) collective-permute-start(bf16[256,2048]{1,0:T(8,128)(2,1)S(1)} %get-tuple-element.25), channel_id=1, source_target_pairs={{0,128},{128,0},{1,129},{129,1},{2,130},{130,2},{3,131},{131,3},{4... | collective-permute-start | bytes 3145736 | tf_op jit(solution)/shard_map/ppermute | solution.py:28
  113.6 2.3 %collective-permute-done.7 = bf16[256,2048]{1,0:T(8,128)(2,1)S(1)} collective-permute-done((bf16[256,2048]{1,0:T(8,128)(2,1)S(1)}, bf16[256,2048]{1,0:T(8,128)(2,1)S(1)}, u32[]{:S(2)}, u32[]{:S(2)}) %collective-permute-start.7) | collective-permute-done | bytes 1048608 | tf_op jit(solution)/shard_map/ppermute | solution.py:28
  115.9 1.3 fusion
  117.1 9.8 %all-to-all-start.1 = ((bf16[32,8,2048]{2,1,0:T(8,128)(2,1)}), bf16[32,8,2048]{2,1,0:T(8,128)(2,1)}, u32[]{:S(2)}, u32[]{:S(2)}) async-start(bf16[32,8,2048]{2,1,0:T(8,128)(2,1)} %fusion), calls=%async_computation.1 | async-start | bytes 2097152 | tf_op jit(solution)/shard_map/all_to_all | solution.py:150
  126.9 1.0 pad_maximum_fusion.refs_0_
  127.9 1.8 collective-permute-start.12
  129.7 2.1 %collective-permute-start.13 = (bf16[2,448,128]{2,1,0:T(8,128)(2,1)S(1)}, bf16[2,448,128]{2,1,0:T(8,128)(2,1)S(1)}, u32[]{:S(2)}, u32[]{:S(2)}) collective-permute-start(bf16[2,448,128]{2,1,0:T(8,128)(2,1)S(1)} %pad_maximum_fusion.refs_0_), channel_id=1, source_target_pairs={{0,8},{4,12},{8,0},{12,4},{1,9},{5,13},{9,1},{13,5},{2,10},{6,14},... | collective-permute-start | bytes 688136 | tf_op jit(solution)/shard_map/ppermute | solution.py:28
  131.8 2.0 %collective-permute-start.14 = (bf16[2,448,128]{2,1,0:T(8,128)(2,1)S(1)}, bf16[2,448,128]{2,1,0:T(8,128)(2,1)S(1)}, u32[]{:S(2)}, u32[]{:S(2)}) collective-permute-start(bf16[2,448,128]{2,1,0:T(8,128)(2,1)S(1)} %pad_maximum_fusion.refs_0_), channel_id=1, source_target_pairs={{0,4},{4,8},{8,12},{12,0},{1,5},{5,9},{9,13},{13,1},{2,6},{6,10},{... | collective-permute-start | bytes 688136 | tf_op jit(solution)/shard_map/ppermute | solution.py:28
  133.9 1.7 collective-permute-done.12.refs_1_
  135.6 21.1 %collective-permute-done.13.refs_2_ = bf16[2,448,128]{2,1,0:T(8,128)(2,1)S(1)} collective-permute-done((bf16[2,448,128]{2,1,0:T(8,128)(2,1)S(1)}, bf16[2,448,128]{2,1,0:T(8,128)(2,1)S(1)}, u32[]{:S(2)}, u32[]{:S(2)}) %collective-permute-start.13) | collective-permute-done | bytes 229408 | tf_op jit(solution)/shard_map/ppermute | solution.py:28
  156.7 3.1 %collective-permute-done.14.refs_3_ = bf16[2,448,128]{2,1,0:T(8,128)(2,1)S(1)} collective-permute-done((bf16[2,448,128]{2,1,0:T(8,128)(2,1)S(1)}, bf16[2,448,128]{2,1,0:T(8,128)(2,1)S(1)}, u32[]{:S(2)}, u32[]{:S(2)}) %collective-permute-start.14) | collective-permute-done | bytes 229408 | tf_op jit(solution)/shard_map/ppermute | solution.py:28
  159.9 1.5 copy-done.8
  161.4 1.5 copy-done.10
  162.9 4.0 %row_sums.3 = (f32[256,2048]{1,0:T(8,128)S(1)}, bf16[256,2048]{1,0:T(8,128)(2,1)S(1)}) custom-call(s32[1]{0:T(128)} %bitcast.me_ref, bf16[2,448,128]{2,1,0:T(8,128)(2,1)S(1)} %pad_maximum_fusion.refs_0_, bf16[2,448,128]{2,1,0:T(8,128)(2,1)S(1)} %collective-permute-done.12.refs_1_, bf16[2,448,128]{2,1,0:T(8,128)(2,1)S(1)} %collective-permute-done.13.refs_2_, ...), custom_call_target="tpu_custom_call" | custom-call | flops 1879048192 | bytes 6815744 | tf_op jit(solution)/shard_map/row_sums/pallas_call | solution.py:86
  166.9 1.3 collective-permute-start.15
  168.2 2.3 %collective-permute-done.15 = bf16[256,2048]{1,0:T(8,128)(2,1)S(1)} collective-permute-done((bf16[256,2048]{1,0:T(8,128)(2,1)S(1)}, bf16[256,2048]{1,0:T(8,128)(2,1)S(1)}, u32[]{:S(2)}, u32[]{:S(2)}) %collective-permute-start.15) | collective-permute-done | bytes 1048608 | tf_op jit(solution)/shard_map/ppermute | solution.py:28
  170.5 1.3 fusion.1
  171.8 9.8 %all-to-all-start.3 = ((bf16[32,8,2048]{2,1,0:T(8,128)(2,1)}), bf16[32,8,2048]{2,1,0:T(8,128)(2,1)}, u32[]{:S(2)}, u32[]{:S(2)}) async-start(bf16[32,8,2048]{2,1,0:T(8,128)(2,1)} %fusion.1), calls=%async_computation.3 | async-start | bytes 2097152 | tf_op jit(solution)/shard_map/all_to_all | solution.py:150
  184.3 3.1 %weight_grads.3 = bf16[448,2048]{1,0:T(8,128)(2,1)} custom-call(s32[1]{0:T(128)} %bitcast.me_ref, bf16[1,448,128]{2,1,0:T(8,128)(2,1)S(1)} %get-tuple-element.37.refs_0_, bf16[1,448,128]{2,1,0:T(8,128)(2,1)S(1)} %copy-done.2, bf16[1,448,128]{2,1,0:T(8,128)(2,1)S(1)} %copy-done.4, bf16[1,448,128]{2,1,0:T(8,128)(2,1)S(1)} %copy-done.6, ...), custom_call_target="tpu_custom_call" | custom-call | flops 939524096 | bytes 3932160 | tf_op jit(solution)/shard_map/weight_grads/pallas_call | solution.py:125
  187.4 3.9 %weight_grads.2 = (bf16[448,2048]{1,0:T(8,128)(2,1)}, bf16[448,2048]{1,0:T(8,128)(2,1)}) custom-call(s32[1]{0:T(128)} %bitcast.me_ref, bf16[2,448,128]{2,1,0:T(8,128)(2,1)S(1)} %pad_maximum_fusion.refs_0_, bf16[2,448,128]{2,1,0:T(8,128)(2,1)S(1)} %copy-done.15, bf16[2,448,128]{2,1,0:T(8,128)(2,1)S(1)} %copy-done.17, bf16[2,448,128]{2,1,0:T(8,128)(2,1)S(1)} %copy-done.19, ...), custom_call_target="tpu_custom_call" | custom-call | flops 1879048192 | bytes 5767168 | tf_op jit(solution)/shard_map/weight_grads/pallas_call | solution.py:125
  191.3 2.0 %reduce_sum.24 = bf16[8,2048]{1,0:T(8,128)(2,1)} reduce(bf16[32,8,2048]{2,1,0:T(8,128)(2,1)} %all-to-all-done.1, bf16[]{:T(256)} %constant.10.clone.1), dimensions={0}, to_apply=%region_0.0 | reduce | flops 507904 | bytes 1081346 | tf_op jit(solution)/shard_map/reduce_sum | solution.py:151
  193.3 3.4 %all-to-all-done.3 = bf16[32,8,2048]{2,1,0:T(8,128)(2,1)} async-done(((bf16[32,8,2048]{2,1,0:T(8,128)(2,1)}), bf16[32,8,2048]{2,1,0:T(8,128)(2,1)}, u32[]{:S(2)}, u32[]{:S(2)}) %all-to-all-start.3) | async-done | bytes 1048608 | tf_op jit(solution)/shard_map/all_to_all | solution.py:150
  196.7 2.0 %reduce_sum.25 = bf16[8,2048]{1,0:T(8,128)(2,1)} reduce(bf16[32,8,2048]{2,1,0:T(8,128)(2,1)} %all-to-all-done.3, bf16[]{:T(256)} %constant.10.clone.1), dimensions={0}, to_apply=%region_1.0 | reduce | flops 507904 | bytes 1081346 | tf_op jit(solution)/shard_map/reduce_sum | solution.py:151
  (47 shorter events, 4.7 us)
Async XLA Ops:
  0.6 30.7 %copy-start.20 = (bf16[8,2048]{1,0:T(8,128)(2,1)S(1)}, bf16[8,2048]{1,0:T(8,128)(2,1)}, u32[]{:S(2)}) copy-start(bf16[8,2048]{1,0:T(8,128)(2,1)} %param.9) | copy-start | bytes 98308
  25.4 4.9 %collective-permute-start = (bf16[256,2048]{1,0:T(8,128)(2,1)S(1)}, bf16[256,2048]{1,0:T(8,128)(2,1)S(1)}, u32[]{:S(2)}, u32[]{:S(2)}) collective-permute-start(bf16[256,2048]{1,0:T(8,128)(2,1)S(1)} %bitcast.10), channel_id=1, source_target_pairs={{0,128},{128,0},{1,129},{129,1},{2,130},{130,2},{3,131},{131,3},{4... | collective-permute-start | bytes 3145736 | tf_op jit(solution)/shard_map/ppermute | solution.py:28
  30.3 1.0 copy-start.11
  51.2 17.3 %collective-permute-start.8 = (bf16[256,2048]{1,0:T(8,128)(2,1)S(1)}, bf16[256,2048]{1,0:T(8,128)(2,1)S(1)}, u32[]{:S(2)}, u32[]{:S(2)}) collective-permute-start(bf16[256,2048]{1,0:T(8,128)(2,1)S(1)} %bitcast.7), channel_id=1, source_target_pairs={{0,128},{128,0},{1,129},{129,1},{2,130},{130,2},{3,131},{131,3},{4... | collective-permute-start | bytes 3145736 | tf_op jit(solution)/shard_map/ppermute | solution.py:28
  53.4 1.5 copy-start.7
  54.9 1.5 copy-start.9
  56.4 1.2 copy-start.12
  57.6 10.9 %copy-start = (bf16[448,2048]{1,0:T(8,128)(2,1)S(1)}, bf16[448,2048]{1,0:T(8,128)(2,1)}, u32[]{:S(2)}) copy-start(bf16[448,2048]{1,0:T(8,128)(2,1)} %refs_0_.3) | copy-start | bytes 5505028
  60.0 15.5 %collective-permute-start.3 = (bf16[2,448,128]{2,1,0:T(8,128)(2,1)S(1)}, bf16[2,448,128]{2,1,0:T(8,128)(2,1)S(1)}, u32[]{:S(2)}, u32[]{:S(2)}) collective-permute-start(bf16[2,448,128]{2,1,0:T(8,128)(2,1)S(1)} %get-tuple-element.23), channel_id=1, source_target_pairs={{0,12},{4,0},{8,4},{12,8},{1,13},{5,1},{9,5},{13,9},{2,14},{6,2},{... | collective-permute-start | bytes 688136 | tf_op jit(solution)/shard_map/ppermute | solution.py:28
  65.3 15.4 %collective-permute-start.2 = (bf16[2,448,128]{2,1,0:T(8,128)(2,1)S(1)}, bf16[2,448,128]{2,1,0:T(8,128)(2,1)S(1)}, u32[]{:S(2)}, u32[]{:S(2)}) collective-permute-start(bf16[2,448,128]{2,1,0:T(8,128)(2,1)S(1)} %get-tuple-element.22), channel_id=1, source_target_pairs={{0,8},{4,12},{8,0},{12,4},{1,9},{5,13},{9,1},{13,5},{2,10},{6,14},... | collective-permute-start | bytes 688136 | tf_op jit(solution)/shard_map/ppermute | solution.py:28
  66.4 15.8 %collective-permute-start.1 = (bf16[2,448,128]{2,1,0:T(8,128)(2,1)S(1)}, bf16[2,448,128]{2,1,0:T(8,128)(2,1)S(1)}, u32[]{:S(2)}, u32[]{:S(2)}) collective-permute-start(bf16[2,448,128]{2,1,0:T(8,128)(2,1)S(1)} %get-tuple-element.21), channel_id=1, source_target_pairs={{0,4},{4,8},{8,12},{12,0},{1,5},{5,9},{9,13},{13,1},{2,6},{6,10},{... | collective-permute-start | bytes 688136 | tf_op jit(solution)/shard_map/ppermute | solution.py:28
  69.8 12.5 %collective-permute-start.11 = (bf16[1,448,128]{2,1,0:T(8,128)(2,1)S(1)}, bf16[1,448,128]{2,1,0:T(8,128)(2,1)S(1)}, u32[]{:S(2)}, u32[]{:S(2)}) collective-permute-start(bf16[1,448,128]{2,1,0:T(8,128)(2,1)S(1)} %get-tuple-element.30), channel_id=1, source_target_pairs={{0,12},{4,0},{8,4},{12,8},{1,13},{5,1},{9,5},{13,9},{2,14},{6,2},{... | collective-permute-start | bytes 344072 | tf_op jit(solution)/shard_map/ppermute | solution.py:28
  71.3 19.2 %collective-permute-start.10 = (bf16[1,448,128]{2,1,0:T(8,128)(2,1)S(1)}, bf16[1,448,128]{2,1,0:T(8,128)(2,1)S(1)}, u32[]{:S(2)}, u32[]{:S(2)}) collective-permute-start(bf16[1,448,128]{2,1,0:T(8,128)(2,1)S(1)} %get-tuple-element.29), channel_id=1, source_target_pairs={{0,8},{4,12},{8,0},{12,4},{1,9},{5,13},{9,1},{13,5},{2,10},{6,14},... | collective-permute-start | bytes 344072 | tf_op jit(solution)/shard_map/ppermute | solution.py:28
  75.6 15.0 %collective-permute-start.9 = (bf16[1,448,128]{2,1,0:T(8,128)(2,1)S(1)}, bf16[1,448,128]{2,1,0:T(8,128)(2,1)S(1)}, u32[]{:S(2)}, u32[]{:S(2)}) collective-permute-start(bf16[1,448,128]{2,1,0:T(8,128)(2,1)S(1)} %get-tuple-element.28), channel_id=1, source_target_pairs={{0,4},{4,8},{8,12},{12,0},{1,5},{5,9},{9,13},{13,1},{2,6},{6,10},{... | collective-permute-start | bytes 344072 | tf_op jit(solution)/shard_map/ppermute | solution.py:28
  91.4 7.8 %collective-permute-start.4 = (bf16[1,448,128]{2,1,0:T(8,128)(2,1)S(1)}, bf16[1,448,128]{2,1,0:T(8,128)(2,1)S(1)}, u32[]{:S(2)}, u32[]{:S(2)}) collective-permute-start(bf16[1,448,128]{2,1,0:T(8,128)(2,1)S(1)} %get-tuple-element.37.refs_0_), channel_id=1, source_target_pairs={{0,12},{4,0},{8,4},{12,8},{1,13},{5,1},{9,5},{13,9},{2,14},{6,2},{... | collective-permute-start | bytes 344072 | tf_op jit(solution)/shard_map/ppermute | solution.py:28
  94.5 8.7 %collective-permute-start.5 = (bf16[1,448,128]{2,1,0:T(8,128)(2,1)S(1)}, bf16[1,448,128]{2,1,0:T(8,128)(2,1)S(1)}, u32[]{:S(2)}, u32[]{:S(2)}) collective-permute-start(bf16[1,448,128]{2,1,0:T(8,128)(2,1)S(1)} %get-tuple-element.37.refs_0_), channel_id=1, source_target_pairs={{0,8},{4,12},{8,0},{12,4},{1,9},{5,13},{9,1},{13,5},{2,10},{6,14},... | collective-permute-start | bytes 344072 | tf_op jit(solution)/shard_map/ppermute | solution.py:28
  98.1 7.9 %collective-permute-start.6 = (bf16[1,448,128]{2,1,0:T(8,128)(2,1)S(1)}, bf16[1,448,128]{2,1,0:T(8,128)(2,1)S(1)}, u32[]{:S(2)}, u32[]{:S(2)}) collective-permute-start(bf16[1,448,128]{2,1,0:T(8,128)(2,1)S(1)} %get-tuple-element.37.refs_0_), channel_id=1, source_target_pairs={{0,4},{4,8},{8,12},{12,0},{1,5},{5,9},{9,13},{13,1},{2,6},{6,10},{... | collective-permute-start | bytes 344072 | tf_op jit(solution)/shard_map/ppermute | solution.py:28
  99.2 9.1 %copy-start.1 = (bf16[1,448,128]{2,1,0:T(8,128)(2,1)}, bf16[1,448,128]{2,1,0:T(8,128)(2,1)S(1)}, u32[]{:S(2)}) copy-start(bf16[1,448,128]{2,1,0:T(8,128)(2,1)S(1)} %collective-permute-done.4.refs_1_) | copy-start | bytes 344068
  103.2 5.1 %copy-start.3 = (bf16[1,448,128]{2,1,0:T(8,128)(2,1)}, bf16[1,448,128]{2,1,0:T(8,128)(2,1)S(1)}, u32[]{:S(2)}) copy-start(bf16[1,448,128]{2,1,0:T(8,128)(2,1)S(1)} %collective-permute-done.5.refs_2_) | copy-start | bytes 344068
  106.0 7.5 %copy-start.5 = (bf16[1,448,128]{2,1,0:T(8,128)(2,1)}, bf16[1,448,128]{2,1,0:T(8,128)(2,1)S(1)}, u32[]{:S(2)}) copy-start(bf16[1,448,128]{2,1,0:T(8,128)(2,1)S(1)} %collective-permute-done.6.refs_3_) | copy-start | bytes 344068
  108.3 7.5 %collective-permute-start.7 = (bf16[256,2048]{1,0:T(8,128)(2,1)S(1)}, bf16[256,2048]{1,0:T(8,128)(2,1)S(1)}, u32[]{:S(2)}, u32[]{:S(2)}) collective-permute-start(bf16[256,2048]{1,0:T(8,128)(2,1)S(1)} %get-tuple-element.25), channel_id=1, source_target_pairs={{0,128},{128,0},{1,129},{129,1},{2,130},{130,2},{3,131},{131,3},{4... | collective-permute-start | bytes 3145736 | tf_op jit(solution)/shard_map/ppermute | solution.py:28
  117.1 54.6 %all-to-all-start.1 = ((bf16[32,8,2048]{2,1,0:T(8,128)(2,1)}), bf16[32,8,2048]{2,1,0:T(8,128)(2,1)}, u32[]{:S(2)}, u32[]{:S(2)}) async-start(bf16[32,8,2048]{2,1,0:T(8,128)(2,1)} %fusion), calls=%async_computation.1 | async-start | bytes 2097152 | tf_op jit(solution)/shard_map/all_to_all | solution.py:150
  127.9 7.7 %collective-permute-start.12 = (bf16[2,448,128]{2,1,0:T(8,128)(2,1)S(1)}, bf16[2,448,128]{2,1,0:T(8,128)(2,1)S(1)}, u32[]{:S(2)}, u32[]{:S(2)}) collective-permute-start(bf16[2,448,128]{2,1,0:T(8,128)(2,1)S(1)} %pad_maximum_fusion.refs_0_), channel_id=1, source_target_pairs={{0,12},{4,0},{8,4},{12,8},{1,13},{5,1},{9,5},{13,9},{2,14},{6,2},{... | collective-permute-start | bytes 688136 | tf_op jit(solution)/shard_map/ppermute | solution.py:28
  129.7 27.0 %collective-permute-start.13 = (bf16[2,448,128]{2,1,0:T(8,128)(2,1)S(1)}, bf16[2,448,128]{2,1,0:T(8,128)(2,1)S(1)}, u32[]{:S(2)}, u32[]{:S(2)}) collective-permute-start(bf16[2,448,128]{2,1,0:T(8,128)(2,1)S(1)} %pad_maximum_fusion.refs_0_), channel_id=1, source_target_pairs={{0,8},{4,12},{8,0},{12,4},{1,9},{5,13},{9,1},{13,5},{2,10},{6,14},... | collective-permute-start | bytes 688136 | tf_op jit(solution)/shard_map/ppermute | solution.py:28
  131.8 28.1 %collective-permute-start.14 = (bf16[2,448,128]{2,1,0:T(8,128)(2,1)S(1)}, bf16[2,448,128]{2,1,0:T(8,128)(2,1)S(1)}, u32[]{:S(2)}, u32[]{:S(2)}) collective-permute-start(bf16[2,448,128]{2,1,0:T(8,128)(2,1)S(1)} %pad_maximum_fusion.refs_0_), channel_id=1, source_target_pairs={{0,4},{4,8},{8,12},{12,0},{1,5},{5,9},{9,13},{13,1},{2,6},{6,10},{... | collective-permute-start | bytes 688136 | tf_op jit(solution)/shard_map/ppermute | solution.py:28
  135.6 31.3 %copy-start.14 = (bf16[2,448,128]{2,1,0:T(8,128)(2,1)}, bf16[2,448,128]{2,1,0:T(8,128)(2,1)S(1)}, u32[]{:S(2)}) copy-start(bf16[2,448,128]{2,1,0:T(8,128)(2,1)S(1)} %collective-permute-done.12.refs_1_) | copy-start | bytes 688132
  156.7 10.2 %copy-start.16 = (bf16[2,448,128]{2,1,0:T(8,128)(2,1)}, bf16[2,448,128]{2,1,0:T(8,128)(2,1)S(1)}, u32[]{:S(2)}) copy-start(bf16[2,448,128]{2,1,0:T(8,128)(2,1)S(1)} %collective-permute-done.13.refs_2_) | copy-start | bytes 688132
  159.9 1.5 copy-start.8
  161.4 1.5 copy-start.10
  162.9 4.0 %copy-start.18 = (bf16[2,448,128]{2,1,0:T(8,128)(2,1)}, bf16[2,448,128]{2,1,0:T(8,128)(2,1)S(1)}, u32[]{:S(2)}) copy-start(bf16[2,448,128]{2,1,0:T(8,128)(2,1)S(1)} %collective-permute-done.14.refs_3_) | copy-start | bytes 688132
  166.9 3.6 %collective-permute-start.15 = (bf16[256,2048]{1,0:T(8,128)(2,1)S(1)}, bf16[256,2048]{1,0:T(8,128)(2,1)S(1)}, u32[]{:S(2)}, u32[]{:S(2)}) collective-permute-start(bf16[256,2048]{1,0:T(8,128)(2,1)S(1)} %get-tuple-element.32), channel_id=1, source_target_pairs={{0,128},{128,0},{1,129},{129,1},{2,130},{130,2},{3,131},{131,3},{4... | collective-permute-start | bytes 3145736 | tf_op jit(solution)/shard_map/ppermute | solution.py:28
  171.8 25.0 %all-to-all-start.3 = ((bf16[32,8,2048]{2,1,0:T(8,128)(2,1)}), bf16[32,8,2048]{2,1,0:T(8,128)(2,1)}, u32[]{:S(2)}, u32[]{:S(2)}) async-start(bf16[32,8,2048]{2,1,0:T(8,128)(2,1)} %fusion.1), calls=%async_computation.3 | async-start | bytes 2097152 | tf_op jit(solution)/shard_map/all_to_all | solution.py:150
  181.6 0.9 copy-start.2
  182.5 0.9 copy-start.4
  183.4 0.9 copy-start.6
  184.3 3.1 %copy-start.13 = (bf16[256,2048]{1,0:T(8,128)(2,1)S(1)}, bf16[256,2048]{1,0:T(8,128)(2,1)}, u32[]{:S(2)}) copy-start(bf16[256,2048]{1,0:T(8,128)(2,1)} %copy-done.11) | copy-start | bytes 3145732
  184.3 3.1 %copy-start.15 = (bf16[2,448,128]{2,1,0:T(8,128)(2,1)S(1)}, bf16[2,448,128]{2,1,0:T(8,128)(2,1)}, u32[]{:S(2)}) copy-start(bf16[2,448,128]{2,1,0:T(8,128)(2,1)} %copy-done.14) | copy-start | bytes 688132
  184.3 3.1 %copy-start.17 = (bf16[2,448,128]{2,1,0:T(8,128)(2,1)S(1)}, bf16[2,448,128]{2,1,0:T(8,128)(2,1)}, u32[]{:S(2)}) copy-start(bf16[2,448,128]{2,1,0:T(8,128)(2,1)} %copy-done.16) | copy-start | bytes 688132
  184.3 3.1 %copy-start.19 = (bf16[2,448,128]{2,1,0:T(8,128)(2,1)S(1)}, bf16[2,448,128]{2,1,0:T(8,128)(2,1)}, u32[]{:S(2)}) copy-start(bf16[2,448,128]{2,1,0:T(8,128)(2,1)} %copy-done.18) | copy-start | bytes 688132

commit v2 on v0

v2 whole, which is shorter than its diff:
```python
import math

import jax
import jax.numpy as jnp
from jax import lax
from jax.experimental import pallas as pl
from jax.experimental.pallas import tpu as pltpu
from jax.sharding import PartitionSpec as P

BF16, F32 = jnp.bfloat16, jnp.float32
PLANE = ("gx", "gz")
WIDTH = 512
WAYS = 4
SMEM = pl.BlockSpec(memory_space=pltpu.SMEM)
VMEM = pl.BlockSpec(memory_space=pltpu.VMEM)
HBM = pl.BlockSpec(memory_space=pltpu.HBM)
PARAMS = pltpu.CompilerParams(vmem_limit_bytes=24 * 1024 * 1024)


def local(kernel, out_shape, *args, scratch=(), flops=1e6, moved=1e6):
    return pl.pallas_call(
        kernel,
        in_specs=[SMEM if a.dtype == jnp.int32 else VMEM for a in args],
        out_specs=[VMEM] * len(out_shape),
        out_shape=[jax.ShapeDtypeStruct(*s) for s in out_shape],
        scratch_shapes=list(scratch),
        compiler_params=PARAMS,
        cost_estimate=pl.CostEstimate(flops=int(flops), bytes_accessed=int(moved), transcendentals=0),
        name=kernel.__name__,
    )(*args)


def swapped(x):
    return lax.ppermute(x, "dcn", [(0, 1), (1, 0)])


def after(x, *others):
    return lax.optimization_barrier((x, *others))[0]


def copies(tokens, out_grad, peers):
    rows, width = tokens.shape

    def copies_of(t_ref, g_ref, out_ref):
        both = jnp.concatenate([t_ref[...].astype(F32), g_ref[...].astype(F32)]).astype(BF16)
        for p in range(peers):
            out_ref[p] = both

    return local(copies_of, [((peers, 2 * rows, width), BF16)], tokens, out_grad)[0]


def parted(rows_of_peers):
    peers, rows, width = rows_of_peers.shape
    half = rows // 2

    def parted_of(in_ref, out_ref):
        for p in range(0, peers, 2):
            first, second = in_ref[p].astype(F32), in_ref[p + 1].astype(F32)
            to = slice(p * half, (p + 2) * half)
            out_ref[0, to] = jnp.concatenate([first[:half], second[:half]]).astype(BF16)
            out_ref[1, to] = jnp.concatenate([first[half:], second[half:]]).astype(BF16)

    return local(parted_of, [((2, peers * half, width), BF16)], rows_of_peers)[0]


def loaded(weights):
    def loaded_of(*refs):
        sems = refs[-1]
        moves = [pltpu.make_async_copy(refs[k], refs[3 + k], sems.at[k]) for k in range(3)]
        for move in moves:
            move.start()
        for move in moves:
            move.wait()

    shape = jax.ShapeDtypeStruct(weights[0].shape, BF16)
    return pl.pallas_call(
        loaded_of,
        in_specs=[HBM] * 3,
        out_specs=[VMEM] * 3,
        out_shape=[shape] * 3,
        scratch_shapes=[pltpu.SemaphoreType.DMA((3,))],
        compiler_params=PARAMS,
        cost_estimate=pl.CostEstimate(flops=1000000, bytes_accessed=20000000, transcendentals=0),
        name="loaded",
    )(*weights)


def partial_sums(own, other, weights):
    units, width = weights[0].shape
    rows = own.shape[1]
    block = rows // 2
    part = 3 * units // 2

    def partial_sums_of(own_ref, other_ref, w0, w1, w2, low, high, after_, before, mine, held):
        for k, w_ref in enumerate((w0, w1, w2)):
            for half, r_ref in enumerate((own_ref, other_ref)):
                sums = lax.dot_general(
                    w_ref[...],
                    r_ref[0 if k < 2 else 1],
                    (((1,), (1,)), ((), ())),
                    preferred_element_type=F32,
                )
                for c in range(2):
                    held[2 * half + c, k * units : (k + 1) * units] = sums[:, c * block : (c + 1) * block]
        me = lax.axis_index("gy")
        far = lax.rem(me + 2, WAYS)
        low[...] = held[far, :part].astype(BF16)
        high[...] = held[far, part:].astype(BF16)
        after_[...] = held[lax.rem(me + 1, WAYS)]
        before[...] = held[lax.rem(me + 3, WAYS)]
        mine[...] = held[me]

    full = ((3 * units, block), F32)
    return local(
        partial_sums_of,
        [((part, block), BF16)] * 2 + [full] * 3,
        own,
        other,
        *weights,
        scratch=[pltpu.VMEM((WAYS, 3 * units, block), F32)],
        flops=12 * units * width * rows,
    )


def shifted(x, by):
    n = lax.axis_size("gy")
    return lax.ppermute(x, "gy", [(i, (i + by) % n) for i in range(n)])


def ring_sums(low, high, following, before, mine):
    rows, block = mine.shape
    part = rows // 2
    low, high = shifted(low, 1), shifted(high, -1)

    def joined_of(low_ref, high_ref, f_ref, b_ref, f_out, b_out):
        f_out[:part] = (f_ref[:part] + low_ref[...].astype(F32)).astype(BF16)
        f_out[part:] = f_ref[part:].astype(BF16)
        b_out[:part] = b_ref[:part].astype(BF16)
        b_out[part:] = (b_ref[part:] + high_ref[...].astype(F32)).astype(BF16)

    following, before = local(joined_of, [((rows, block), BF16)] * 2, low, high, following, before)
    return shifted(following, 1), shifted(before, -1)


def activations(behind, ahead, mine):
    rows, block = mine.shape
    units = rows // 3

    def activations_of(behind_ref, ahead_ref, mine_ref, out_ref):
        def total(k):
            at = slice(k * units, (k + 1) * units)
            return mine_ref[at] + behind_ref[at].astype(F32) + ahead_ref[at].astype(F32)

        gate, up, hidden_grad = total(0), total(1), total(2)
        sigmoid = jax.nn.sigmoid(gate)
        silu = gate * sigmoid
        out_ref[:units] = (silu * up).astype(BF16)
        out_ref[units : 2 * units] = (
            hidden_grad * up * sigmoid * (1.0 + gate * (1.0 - sigmoid))
        ).astype(BF16)
        out_ref[2 * units :] = (hidden_grad * silu).astype(BF16)

    return local(activations_of, [((rows, block), BF16)], behind, ahead, mine)[0]


def ring_gather(mine):
    rows, block = mine.shape
    part = rows // 2
    behind, ahead = shifted(mine, 1), shifted(mine, -1)
    low, high = shifted(behind[:part], 1), shifted(ahead[part:], -1)

    def placed_of(mine_ref, behind_ref, ahead_ref, low_ref, high_ref, out_ref):
        me = lax.axis_index("gy")
        far = lax.rem(me + 2, WAYS)
        out_ref[me] = mine_ref[...]
        out_ref[lax.rem(me + 3, WAYS)] = behind_ref[...]
        out_ref[lax.rem(me + 1, WAYS)] = ahead_ref[...]
        out_ref[far, :part] = low_ref[...]
        out_ref[far, part:] = high_ref[...]

    return local(
        placed_of, [((WAYS, rows, block), BF16)], mine, behind, ahead, low, high
    )[0]


def row_sums(blocks, weights, half, dtype):
    _, rows, block = blocks.shape
    units, width = weights[0].shape

    def row_sums_of(b_ref, w0, w1, w2, out_ref, held):
        for c in range(2):
            for k in range(3):
                at = slice(k * units, (k + 1) * units)
                held[k, c * block : (c + 1) * block] = b_ref[2 * half + c, at].T
        for p in range(width // WIDTH):
            at = slice(p * WIDTH, (p + 1) * WIDTH)
            dot = lambda k, w: jnp.dot(held[k], w[:, at], preferred_element_type=F32)
            out_ref[0, :, at] = dot(0, w2).astype(dtype)
            out_ref[1, :, at] = (dot(1, w0) + dot(2, w1)).astype(dtype)

    return local(
        row_sums_of,
        [((2, 2 * block, width), dtype)],
        blocks,
        *weights,
        scratch=[pltpu.VMEM((3, 2 * block, units), BF16)],
        flops=12 * block * units * width,
    )[0]


def merged(own, other, peers):
    _, rows, width = own.shape
    each = rows // peers

    def merged_of(own_ref, other_ref, out_ref):
        for p in range(0, peers, 2):
            at = slice(p * each, (p + 2) * each)
            out, grad = (own_ref[k, at] + other_ref[k, at].astype(F32) for k in range(2))
            out_ref[p] = jnp.concatenate([out[:each], grad[:each]]).astype(BF16)
            out_ref[p + 1] = jnp.concatenate([out[each:], grad[each:]]).astype(BF16)

    return local(merged_of, [((peers, 2 * each, width), BF16)], own, other)[0]


def totals(parts):
    peers, rows, width = parts.shape

    def totals_of(parts_ref, out_ref, grad_ref):
        for at in range(0, width, WIDTH):
            columns = slice(at, at + WIDTH)
            total = parts_ref[0, :, columns].astype(F32)
            for p in range(1, peers):
                total += parts_ref[p, :, columns].astype(F32)
            out_ref[:, columns] = total[: rows // 2].astype(BF16)
            grad_ref[:, columns] = total[rows // 2 :].astype(BF16)

    return local(totals_of, [((rows // 2, width), BF16)] * 2, parts)


def weight_grads(blocks, own, other, factor):
    _, rows, block = blocks.shape
    units, width = rows // 3, own.shape[2]

    def weight_grads_of(b_ref, own_ref, other_ref, gate_ref, up_ref, down_ref, held):
        @pl.when(pl.program_id(0) == 0)
        def _():
            for k in range(3):
                for c in range(WAYS):
                    at = slice(k * units, (k + 1) * units)
                    held[k, :, c * block : (c + 1) * block] = b_ref[c, at]

        for k, kind, out_ref in ((0, 1, down_ref), (1, 0, gate_ref), (2, 0, up_ref)):
            total = jnp.dot(held[k, :, : 2 * block], own_ref[kind], preferred_element_type=F32)
            total += jnp.dot(held[k, :, 2 * block :], other_ref[kind], preferred_element_type=F32)
            out_ref[...] = (total * factor).astype(BF16)

    token_rows = pl.BlockSpec((2, 2 * block, WIDTH), lambda i: (0, 0, i))
    columns = pl.BlockSpec((units, WIDTH), lambda i: (0, i))
    return pl.pallas_call(
        weight_grads_of,
        grid=(width // WIDTH,),
        in_specs=[VMEM, token_rows, token_rows],
        out_specs=[columns] * 3,
        out_shape=[jax.ShapeDtypeStruct((units, width), BF16)] * 3,
        scratch_shapes=[pltpu.VMEM((3, units, WAYS * block), BF16)],
        compiler_params=PARAMS,
        cost_estimate=pl.CostEstimate(
            flops=24 * block * units * width, bytes_accessed=6 * units * width, transcendentals=0
        ),
        name="weight_grads",
    )(blocks, own, other)


def per_device(tokens, gate_weight, up_weight, down_weight, out_grad):
    rows, width = tokens.shape
    peers = lax.axis_size("gx") * lax.axis_size("gz")
    factor = 1.0 / math.sqrt(rows * lax.axis_size("dcn") * peers)
    weights = (gate_weight, up_weight, down_weight)

    both = copies(tokens, out_grad, peers)
    own = parted(lax.all_to_all(both, PLANE, 0, 0, tiled=True))
    other = swapped(own)
    sums = partial_sums(own, other, weights)
    mine = activations(*ring_sums(*sums), sums[-1])
    blocks = ring_gather(mine)

    theirs = row_sums(blocks, weights, 1, BF16)
    ours = row_sums(after(blocks, theirs), weights, 0, F32)
    merged_rows = merged(ours, swapped(theirs), peers)
    parts = lax.all_to_all(merged_rows, PLANE, 0, 0, tiled=True)
    gate_grad, up_grad, down_grad = weight_grads(after(blocks, merged_rows), own, other, factor)
    output, tokens_grad = totals(parts)
    return output, tokens_grad, gate_grad, up_grad, down_grad


def solution(mesh):
    placed = P(("dcn", "gx", "gz"), "gy")
    return jax.shard_map(
        per_device,
        mesh=mesh,
        in_specs=(placed,) * 5,
        out_specs=(placed,) * 5,
        check_vma=False,
    )
```

time: 923 us -> 154 us (0.17)
  waiting for transfers between devices: 814 us -> 68.9 us
  matrix products: 36.3 us -> 0 us
  starting transfers between devices: 0.52 us -> 27.5 us
  other arithmetic: 15 us -> 0 us
  Pallas kernels: 0 us -> 14.3 us
  between operations: 13.9 us -> 0.78 us
    reduce_scatter x8 -> x0, waiting for transfers between devices: 445 us -> none  [the longest x1 163 us: per_device(): lax.psum_scatter(jnp.dot(gate_rows, w_gate, preferred_element_type=jnp.fl...]
    all_gather x5 -> x0, waiting for transfers between devices: 366 us -> none  [the longest x1 135 us: per_device(): lax.all_gather(out_grad, ('gx', 'gz'), axis=0, tiled=True)]
    ppermute x0 -> x10, waiting for transfers between devices: none -> 50.6 us  [the longest x8 44.8 us: shifted(): return lax.ppermute(x, 'gy', [(i, (i + by) % n) for i in range(n)])]
    all_gather x3 -> x0, blocking collectives: 41.4 us -> none  [the longest x1 16 us: per_device(): lax.all_gather(up_delta, 'gy', axis=0, tiled=True)]
    dot_general x9 -> x0, matrix products: 36.3 us -> none  [the longest x3 13.4 us: by_features(): lax.dot_general(left, right, (((1,), (1,)), ((), ())), preferred_element_...]
    all_to_all x0 -> x1, blocking collectives: none -> 35.2 us  [per_device(): own = parted(lax.all_to_all(both, PLANE, 0, 0, tiled=True))]
    ppermute x0 -> x10, starting transfers between devices: none -> 22.2 us  [the longest x8 18.2 us: shifted(): return lax.ppermute(x, 'gy', [(i, (i + by) % n) for i in range(n)])]
    all_to_all x0 -> x1, waiting for transfers between devices: none -> 18.3 us  [per_device(): parts = lax.all_to_all(merged_rows, PLANE, 0, 0, tiled=True)]
  transfers between devices with their start and end apart: 13 -> 11, of which waited for: 13 -> 9; matrix products, arithmetic and copies ran while one was open for 5% -> 0% of each run, Pallas kernels for 0% -> 5%
where the time goes in v2:
time: 154 us; the launch traced here: 153 us
  waiting for transfers between devices  68.9 us (45%)
  blocking collectives  35.2 us (23%)
  starting transfers between devices  27.5 us (18%)
  Pallas kernels  14.3 us (9%)
  local copies, waits for them, and re-layouts  6.06 us (4%)
    ppermute x8, waiting for transfers between devices, shifted(): return lax.ppermute(x, 'gy', [(i, (i + by) % n) for i in range(n)])  44.8 us
    all_to_all x1, blocking collectives, per_device(): own = parted(lax.all_to_all(both, PLANE, 0, 0, tiled=True))  35.2 us
    all_to_all x1, waiting for transfers between devices, per_device(): parts = lax.all_to_all(merged_rows, PLANE, 0, 0, tiled=True)  18.3 us
    ppermute x8, starting transfers between devices, shifted(): return lax.ppermute(x, 'gy', [(i, (i + by) % n) for i in range(n)])  18.2 us
    pallas_call x10, Pallas kernels, local(): pl.pallas_call(kernel, in_specs=[SMEM if a.dtype == jnp.int32 else VMEM f...  9.2 us
    unnamed x20, local copies, waits for them, and re-layouts  6.03 us
    ppermute x2, waiting for transfers between devices, swapped(): return lax.ppermute(x, 'dcn', [(0, 1), (1, 0)])  5.75 us
    all_to_all x1, starting transfers between devices, per_device(): parts = lax.all_to_all(merged_rows, PLANE, 0, 0, tiled=True)  5.25 us
  transfers between devices with their start and end apart: 11, of which 9 were waited for; matrix products, arithmetic and copies ran while one was open for 0% of the time, Pallas kernels for 5%

profile of v2, /device:TPU:1, one launch (start us, length us, event | category | flops | bytes accessed | tf_op | source)
XLA Modules:
  0.0 152.7 jit_solution(1596201849840519152)
XLA Ops:
  0.6 0.0 copy-start.6
  0.6 0.7 copy-done.6
  1.4 0.8 copy-done.7
  2.1 0.2 copies_of.1
  2.4 0.0 copy-start.3
  2.4 35.2 %all_to_all.10.in_ref = bf16[32,16,2048]{2,1,0:T(8,128)(2,1)S(1)} all-to-all(bf16[32,16,2048]{2,1,0:T(8,128)(2,1)S(1)} %copies_of.1), channel_id=1, replica_groups=mesh['dcn'=2,'gx'=8,'gy'=4,'gz'=4] {'gx','gz'}, dimensions={0} | all-to-all | bytes 4194304 | tf_op jit(solution)/shard_map/all_to_all | solution.py:281
  37.6 0.1 parted_of.1.own_ref
  37.8 0.0 copy-start.4
  37.8 2.7 %collective-permute-start = (bf16[2,256,2048]{2,1,0:T(8,128)(2,1)S(1)}, bf16[2,256,2048]{2,1,0:T(8,128)(2,1)S(1)}, u32[]{:S(2)}, u32[]{:S(2)}) collective-permute-start(bf16[2,256,2048]{2,1,0:T(8,128)(2,1)S(1)} %parted_of.1.own_ref), channel_id=1, source_target_pairs={{0,128},{128,0},{1,129},{129,1},{2,130},{130,2},{3,131},{131,3},{4... | collective-permute-start | bytes 6291464 | tf_op jit(solution)/shard_map/ppermute | solution.py:34
  40.5 3.8 %collective-permute-done.other_ref = bf16[2,256,2048]{2,1,0:T(8,128)(2,1)S(1)} collective-permute-done((bf16[2,256,2048]{2,1,0:T(8,128)(2,1)S(1)}, bf16[2,256,2048]{2,1,0:T(8,128)(2,1)S(1)}, u32[]{:S(2)}, u32[]{:S(2)}) %collective-permute-start) | collective-permute-done | bytes 2097184 | tf_op jit(solution)/shard_map/ppermute | solution.py:34
  44.3 0.0 copy-done.3
  44.3 0.0 copy-done.1
  44.3 0.0 copy-done.2
  44.3 3.6 %partial_sums_of.1 = (bf16[672,128]{1,0:T(8,128)(2,1)S(1)}, bf16[672,128]{1,0:T(8,128)(2,1)S(1)}, f32[1344,128]{1,0:T(8,128)S(1)}, f32[1344,128]{1,0:T(8,128)S(1)}, f32[1344,128]{1,0:T(8,128)S(1)}) custom-call(bf16[2,256,2048]{2,1,0:T(8,128)(2,1)S(1)} %parted_of.1.own_ref, bf16[2,256,2048]{2,1,0:T(8,128)(2,1)S(1)} %collective-permute-done.other_ref, ...), custom_call_target="tpu_custom_call" | custom-call | flops 2818572288 | bytes 1000000 | tf_op jit(solution)/shard_map/partial_sums_of/pallas_call | solution.py:21
  47.9 0.0 copy-done.4
  47.9 0.0 copy-done.8
  47.9 3.1 %collective-permute-start.1 = (bf16[672,128]{1,0:T(8,128)(2,1)S(1)}, bf16[672,128]{1,0:T(8,128)(2,1)S(1)}, u32[]{:S(2)}, u32[]{:S(2)}) collective-permute-start(bf16[672,128]{1,0:T(8,128)(2,1)S(1)} %get-tuple-element.19), channel_id=1, source_target_pairs={{0,4},{4,8},{8,12},{12,0},{1,5},{5,9},{9,13},{13,1},{2,6},{6,10},{... | collective-permute-start | bytes 516104 | tf_op jit(solution)/shard_map/ppermute | solution.py:127
  51.0 2.2 %collective-permute-start.2 = (bf16[672,128]{1,0:T(8,128)(2,1)S(1)}, bf16[672,128]{1,0:T(8,128)(2,1)S(1)}, u32[]{:S(2)}, u32[]{:S(2)}) collective-permute-start(bf16[672,128]{1,0:T(8,128)(2,1)S(1)} %get-tuple-element.20), channel_id=1, source_target_pairs={{0,12},{4,0},{8,4},{12,8},{1,13},{5,1},{9,5},{13,9},{2,14},{6,2},{... | collective-permute-start | bytes 516104 | tf_op jit(solution)/shard_map/ppermute | solution.py:127
  53.2 4.5 %collective-permute-done.1.low_ref = bf16[672,128]{1,0:T(8,128)(2,1)S(1)} collective-permute-done((bf16[672,128]{1,0:T(8,128)(2,1)S(1)}, bf16[672,128]{1,0:T(8,128)(2,1)S(1)}, u32[]{:S(2)}, u32[]{:S(2)}) %collective-permute-start.1) | collective-permute-done | bytes 172064 | tf_op jit(solution)/shard_map/ppermute | solution.py:127
  57.7 3.2 %collective-permute-done.2.high_ref = bf16[672,128]{1,0:T(8,128)(2,1)S(1)} collective-permute-done((bf16[672,128]{1,0:T(8,128)(2,1)S(1)}, bf16[672,128]{1,0:T(8,128)(2,1)S(1)}, u32[]{:S(2)}, u32[]{:S(2)}) %collective-permute-start.2) | collective-permute-done | bytes 172064 | tf_op jit(solution)/shard_map/ppermute | solution.py:127
  60.8 0.1 joined_of.1
  60.9 1.0 collective-permute-start.3
  61.9 2.7 %collective-permute-start.4 = (bf16[1344,128]{1,0:T(8,128)(2,1)S(1)}, bf16[1344,128]{1,0:T(8,128)(2,1)S(1)}, u32[]{:S(2)}, u32[]{:S(2)}) collective-permute-start(bf16[1344,128]{1,0:T(8,128)(2,1)S(1)} %get-tuple-element.24), channel_id=1, source_target_pairs={{0,12},{4,0},{8,4},{12,8},{1,13},{5,1},{9,5},{13,9},{2,14},{6,2},{... | collective-permute-start | bytes 1032200 | tf_op jit(solution)/shard_map/ppermute | solution.py:127
  64.6 7.0 %collective-permute-done.3.behind_ref = bf16[1344,128]{1,0:T(8,128)(2,1)S(1)} collective-permute-done((bf16[1344,128]{1,0:T(8,128)(2,1)S(1)}, bf16[1344,128]{1,0:T(8,128)(2,1)S(1)}, u32[]{:S(2)}, u32[]{:S(2)}) %collective-permute-start.3) | collective-permute-done | bytes 344096 | tf_op jit(solution)/shard_map/ppermute | solution.py:127
  71.6 0.0 collective-permute-done.4.ahead_ref
  71.6 0.2 activations_of.1.mine_ref
  71.8 3.1 %collective-permute-start.6 = (bf16[1344,128]{1,0:T(8,128)(2,1)S(1)}, bf16[1344,128]{1,0:T(8,128)(2,1)S(1)}, u32[]{:S(2)}, u32[]{:S(2)}) collective-permute-start(bf16[1344,128]{1,0:T(8,128)(2,1)S(1)} %activations_of.1.mine_ref), channel_id=1, source_target_pairs={{0,12},{4,0},{8,4},{12,8},{1,13},{5,1},{9,5},{13,9},{2,14},{6,2},{... | collective-permute-start | bytes 1032200 | tf_op jit(solution)/shard_map/ppermute | solution.py:127
  74.9 1.6 %collective-permute-start.5 = (bf16[1344,128]{1,0:T(8,128)(2,1)S(1)}, bf16[1344,128]{1,0:T(8,128)(2,1)S(1)}, u32[]{:S(2)}, u32[]{:S(2)}) collective-permute-start(bf16[1344,128]{1,0:T(8,128)(2,1)S(1)} %activations_of.1.mine_ref), channel_id=1, source_target_pairs={{0,4},{4,8},{8,12},{12,0},{1,5},{5,9},{9,13},{13,1},{2,6},{6,10},{... | collective-permute-start | bytes 1032200 | tf_op jit(solution)/shard_map/ppermute | solution.py:127
  76.6 18.8 %collective-permute-done.6.ahead_ref = bf16[1344,128]{1,0:T(8,128)(2,1)S(1)} collective-permute-done((bf16[1344,128]{1,0:T(8,128)(2,1)S(1)}, bf16[1344,128]{1,0:T(8,128)(2,1)S(1)}, u32[]{:S(2)}, u32[]{:S(2)}) %collective-permute-start.6) | collective-permute-done | bytes 344096 | tf_op jit(solution)/shard_map/ppermute | solution.py:127
  95.4 4.4 %collective-permute-start.8 = (bf16[672,128]{1,0:T(8,128)(2,1)S(1)}, bf16[672,128]{1,0:T(8,128)(2,1)S(1)}, u32[]{:S(2)}, u32[]{:S(2)}) collective-permute-start(bf16[672,128]{1,0:T(8,128)(2,1)S(1)} %slice.9), channel_id=1, source_target_pairs={{0,12},{4,0},{8,4},{12,8},{1,13},{5,1},{9,5},{13,9},{2,14},{6,2},{... | collective-permute-start | bytes 516104 | tf_op jit(solution)/shard_map/ppermute | solution.py:127
  99.8 0.0 collective-permute-done.5.behind_ref
  99.8 0.1 collective-permute-start.7
  99.9 7.2 %collective-permute-done.8.high_ref = bf16[672,128]{1,0:T(8,128)(2,1)S(1)} collective-permute-done((bf16[672,128]{1,0:T(8,128)(2,1)S(1)}, bf16[672,128]{1,0:T(8,128)(2,1)S(1)}, u32[]{:S(2)}, u32[]{:S(2)}) %collective-permute-start.8) | collective-permute-done | bytes 172064 | tf_op jit(solution)/shard_map/ppermute | solution.py:127
  107.1 4.2 %collective-permute-done.7.low_ref = bf16[672,128]{1,0:T(8,128)(2,1)S(1)} collective-permute-done((bf16[672,128]{1,0:T(8,128)(2,1)S(1)}, bf16[672,128]{1,0:T(8,128)(2,1)S(1)}, u32[]{:S(2)}, u32[]{:S(2)}) %collective-permute-start.7) | collective-permute-done | bytes 172064 | tf_op jit(solution)/shard_map/ppermute | solution.py:127
  111.3 0.1 placed_of.1.b_ref
  111.4 1.8 %row_sums_of.2 = bf16[2,256,2048]{2,1,0:T(8,128)(2,1)S(1)} custom-call(bf16[4,1344,128]{2,1,0:T(8,128)(2,1)S(1)} %placed_of.1.b_ref, bf16[448,2048]{1,0:T(8,128)(2,1)S(1)} %copy-done.1, bf16[448,2048]{1,0:T(8,128)(2,1)S(1)} %copy-done.2, bf16[448,2048]{1,0:T(8,128)(2,1)S(1)} %copy-done.3), custom_call_target="tpu_custom_call" | custom-call | flops 1409286144 | bytes 1000000 | tf_op jit(solution)/shard_map/row_sums_of/pallas_call | solution.py:21
  113.2 1.3 collective-permute-start.9
  114.5 1.8 %row_sums_of.3.own_ref = f32[2,256,2048]{2,1,0:T(8,128)S(1)} custom-call(bf16[4,1344,128]{2,1,0:T(8,128)(2,1)S(1)} %placed_of.1.b_ref, bf16[448,2048]{1,0:T(8,128)(2,1)S(1)} %copy-done.1, bf16[448,2048]{1,0:T(8,128)(2,1)S(1)} %copy-done.2, bf16[448,2048]{1,0:T(8,128)(2,1)S(1)} %copy-done.3), custom_call_target="tpu_custom_call" | custom-call | flops 1409286144 | bytes 1000000 | tf_op jit(solution)/shard_map/row_sums_of/pallas_call | solution.py:21
  116.3 2.0 %collective-permute-done.9.other_ref = bf16[2,256,2048]{2,1,0:T(8,128)(2,1)S(1)} collective-permute-done((bf16[2,256,2048]{2,1,0:T(8,128)(2,1)S(1)}, bf16[2,256,2048]{2,1,0:T(8,128)(2,1)S(1)}, u32[]{:S(2)}, u32[]{:S(2)}) %collective-permute-start.9) | collective-permute-done | bytes 2097184 | tf_op jit(solution)/shard_map/ppermute | solution.py:34
  118.3 0.3 merged_of.1
  118.6 0.0 copy-start
  118.6 1.3 copy-done
  120.0 5.2 %all-to-all-start.1 = ((bf16[32,16,2048]{2,1,0:T(8,128)(2,1)}), bf16[32,16,2048]{2,1,0:T(8,128)(2,1)S(1)}, u32[]{:S(2)}, u32[]{:S(2)}) async-start(bf16[32,16,2048]{2,1,0:T(8,128)(2,1)} %copy-done), calls=%async_computation.1 | async-start | bytes 4194304 | tf_op jit(solution)/shard_map/all_to_all | solution.py:290
  125.2 1.6 %copy-done.5 = bf16[2,256,2048]{2,1,0:T(8,128)(2,1)S(1)} copy-done((bf16[2,256,2048]{2,1,0:T(8,128)(2,1)S(1)}, bf16[2,256,2048]{2,1,0:T(8,128)(2,1)}, u32[]{:S(2)}) %copy-start.5) | copy-done | bytes 2097176
  126.8 1.6 %copy-done.9 = bf16[2,256,2048]{2,1,0:T(8,128)(2,1)S(1)} copy-done((bf16[2,256,2048]{2,1,0:T(8,128)(2,1)S(1)}, bf16[2,256,2048]{2,1,0:T(8,128)(2,1)}, u32[]{:S(2)}) %copy-start.9) | copy-done | bytes 2097176
  128.4 5.1 %weight_grads.1 = (bf16[448,2048]{1,0:T(8,128)(2,1)}, bf16[448,2048]{1,0:T(8,128)(2,1)}, bf16[448,2048]{1,0:T(8,128)(2,1)}) custom-call(bf16[4,1344,128]{2,1,0:T(8,128)(2,1)S(1)} %placed_of.1.b_ref, bf16[2,256,2048]{2,1,0:T(8,128)(2,1)S(1)} %copy-done.5, bf16[2,256,2048]{2,1,0:T(8,128)(2,1)S(1)} %copy-done.9), custom_call_target="tpu_custom_call" | custom-call | flops 2818572288 | bytes 5505024 | tf_op jit(solution)/shard_map/weight_grads/pallas_call | solution.py:259
  133.5 18.3 %all-to-all-done.1.parts_ref = bf16[32,16,2048]{2,1,0:T(8,128)(2,1)S(1)} async-done(((bf16[32,16,2048]{2,1,0:T(8,128)(2,1)}), bf16[32,16,2048]{2,1,0:T(8,128)(2,1)S(1)}, u32[]{:S(2)}, u32[]{:S(2)}) %all-to-all-start.1) | async-done | bytes 2097184 | tf_op jit(solution)/shard_map/all_to_all | solution.py:290
  151.8 0.9 totals_of.1
  (8 shorter events, 0.0 us)
Async XLA Ops:
  0.6 0.8 copy-start.6
  1.4 0.8 copy-start.7
  2.4 41.9 %copy-start.3 = (bf16[448,2048]{1,0:T(8,128)(2,1)S(1)}, bf16[448,2048]{1,0:T(8,128)(2,1)}, u32[]{:S(2)}) copy-start(bf16[448,2048]{1,0:T(8,128)(2,1)} %w2.5) | copy-start | bytes 5505028
  37.6 6.7 %copy-start.1 = (bf16[448,2048]{1,0:T(8,128)(2,1)S(1)}, bf16[448,2048]{1,0:T(8,128)(2,1)}, u32[]{:S(2)}) copy-start(bf16[448,2048]{1,0:T(8,128)(2,1)} %w0.5) | copy-start | bytes 5505028
  37.6 6.7 %copy-start.2 = (bf16[448,2048]{1,0:T(8,128)(2,1)S(1)}, bf16[448,2048]{1,0:T(8,128)(2,1)}, u32[]{:S(2)}) copy-start(bf16[448,2048]{1,0:T(8,128)(2,1)} %w1.5) | copy-start | bytes 5505028
  37.8 10.1 %copy-start.4 = (bf16[2,256,2048]{2,1,0:T(8,128)(2,1)}, bf16[2,256,2048]{2,1,0:T(8,128)(2,1)S(1)}, u32[]{:S(2)}) copy-start(bf16[2,256,2048]{2,1,0:T(8,128)(2,1)S(1)} %parted_of.1.own_ref) | copy-start | bytes 6291460
  37.8 6.5 %collective-permute-start = (bf16[2,256,2048]{2,1,0:T(8,128)(2,1)S(1)}, bf16[2,256,2048]{2,1,0:T(8,128)(2,1)S(1)}, u32[]{:S(2)}, u32[]{:S(2)}) collective-permute-start(bf16[2,256,2048]{2,1,0:T(8,128)(2,1)S(1)} %parted_of.1.own_ref), channel_id=1, source_target_pairs={{0,128},{128,0},{1,129},{129,1},{2,130},{130,2},{3,131},{131,3},{4... | collective-permute-start | bytes 6291464 | tf_op jit(solution)/shard_map/ppermute | solution.py:34
  44.3 3.6 %copy-start.8 = (bf16[2,256,2048]{2,1,0:T(8,128)(2,1)}, bf16[2,256,2048]{2,1,0:T(8,128)(2,1)S(1)}, u32[]{:S(2)}) copy-start(bf16[2,256,2048]{2,1,0:T(8,128)(2,1)S(1)} %collective-permute-done.other_ref) | copy-start | bytes 6291460
  47.9 9.8 %collective-permute-start.1 = (bf16[672,128]{1,0:T(8,128)(2,1)S(1)}, bf16[672,128]{1,0:T(8,128)(2,1)S(1)}, u32[]{:S(2)}, u32[]{:S(2)}) collective-permute-start(bf16[672,128]{1,0:T(8,128)(2,1)S(1)} %get-tuple-element.19), channel_id=1, source_target_pairs={{0,4},{4,8},{8,12},{12,0},{1,5},{5,9},{9,13},{13,1},{2,6},{6,10},{... | collective-permute-start | bytes 516104 | tf_op jit(solution)/shard_map/ppermute | solution.py:127
  51.0 9.9 %collective-permute-start.2 = (bf16[672,128]{1,0:T(8,128)(2,1)S(1)}, bf16[672,128]{1,0:T(8,128)(2,1)S(1)}, u32[]{:S(2)}, u32[]{:S(2)}) collective-permute-start(bf16[672,128]{1,0:T(8,128)(2,1)S(1)} %get-tuple-element.20), channel_id=1, source_target_pairs={{0,12},{4,0},{8,4},{12,8},{1,13},{5,1},{9,5},{13,9},{2,14},{6,2},{... | collective-permute-start | bytes 516104 | tf_op jit(solution)/shard_map/ppermute | solution.py:127
  60.9 10.7 %collective-permute-start.3 = (bf16[1344,128]{1,0:T(8,128)(2,1)S(1)}, bf16[1344,128]{1,0:T(8,128)(2,1)S(1)}, u32[]{:S(2)}, u32[]{:S(2)}) collective-permute-start(bf16[1344,128]{1,0:T(8,128)(2,1)S(1)} %get-tuple-element.23), channel_id=1, source_target_pairs={{0,4},{4,8},{8,12},{12,0},{1,5},{5,9},{9,13},{13,1},{2,6},{6,10},{... | collective-permute-start | bytes 1032200 | tf_op jit(solution)/shard_map/ppermute | solution.py:127
  61.9 9.7 %collective-permute-start.4 = (bf16[1344,128]{1,0:T(8,128)(2,1)S(1)}, bf16[1344,128]{1,0:T(8,128)(2,1)S(1)}, u32[]{:S(2)}, u32[]{:S(2)}) collective-permute-start(bf16[1344,128]{1,0:T(8,128)(2,1)S(1)} %get-tuple-element.24), channel_id=1, source_target_pairs={{0,12},{4,0},{8,4},{12,8},{1,13},{5,1},{9,5},{13,9},{2,14},{6,2},{... | collective-permute-start | bytes 1032200 | tf_op jit(solution)/shard_map/ppermute | solution.py:127
  71.8 23.6 %collective-permute-start.6 = (bf16[1344,128]{1,0:T(8,128)(2,1)S(1)}, bf16[1344,128]{1,0:T(8,128)(2,1)S(1)}, u32[]{:S(2)}, u32[]{:S(2)}) collective-permute-start(bf16[1344,128]{1,0:T(8,128)(2,1)S(1)} %activations_of.1.mine_ref), channel_id=1, source_target_pairs={{0,12},{4,0},{8,4},{12,8},{1,13},{5,1},{9,5},{13,9},{2,14},{6,2},{... | collective-permute-start | bytes 1032200 | tf_op jit(solution)/shard_map/ppermute | solution.py:127
  74.9 24.8 %collective-permute-start.5 = (bf16[1344,128]{1,0:T(8,128)(2,1)S(1)}, bf16[1344,128]{1,0:T(8,128)(2,1)S(1)}, u32[]{:S(2)}, u32[]{:S(2)}) collective-permute-start(bf16[1344,128]{1,0:T(8,128)(2,1)S(1)} %activations_of.1.mine_ref), channel_id=1, source_target_pairs={{0,4},{4,8},{8,12},{12,0},{1,5},{5,9},{9,13},{13,1},{2,6},{6,10},{... | collective-permute-start | bytes 1032200 | tf_op jit(solution)/shard_map/ppermute | solution.py:127
  95.4 11.7 %collective-permute-start.8 = (bf16[672,128]{1,0:T(8,128)(2,1)S(1)}, bf16[672,128]{1,0:T(8,128)(2,1)S(1)}, u32[]{:S(2)}, u32[]{:S(2)}) collective-permute-start(bf16[672,128]{1,0:T(8,128)(2,1)S(1)} %slice.9), channel_id=1, source_target_pairs={{0,12},{4,0},{8,4},{12,8},{1,13},{5,1},{9,5},{13,9},{2,14},{6,2},{... | collective-permute-start | bytes 516104 | tf_op jit(solution)/shard_map/ppermute | solution.py:127
  99.8 11.5 %collective-permute-start.7 = (bf16[672,128]{1,0:T(8,128)(2,1)S(1)}, bf16[672,128]{1,0:T(8,128)(2,1)S(1)}, u32[]{:S(2)}, u32[]{:S(2)}) collective-permute-start(bf16[672,128]{1,0:T(8,128)(2,1)S(1)} %slice.8), channel_id=1, source_target_pairs={{0,4},{4,8},{8,12},{12,0},{1,5},{5,9},{9,13},{13,1},{2,6},{6,10},{... | collective-permute-start | bytes 516104 | tf_op jit(solution)/shard_map/ppermute | solution.py:127
  113.2 5.1 %collective-permute-start.9 = (bf16[2,256,2048]{2,1,0:T(8,128)(2,1)S(1)}, bf16[2,256,2048]{2,1,0:T(8,128)(2,1)S(1)}, u32[]{:S(2)}, u32[]{:S(2)}) collective-permute-start(bf16[2,256,2048]{2,1,0:T(8,128)(2,1)S(1)} %row_sums_of.2), channel_id=1, source_target_pairs={{0,128},{128,0},{1,129},{129,1},{2,130},{130,2},{3,131},{131,3},{4... | collective-permute-start | bytes 6291464 | tf_op jit(solution)/shard_map/ppermute | solution.py:34
  118.6 1.3 copy-start
  120.0 31.8 %all-to-all-start.1 = ((bf16[32,16,2048]{2,1,0:T(8,128)(2,1)}), bf16[32,16,2048]{2,1,0:T(8,128)(2,1)S(1)}, u32[]{:S(2)}, u32[]{:S(2)}) async-start(bf16[32,16,2048]{2,1,0:T(8,128)(2,1)} %copy-done), calls=%async_computation.1 | async-start | bytes 4194304 | tf_op jit(solution)/shard_map/all_to_all | solution.py:290
  125.2 1.6 %copy-start.5 = (bf16[2,256,2048]{2,1,0:T(8,128)(2,1)S(1)}, bf16[2,256,2048]{2,1,0:T(8,128)(2,1)}, u32[]{:S(2)}) copy-start(bf16[2,256,2048]{2,1,0:T(8,128)(2,1)} %copy-done.4) | copy-start | bytes 6291460
  126.8 1.6 %copy-start.9 = (bf16[2,256,2048]{2,1,0:T(8,128)(2,1)S(1)}, bf16[2,256,2048]{2,1,0:T(8,128)(2,1)}, u32[]{:S(2)}) copy-start(bf16[2,256,2048]{2,1,0:T(8,128)(2,1)} %copy-done.8) | copy-start | bytes 6291460

commit v3 on v2

v3 whole, which is shorter than its diff:
```python
import math

import jax
import jax.numpy as jnp
from jax import lax
from jax.experimental import pallas as pl
from jax.experimental.pallas import tpu as pltpu
from jax.sharding import PartitionSpec as P

BF16, F32 = jnp.bfloat16, jnp.float32
CUBE = ("dcn", "gx", "gz")
NEAR = 2
WIDTH = 512
WAYS = 4
SMEM = pl.BlockSpec(memory_space=pltpu.SMEM)
VMEM = pl.BlockSpec(memory_space=pltpu.VMEM)
PARAMS = pltpu.CompilerParams(vmem_limit_bytes=24 * 1024 * 1024)


def local(kernel, out_shape, *args, scratch=(), flops=1e6, moved=1e6):
    return pl.pallas_call(
        kernel,
        in_specs=[SMEM if a.dtype == jnp.int32 else VMEM for a in args],
        out_specs=[VMEM] * len(out_shape),
        out_shape=[jax.ShapeDtypeStruct(*s) for s in out_shape],
        scratch_shapes=list(scratch),
        compiler_params=PARAMS,
        cost_estimate=pl.CostEstimate(flops=int(flops), bytes_accessed=int(moved), transcendentals=0),
        name=kernel.__name__,
    )(*args)


def swapped(x):
    return lax.ppermute(x, "dcn", [(0, 1), (1, 0)])


def after(x, *others):
    return lax.optimization_barrier((x, *others))[0]


def copies(tokens, out_grad, peers):
    rows, width = tokens.shape

    def copies_of(t_hbm, g_hbm, out_ref, t_ref, g_ref, sems):
        moves = [
            pltpu.make_async_copy(t_hbm, t_ref, sems.at[0]),
            pltpu.make_async_copy(g_hbm, g_ref, sems.at[1]),
        ]
        for move in moves:
            move.start()
        for move in moves:
            move.wait()
        both = jnp.concatenate([t_ref[...].astype(F32), g_ref[...].astype(F32)]).astype(BF16)
        for p in range(peers):
            out_ref[p] = both

    in_hbm = pl.BlockSpec(memory_space=pltpu.HBM)
    return pl.pallas_call(
        copies_of,
        in_specs=[in_hbm] * 2,
        out_specs=VMEM,
        out_shape=jax.ShapeDtypeStruct((peers, 2 * rows, width), BF16),
        scratch_shapes=[pltpu.VMEM((rows, width), BF16)] * 2 + [pltpu.SemaphoreType.DMA((2,))],
        compiler_params=PARAMS,
        name="copies",
    )(*(pltpu.with_memory_space_constraint(x, pltpu.HBM) for x in (tokens, out_grad)))


def parted(rows_of_peers):
    peers, rows, width = rows_of_peers.shape
    half = rows // 2

    def parted_of(in_ref, t_ref, g_ref):
        for p in range(0, peers, 2):
            first, second = in_ref[p].astype(F32), in_ref[p + 1].astype(F32)
            to = slice(p * half, (p + 2) * half)
            t_ref[to] = jnp.concatenate([first[:half], second[:half]]).astype(BF16)
            g_ref[to] = jnp.concatenate([first[half:], second[half:]]).astype(BF16)

    return local(parted_of, [((peers * half, width), BF16)] * 2, rows_of_peers)


def stacked(*blocks):
    rows, width = blocks[0].shape

    def stacked_of(*refs):
        for k, ref in enumerate(refs[:-1]):
            refs[-1][k * rows : (k + 1) * rows] = ref[...]

    return local(stacked_of, [((len(blocks) * rows, width), BF16)], *blocks)[0]


def sums_into(held, first, w_ref, own_ref, other_ref):
    units, block = w_ref.shape[0], held.shape[-1]
    for half, rows_ref in enumerate((own_ref, other_ref)):
        sums = lax.dot_general(
            w_ref[...], rows_ref[...], (((1,), (1,)), ((), ())), preferred_element_type=F32
        )
        for c in range(2):
            held[2 * half + c, first : first + units] = sums[:, c * block : (c + 1) * block]


def gate_up_sums(own, other, gate, up):
    units, width = gate.shape
    rows = own.shape[0]

    def gate_up_sums_of(own_ref, other_ref, gate_ref, up_ref, out_ref):
        sums_into(out_ref, 0, gate_ref, own_ref, other_ref)
        sums_into(out_ref, units, up_ref, own_ref, other_ref)

    return local(
        gate_up_sums_of,
        [((WAYS, 2 * units, rows // 2), F32)],
        own,
        other,
        gate,
        up,
        flops=8 * units * width * rows,
    )[0]


def ring_blocks(gate_up, own, other, down):
    units, width = down.shape
    rows, block = own.shape[0], gate_up.shape[-1]
    part = 3 * units // 2

    def ring_blocks_of(gu_ref, own_ref, other_ref, w_ref, forth, back, next_, before, mine, held):
        sums_into(held, 0, w_ref, own_ref, other_ref)
        me = lax.axis_index("gy")
        after_, far, last = (lax.rem(me + s, WAYS) for s in (1, 2, 3))
        split = 2 * units - part

        def upper(ref, first, at):
            ref[first : first + split] = gu_ref[at, part:].astype(ref.dtype)
            ref[first + split : first + part] = held[at].astype(ref.dtype)

        forth[:part] = gu_ref[far, :part].astype(BF16)
        upper(forth, part, after_)
        upper(back, 0, far)
        back[part:] = gu_ref[last, :part].astype(BF16)
        next_[...] = gu_ref[after_, :part]
        upper(before, 0, last)
        mine[:part] = gu_ref[me, :part]
        upper(mine, part, me)

    full = (3 * units, block)
    return local(
        ring_blocks_of,
        [(full, BF16)] * 2 + [((part, block), F32)] * 2 + [(full, F32)],
        gate_up,
        own,
        other,
        down,
        scratch=[pltpu.VMEM((WAYS, units, block), F32)],
        flops=4 * units * width * rows,
    )


def shifted(x, by):
    n = lax.axis_size("gy")
    return lax.ppermute(x, "gy", [(i, (i + by) % n) for i in range(n)])


def plane():
    cores, ys, zs = lax.axis_size("dcn"), lax.axis_size("gx") // NEAR, lax.axis_size("gz")
    return cores, ys, zs, lambda d, n, y, z: ((d * NEAR + n) * ys + y) * zs + z


def first_groups():
    cores, ys, zs, place = plane()
    by_z = [[place(0, n, y, z) for n in range(NEAR) for z in range(zs)] for y in range(ys)]
    by_y = [[place(1, n, y, z) for n in range(NEAR) for y in range(ys)] for z in range(zs)]
    return by_z + by_y


def first_exchange(x):
    return lax.all_to_all(x, CUBE, 0, 0, axis_index_groups=first_groups(), tiled=True)


def turned(x, by):
    cores, ys, zs, place = plane()
    pairs = []
    for n in range(NEAR):
        for y in range(ys):
            for z in range(zs):
                pairs.append((place(0, n, y, z), place(0, n, (y + by) % ys, z)))
                pairs.append((place(1, n, y, z), place(1, n, y, (z + by) % zs)))
    return lax.ppermute(x, CUBE, pairs)


def ring_sums(forth, back, following, before):
    rows, block = forth.shape
    part = rows // 2
    behind, ahead = shifted(forth, 1), shifted(back, -1)

    def joined_of(here_ref, there_ref, out_ref):
        out_ref[...] = (here_ref[...] + there_ref[:part].astype(F32)).astype(BF16)

    def joined(here, there):
        return local(joined_of, [((part, block), BF16)], here, there)[0]

    low, high = shifted(joined(following, behind), 1), shifted(joined(before, ahead), -1)
    return behind, ahead, low, high


def activations(behind, ahead, low, high, mine):
    rows, block = mine.shape
    units, part = rows // 3, rows // 2

    def activations_of(behind_ref, ahead_ref, low_ref, high_ref, mine_ref, out_ref, total):
        total[:part] = (
            mine_ref[:part] + low_ref[...].astype(F32) + ahead_ref[part:].astype(F32)
        )
        total[part:] = (
            mine_ref[part:] + high_ref[...].astype(F32) + behind_ref[part:].astype(F32)
        )
        gate, up, hidden_grad = (total[k * units : (k + 1) * units] for k in range(3))
        sigmoid = jax.nn.sigmoid(gate)
        silu = gate * sigmoid
        out_ref[:units] = (silu * up).astype(BF16)
        out_ref[units : 2 * units] = (
            hidden_grad * up * sigmoid * (1.0 + gate * (1.0 - sigmoid))
        ).astype(BF16)
        out_ref[2 * units :] = (hidden_grad * silu).astype(BF16)

    return local(
        activations_of,
        [((rows, block), BF16)],
        behind,
        ahead,
        low,
        high,
        mine,
        scratch=[pltpu.VMEM((rows, block), F32)],
    )[0]


def ring_gather(mine):
    rows, block = mine.shape
    part = rows // 2
    behind, ahead = shifted(mine, 1), shifted(mine, -1)
    low, high = shifted(behind[:part], 1), shifted(ahead[part:], -1)

    def placed_of(mine_ref, behind_ref, ahead_ref, low_ref, high_ref, out_ref):
        me = lax.axis_index("gy")
        far = lax.rem(me + 2, WAYS)
        out_ref[me] = mine_ref[...]
        out_ref[lax.rem(me + 3, WAYS)] = behind_ref[...]
        out_ref[lax.rem(me + 1, WAYS)] = ahead_ref[...]
        out_ref[far, :part] = low_ref[...]
        out_ref[far, part:] = high_ref[...]

    return local(
        placed_of, [((WAYS, rows, block), BF16)], mine, behind, ahead, low, high
    )[0]


def row_sums(blocks, first, weights, half, dtype):
    count, block = len(weights), blocks.shape[-1]
    units, width = weights[0].shape

    def row_sums_of(b_ref, *refs):
        w_refs, out_ref, held = refs[:count], refs[count], refs[count + 1]
        for c in range(2):
            for k in range(count):
                at = slice((first + k) * units, (first + k + 1) * units)
                held[k, c * block : (c + 1) * block] = b_ref[2 * half + c, at].T
        for p in range(width // WIDTH):
            at = slice(p * WIDTH, (p + 1) * WIDTH)
            total = jnp.dot(held[0], w_refs[0][:, at], preferred_element_type=F32)
            for k in range(1, count):
                total += jnp.dot(held[k], w_refs[k][:, at], preferred_element_type=F32)
            out_ref[:, at] = total.astype(dtype)

    return local(
        row_sums_of,
        [((2 * block, width), dtype)],
        blocks,
        *weights,
        scratch=[pltpu.VMEM((count, 2 * block, units), BF16)],
        flops=4 * count * block * units * width,
    )[0]


def merged(own, other):
    rows, width = own.shape
    each = rows // WAYS

    def merged_of(own_ref, other_ref, *out_refs):
        for k, out_ref in enumerate(out_refs):
            at = slice(k * each, (k + 1) * each)
            out_ref[...] = (own_ref[at] + other_ref[at].astype(F32)).astype(out_ref.dtype)

    return local(
        merged_of, [((each, width), F32 if k == 0 else BF16) for k in range(WAYS)], own, other
    )


def collected(outs, grads, peers):
    rows, width = outs[0].shape
    each = rows // peers

    def collected_of(*refs):
        def total(parts, at):
            value = parts[0][at]
            for part in parts[1:]:
                value = value + part[at].astype(F32)
            return value

        for p in range(0, peers, 2):
            at = slice(p * each, (p + 2) * each)
            out, grad = total(refs[:WAYS], at), total(refs[WAYS : 2 * WAYS], at)
            refs[-1][p] = jnp.concatenate([out[:each], grad[:each]]).astype(BF16)
            refs[-1][p + 1] = jnp.concatenate([out[each:], grad[each:]]).astype(BF16)

    return local(collected_of, [((peers, 2 * each, width), BF16)], *outs, *grads)[0]


def totals(parts):
    peers, rows, width = parts.shape

    def totals_of(parts_ref, out_ref, grad_ref):
        for at in range(0, width, WIDTH):
            columns = slice(at, at + WIDTH)
            total = parts_ref[0, :, columns].astype(F32)
            for p in range(1, peers):
                total += parts_ref[p, :, columns].astype(F32)
            out_ref[:, columns] = total[: rows // 2].astype(BF16)
            grad_ref[:, columns] = total[rows // 2 :].astype(BF16)

    return local(totals_of, [((rows // 2, width), BF16)] * 2, parts)


def weight_grads(blocks, own_t, other_t, own_g, other_g, factor):
    _, rows, block = blocks.shape
    units, width = rows // 3, own_t.shape[1]

    def weight_grads_of(b_ref, own_t, other_t, own_g, other_g, gate_ref, up_ref, down_ref, held):
        @pl.when(pl.program_id(0) == 0)
        def _():
            for c in range(WAYS):
                held[:, c * block : (c + 1) * block] = b_ref[c]

        for k, out_ref in enumerate((down_ref, gate_ref, up_ref)):
            own_ref, other_ref = (own_t, other_t) if k else (own_g, other_g)
            at = slice(k * units, (k + 1) * units)
            total = jnp.dot(held[at, : 2 * block], own_ref[...], preferred_element_type=F32)
            total += jnp.dot(held[at, 2 * block :], other_ref[...], preferred_element_type=F32)
            out_ref[...] = (total * factor).astype(BF16)

    token_rows = pl.BlockSpec((2 * block, WIDTH), lambda i: (0, i))
    columns = pl.BlockSpec((units, WIDTH), lambda i: (0, i))
    return pl.pallas_call(
        weight_grads_of,
        grid=(width // WIDTH,),
        in_specs=[VMEM] + [token_rows] * 4,
        out_specs=[columns] * 3,
        out_shape=[jax.ShapeDtypeStruct((units, width), BF16)] * 3,
        scratch_shapes=[pltpu.VMEM((rows, WAYS * block), BF16)],
        compiler_params=PARAMS,
        cost_estimate=pl.CostEstimate(
            flops=8 * block * rows * width, bytes_accessed=2 * rows * width, transcendentals=0
        ),
        name="weight_grads",
    )(blocks, own_t, other_t, own_g, other_g)


def per_device(tokens, gate_weight, up_weight, down_weight, out_grad):
    rows, width = tokens.shape
    factor = 1.0 / math.sqrt(rows * math.prod(lax.axis_size(axis) for axis in CUBE))

    peers = NEAR * lax.axis_size("gz")
    by_peer = first_exchange(copies(tokens, out_grad, peers))
    t_rows, g_rows = parted(by_peer)
    t_rows = [t_rows] + [turned(t_rows, k) for k in (1, 2, 3)]
    g_rows = [g_rows] + [turned(g_rows, k) for k in (1, 2, 3)]
    own_t = stacked(*t_rows)
    other_t = swapped(own_t)
    gate_up = gate_up_sums(own_t, other_t, gate_weight, up_weight)
    own_g = stacked(*g_rows)
    other_g = swapped(own_g)
    *sums, mine = ring_blocks(gate_up, own_g, other_g, down_weight)
    mine = activations(*ring_sums(*sums), mine)
    blocks = ring_gather(mine)

    out_theirs = row_sums(blocks, 0, (down_weight,), 1, BF16)
    grad_theirs = row_sums(after(blocks, out_theirs), 1, (gate_weight, up_weight), 1, BF16)
    out_ours = row_sums(after(blocks, grad_theirs), 0, (down_weight,), 0, F32)
    grad_ours = row_sums(after(blocks, out_ours), 1, (gate_weight, up_weight), 0, F32)
    outs = merged(after(out_ours, grad_ours), swapped(out_theirs))
    outs = [outs[0]] + [turned(outs[k], -k) for k in (1, 2, 3)]
    grads = merged(grad_ours, swapped(grad_theirs))
    rows_all = after((own_t, other_t, own_g, other_g), grads)
    grads = [grads[0]] + [turned(grads[k], -k) for k in (1, 2, 3)]
    gate_grad, up_grad, down_grad = weight_grads(blocks, *rows_all, factor)
    outs[0] = after(outs[0], gate_grad)
    parts = first_exchange(collected(outs, grads, peers))
    output, tokens_grad = totals(parts)
    return output, tokens_grad, gate_grad, up_grad, down_grad


def solution(mesh):
    placed = P(("dcn", "gx", "gz"), "gy")
    return jax.shard_map(
        per_device,
        mesh=mesh,
        in_specs=(placed,) * 5,
        out_specs=(placed,) * 5,
        check_vma=False,
    )
```

time: 154 us -> 137 us (0.89)
  waiting for transfers between devices: 68.9 us -> 53.7 us
  starting transfers between devices: 27.5 us -> 38.5 us
  blocking collectives: 35.2 us -> 28.5 us
  local copies, waits for them, and re-layouts: 6.06 us -> 0.04 us
    all_to_all x1 -> x0, waiting for transfers between devices: 18.3 us -> none  [per_device(): parts = lax.all_to_all(merged_rows, PLANE, 0, 0, tiled=True)]
    ppermute x0 -> x12, starting transfers between devices: none -> 13 us  [turned(): return lax.ppermute(x, CUBE, pairs)]
    ppermute x0 -> x12, waiting for transfers between devices: none -> 11.8 us  [turned(): return lax.ppermute(x, CUBE, pairs)]
    ppermute x2 -> x4, starting transfers between devices: 4.02 us -> 11.2 us  [swapped(): return lax.ppermute(x, 'dcn', [(0, 1), (1, 0)])]
    all_to_all x1 -> x2, blocking collectives: 35.2 us -> 28.5 us  [first_exchange(): lax.all_to_all(x, CUBE, 0, 0, axis_index_groups=first_groups(), tiled=True)]
    unnamed x20 -> x6, local copies, waits for them, and re-layouts: 6.03 us -> 0.01 us
    ppermute x2 -> x4, waiting for transfers between devices: 5.75 us -> 0.34 us  [swapped(): return lax.ppermute(x, 'dcn', [(0, 1), (1, 0)])]
    all_to_all x1 -> x0, starting transfers between devices: 5.25 us -> none  [per_device(): parts = lax.all_to_all(merged_rows, PLANE, 0, 0, tiled=True)]
  transfers between devices with their start and end apart: 11 -> 24, of which waited for: 9 -> 15; matrix products, arithmetic and copies ran while one was open for 0% -> 0% of each run, Pallas kernels for 5% -> 7%
where the time goes in v3:
time: 137 us
  waiting for transfers between devices  53.7 us (39%)
  starting transfers between devices  38.5 us (28%)
  blocking collectives  28.5 us (21%)
  Pallas kernels  15.2 us (11%)
    ppermute x8, waiting for transfers between devices, shifted(): return lax.ppermute(x, 'gy', [(i, (i + by) % n) for i in range(n)])  41.5 us
    all_to_all x2, blocking collectives, first_exchange(): lax.all_to_all(x, CUBE, 0, 0, axis_index_groups=first_groups(), tiled=True)  28.5 us
    ppermute x8, starting transfers between devices, shifted(): return lax.ppermute(x, 'gy', [(i, (i + by) % n) for i in range(n)])  14.2 us
    ppermute x12, starting transfers between devices, turned(): return lax.ppermute(x, CUBE, pairs)  13 us
    ppermute x12, waiting for transfers between devices, turned(): return lax.ppermute(x, CUBE, pairs)  11.8 us
    ppermute x4, starting transfers between devices, swapped(): return lax.ppermute(x, 'dcn', [(0, 1), (1, 0)])  11.2 us
    pallas_call x17, Pallas kernels, local(): pl.pallas_call(kernel, in_specs=[SMEM if a.dtype == jnp.int32 else VMEM f...  9.22 us
    pallas_call x1, Pallas kernels, weight_grads(): pl.pallas_call(weight_grads_of, grid=(width // WIDTH,), in_specs=[VMEM] +...  5.11 us
  transfers between devices with their start and end apart: 24, of which 15 were waited for; matrix products, arithmetic and copies ran while one was open for 0% of the time, Pallas kernels for 7%

profile of v3, /device:TPU:1, one launch (start us, length us, event | category | flops | bytes accessed | tf_op | source)
XLA Modules:
  0.0 136.7 jit_solution(6008958803503811672)
XLA Ops:
  0.6 0.8 copies.1
  1.5 14.5 %all_to_all.10.in_ref = bf16[8,16,2048]{2,1,0:T(8,128)(2,1)S(1)} all-to-all(bf16[8,16,2048]{2,1,0:T(8,128)(2,1)S(1)} %copies.1), channel_id=1, replica_groups={{0,1,2,3,64,65,66,67},{16,17,18,19,80,81,82,83},{32,33,34,35,96,97,98,9..., dimensions={0} | all-to-all | bytes 1048576 | tf_op jit(solution)/shard_map/all_to_all | solution.py:177
  16.0 2.6 %collective-permute-start.2 = (bf16[64,2048]{1,0:T(8,128)(2,1)S(1)}, bf16[64,2048]{1,0:T(8,128)(2,1)S(1)}, u32[]{:S(2)}, u32[]{:S(2)}) collective-permute-start(bf16[64,2048]{1,0:T(8,128)(2,1)S(1)} %get-tuple-element.34.refs_0_), channel_id=1, source_target_pairs={{0,48},{128,131},{1,49},{129,128},{2,50},{130,129},{3,51},{131,130... | collective-permute-start | bytes 786440 | tf_op jit(solution)/shard_map/ppermute | solution.py:188
  18.6 0.2 collective-permute-start.1
  18.8 0.6 collective-permute-start
  19.4 2.0 %collective-permute-start.6 = (bf16[64,2048]{1,0:T(8,128)(2,1)S(1)}, bf16[64,2048]{1,0:T(8,128)(2,1)S(1)}, u32[]{:S(2)}, u32[]{:S(2)}) collective-permute-start(bf16[64,2048]{1,0:T(8,128)(2,1)S(1)} %get-tuple-element.35.refs_0_), channel_id=1, source_target_pairs={{0,48},{128,131},{1,49},{129,128},{2,50},{130,129},{3,51},{131,130... | collective-permute-start | bytes 786440 | tf_op jit(solution)/shard_map/ppermute | solution.py:188
  21.5 1.6 %collective-permute-start.5 = (bf16[64,2048]{1,0:T(8,128)(2,1)S(1)}, bf16[64,2048]{1,0:T(8,128)(2,1)S(1)}, u32[]{:S(2)}, u32[]{:S(2)}) collective-permute-start(bf16[64,2048]{1,0:T(8,128)(2,1)S(1)} %get-tuple-element.35.refs_0_), channel_id=1, source_target_pairs={{0,32},{128,130},{1,33},{129,131},{2,34},{130,128},{3,35},{131,129... | collective-permute-start | bytes 786440 | tf_op jit(solution)/shard_map/ppermute | solution.py:188
  23.0 1.7 %collective-permute-done.2.refs_3_ = bf16[64,2048]{1,0:T(8,128)(2,1)S(1)} collective-permute-done((bf16[64,2048]{1,0:T(8,128)(2,1)S(1)}, bf16[64,2048]{1,0:T(8,128)(2,1)S(1)}, u32[]{:S(2)}, u32[]{:S(2)}) %collective-permute-start.2) | collective-permute-done | bytes 262176 | tf_op jit(solution)/shard_map/ppermute | solution.py:188
  24.7 0.7 collective-permute-done.1.refs_2_
  25.4 2.9 %collective-permute-done.refs_1_ = bf16[64,2048]{1,0:T(8,128)(2,1)S(1)} collective-permute-done((bf16[64,2048]{1,0:T(8,128)(2,1)S(1)}, bf16[64,2048]{1,0:T(8,128)(2,1)S(1)}, u32[]{:S(2)}, u32[]{:S(2)}) %collective-permute-start) | collective-permute-done | bytes 262176 | tf_op jit(solution)/shard_map/ppermute | solution.py:188
  28.4 3.9 %collective-permute-start.3 = (bf16[256,2048]{1,0:T(8,128)(2,1)S(1)}, bf16[256,2048]{1,0:T(8,128)(2,1)S(1)}, u32[]{:S(2)}, u32[]{:S(2)}) collective-permute-start(bf16[256,2048]{1,0:T(8,128)(2,1)S(1)} %stacked_of.2.own_ref.own_t), channel_id=1, source_target_pairs={{0,128},{128,0},{1,129},{129,1},{2,130},{130,2},{3,131},{131,3},{4... | collective-permute-start | bytes 3145736 | tf_op jit(solution)/shard_map/ppermute | solution.py:34
  32.3 1.8 %collective-permute-done.4.refs_1_ = bf16[64,2048]{1,0:T(8,128)(2,1)S(1)} collective-permute-done((bf16[64,2048]{1,0:T(8,128)(2,1)S(1)}, bf16[64,2048]{1,0:T(8,128)(2,1)S(1)}, u32[]{:S(2)}, u32[]{:S(2)}) %collective-permute-start.4) | collective-permute-done | bytes 262176 | tf_op jit(solution)/shard_map/ppermute | solution.py:188
  34.2 3.8 %collective-permute-start.7 = (bf16[256,2048]{1,0:T(8,128)(2,1)S(1)}, bf16[256,2048]{1,0:T(8,128)(2,1)S(1)}, u32[]{:S(2)}, u32[]{:S(2)}) collective-permute-start(bf16[256,2048]{1,0:T(8,128)(2,1)S(1)} %stacked_of.3.own_ref.own_g), channel_id=1, source_target_pairs={{0,128},{128,0},{1,129},{129,1},{2,130},{130,2},{3,131},{131,3},{4... | collective-permute-start | bytes 3145736 | tf_op jit(solution)/shard_map/ppermute | solution.py:34
  38.0 2.1 %gate_up_sums_of.1.gu_ref = f32[4,896,128]{2,1,0:T(8,128)S(1)} custom-call(bf16[256,2048]{1,0:T(8,128)(2,1)S(1)} %stacked_of.2.own_ref.own_t, bf16[256,2048]{1,0:T(8,128)(2,1)S(1)} %collective-permute-done.3.other_ref.other_t, bf16[448,2048]{1,0:T(8,128)(2,1)S(1)} %copy-done.1, bf16[448,2048]{1,0:T(8,128)(2,1)S(1)} %copy-done.2), custom_call_target="tpu_custom_call" | custom-call | flops 1879048192 | bytes 1000000 | tf_op jit(solution)/shard_map/gate_up_sums_of/pallas_call | solution.py:21
  40.1 0.2 collective-permute-done.7.other_ref.other_g
  40.3 1.3 ring_blocks_of.1
  41.6 3.1 %collective-permute-start.8 = (bf16[1344,128]{1,0:T(8,128)(2,1)S(1)}, bf16[1344,128]{1,0:T(8,128)(2,1)S(1)}, u32[]{:S(2)}, u32[]{:S(2)}) collective-permute-start(bf16[1344,128]{1,0:T(8,128)(2,1)S(1)} %get-tuple-element.36), channel_id=1, source_target_pairs={{0,4},{4,8},{8,12},{12,0},{1,5},{5,9},{9,13},{13,1},{2,6},{6,10},{... | collective-permute-start | bytes 1032200 | tf_op jit(solution)/shard_map/ppermute | solution.py:161
  44.6 2.2 %collective-permute-start.9 = (bf16[1344,128]{1,0:T(8,128)(2,1)S(1)}, bf16[1344,128]{1,0:T(8,128)(2,1)S(1)}, u32[]{:S(2)}, u32[]{:S(2)}) collective-permute-start(bf16[1344,128]{1,0:T(8,128)(2,1)S(1)} %get-tuple-element.37), channel_id=1, source_target_pairs={{0,12},{4,0},{8,4},{12,8},{1,13},{5,1},{9,5},{13,9},{2,14},{6,2},{... | collective-permute-start | bytes 1032200 | tf_op jit(solution)/shard_map/ppermute | solution.py:161
  46.9 15.1 %collective-permute-done.8.there_ref.behind_ref = bf16[1344,128]{1,0:T(8,128)(2,1)S(1)} collective-permute-done((bf16[1344,128]{1,0:T(8,128)(2,1)S(1)}, bf16[1344,128]{1,0:T(8,128)(2,1)S(1)}, u32[]{:S(2)}, u32[]{:S(2)}) %collective-permute-start.8) | collective-permute-done | bytes 344096 | tf_op jit(solution)/shard_map/ppermute | solution.py:161
  61.9 0.3 collective-permute-start.10
  62.3 1.6 %collective-permute-done.9.there_ref.ahead_ref = bf16[1344,128]{1,0:T(8,128)(2,1)S(1)} collective-permute-done((bf16[1344,128]{1,0:T(8,128)(2,1)S(1)}, bf16[1344,128]{1,0:T(8,128)(2,1)S(1)}, u32[]{:S(2)}, u32[]{:S(2)}) %collective-permute-start.9) | collective-permute-done | bytes 344096 | tf_op jit(solution)/shard_map/ppermute | solution.py:161
  63.9 2.6 %collective-permute-start.11 = (bf16[672,128]{1,0:T(8,128)(2,1)S(1)}, bf16[672,128]{1,0:T(8,128)(2,1)S(1)}, u32[]{:S(2)}, u32[]{:S(2)}) collective-permute-start(bf16[672,128]{1,0:T(8,128)(2,1)S(1)} %joined_of.3), channel_id=1, source_target_pairs={{0,12},{4,0},{8,4},{12,8},{1,13},{5,1},{9,5},{13,9},{2,14},{6,2},{... | collective-permute-start | bytes 516104 | tf_op jit(solution)/shard_map/ppermute | solution.py:161
  66.4 5.6 %collective-permute-done.10.low_ref = bf16[672,128]{1,0:T(8,128)(2,1)S(1)} collective-permute-done((bf16[672,128]{1,0:T(8,128)(2,1)S(1)}, bf16[672,128]{1,0:T(8,128)(2,1)S(1)}, u32[]{:S(2)}, u32[]{:S(2)}) %collective-permute-start.10) | collective-permute-done | bytes 172064 | tf_op jit(solution)/shard_map/ppermute | solution.py:161
  72.1 2.0 %collective-permute-done.11.high_ref = bf16[672,128]{1,0:T(8,128)(2,1)S(1)} collective-permute-done((bf16[672,128]{1,0:T(8,128)(2,1)S(1)}, bf16[672,128]{1,0:T(8,128)(2,1)S(1)}, u32[]{:S(2)}, u32[]{:S(2)}) %collective-permute-start.11) | collective-permute-done | bytes 172064 | tf_op jit(solution)/shard_map/ppermute | solution.py:161
  74.1 0.2 activations_of.1.mine_ref
  74.3 2.5 %collective-permute-start.13 = (bf16[1344,128]{1,0:T(8,128)(2,1)S(1)}, bf16[1344,128]{1,0:T(8,128)(2,1)S(1)}, u32[]{:S(2)}, u32[]{:S(2)}) collective-permute-start(bf16[1344,128]{1,0:T(8,128)(2,1)S(1)} %activations_of.1.mine_ref), channel_id=1, source_target_pairs={{0,12},{4,0},{8,4},{12,8},{1,13},{5,1},{9,5},{13,9},{2,14},{6,2},{... | collective-permute-start | bytes 1032200 | tf_op jit(solution)/shard_map/ppermute | solution.py:161
  76.9 10.0 %collective-permute-done.13.ahead_ref = bf16[1344,128]{1,0:T(8,128)(2,1)S(1)} collective-permute-done((bf16[1344,128]{1,0:T(8,128)(2,1)S(1)}, bf16[1344,128]{1,0:T(8,128)(2,1)S(1)}, u32[]{:S(2)}, u32[]{:S(2)}) %collective-permute-start.13) | collective-permute-done | bytes 344096 | tf_op jit(solution)/shard_map/ppermute | solution.py:161
  86.9 3.3 %collective-permute-start.15 = (bf16[672,128]{1,0:T(8,128)(2,1)S(1)}, bf16[672,128]{1,0:T(8,128)(2,1)S(1)}, u32[]{:S(2)}, u32[]{:S(2)}) collective-permute-start(bf16[672,128]{1,0:T(8,128)(2,1)S(1)} %slice.9), channel_id=1, source_target_pairs={{0,12},{4,0},{8,4},{12,8},{1,13},{5,1},{9,5},{13,9},{2,14},{6,2},{... | collective-permute-start | bytes 516104 | tf_op jit(solution)/shard_map/ppermute | solution.py:161
  90.4 7.2 %collective-permute-done.15.high_ref = bf16[672,128]{1,0:T(8,128)(2,1)S(1)} collective-permute-done((bf16[672,128]{1,0:T(8,128)(2,1)S(1)}, bf16[672,128]{1,0:T(8,128)(2,1)S(1)}, u32[]{:S(2)}, u32[]{:S(2)}) %collective-permute-start.15) | collective-permute-done | bytes 172064 | tf_op jit(solution)/shard_map/ppermute | solution.py:161
  97.7 0.7 row_sums_of.4
  98.5 1.3 row_sums_of.5
  99.8 3.4 %collective-permute-start.17 = (bf16[256,2048]{1,0:T(8,128)(2,1)S(1)}, bf16[256,2048]{1,0:T(8,128)(2,1)S(1)}, u32[]{:S(2)}, u32[]{:S(2)}) collective-permute-start(bf16[256,2048]{1,0:T(8,128)(2,1)S(1)} %row_sums_of.5), channel_id=1, source_target_pairs={{0,128},{128,0},{1,129},{129,1},{2,130},{130,2},{3,131},{131,3},{4... | collective-permute-start | bytes 3145736 | tf_op jit(solution)/shard_map/ppermute | solution.py:34
  103.3 0.7 row_sums_of.6.own_ref
  104.0 1.3 row_sums_of.7.own_ref
  105.3 0.2 collective-permute-done.17.other_ref
  105.5 0.2 merged_of.3
  105.6 0.6 collective-permute-start.21
  106.2 1.2 collective-permute-start.22
  107.5 0.2 merged_of.2
  107.7 2.8 %collective-permute-start.18 = (bf16[64,2048]{1,0:T(8,128)(2,1)S(1)}, bf16[64,2048]{1,0:T(8,128)(2,1)S(1)}, u32[]{:S(2)}, u32[]{:S(2)}) collective-permute-start(bf16[64,2048]{1,0:T(8,128)(2,1)S(1)} %get-tuple-element.56), channel_id=1, source_target_pairs={{0,48},{128,131},{1,49},{129,128},{2,50},{130,129},{3,51},{131,130... | collective-permute-start | bytes 786440 | tf_op jit(solution)/shard_map/ppermute | solution.py:188
  110.4 0.7 collective-permute-start.19
  111.2 0.6 collective-permute-start.20
  111.9 5.1 %weight_grads.1 = (bf16[448,2048]{1,0:T(8,128)(2,1)}, bf16[448,2048]{1,0:T(8,128)(2,1)}, bf16[448,2048]{1,0:T(8,128)(2,1)}) custom-call(bf16[4,1344,128]{2,1,0:T(8,128)(2,1)S(1)} %placed_of.1.b_ref, bf16[256,2048]{1,0:T(8,128)(2,1)S(1)} %stacked_of.2.own_ref.own_t, bf16[256,2048]{1,0:T(8,128)(2,1)S(1)} %collective-permute-done.3.other_ref.other_t, ...), custom_call_target="tpu_custom_call" | custom-call | flops 2818572288 | bytes 5505024 | tf_op jit(solution)/shard_map/weight_grads/pallas_call | solution.py:353
  117.0 2.0 %collective-permute-done.19.refs_2_ = bf16[64,2048]{1,0:T(8,128)(2,1)S(1)} collective-permute-done((bf16[64,2048]{1,0:T(8,128)(2,1)S(1)}, bf16[64,2048]{1,0:T(8,128)(2,1)S(1)}, u32[]{:S(2)}, u32[]{:S(2)}) %collective-permute-start.19) | collective-permute-done | bytes 262176 | tf_op jit(solution)/shard_map/ppermute | solution.py:188
  119.0 2.7 %collective-permute-done.20.refs_3_ = bf16[64,2048]{1,0:T(8,128)(2,1)S(1)} collective-permute-done((bf16[64,2048]{1,0:T(8,128)(2,1)S(1)}, bf16[64,2048]{1,0:T(8,128)(2,1)S(1)}, u32[]{:S(2)}, u32[]{:S(2)}) %collective-permute-start.20) | collective-permute-done | bytes 262176 | tf_op jit(solution)/shard_map/ppermute | solution.py:188
  121.7 0.2 collected_of.1
  121.9 14.1 %all_to_all.11.parts_ref = bf16[8,16,2048]{2,1,0:T(8,128)(2,1)S(1)} all-to-all(bf16[8,16,2048]{2,1,0:T(8,128)(2,1)S(1)} %collected_of.1), channel_id=1, replica_groups={{0,1,2,3,64,65,66,67},{16,17,18,19,80,81,82,83},{32,33,34,35,96,97,98,9..., dimensions={0} | all-to-all | bytes 1048576 | tf_op jit(solution)/shard_map/all_to_all | solution.py:177
  136.0 0.7 totals_of.1
  (29 shorter events, 0.8 us)
Async XLA Ops:
  16.0 8.8 %collective-permute-start.2 = (bf16[64,2048]{1,0:T(8,128)(2,1)S(1)}, bf16[64,2048]{1,0:T(8,128)(2,1)S(1)}, u32[]{:S(2)}, u32[]{:S(2)}) collective-permute-start(bf16[64,2048]{1,0:T(8,128)(2,1)S(1)} %get-tuple-element.34.refs_0_), channel_id=1, source_target_pairs={{0,48},{128,131},{1,49},{129,128},{2,50},{130,129},{3,51},{131,130... | collective-permute-start | bytes 786440 | tf_op jit(solution)/shard_map/ppermute | solution.py:188
  18.6 6.8 %collective-permute-start.1 = (bf16[64,2048]{1,0:T(8,128)(2,1)S(1)}, bf16[64,2048]{1,0:T(8,128)(2,1)S(1)}, u32[]{:S(2)}, u32[]{:S(2)}) collective-permute-start(bf16[64,2048]{1,0:T(8,128)(2,1)S(1)} %get-tuple-element.34.refs_0_), channel_id=1, source_target_pairs={{0,32},{128,130},{1,33},{129,131},{2,34},{130,128},{3,35},{131,129... | collective-permute-start | bytes 786440 | tf_op jit(solution)/shard_map/ppermute | solution.py:188
  18.8 9.5 %collective-permute-start = (bf16[64,2048]{1,0:T(8,128)(2,1)S(1)}, bf16[64,2048]{1,0:T(8,128)(2,1)S(1)}, u32[]{:S(2)}, u32[]{:S(2)}) collective-permute-start(bf16[64,2048]{1,0:T(8,128)(2,1)S(1)} %get-tuple-element.34.refs_0_), channel_id=1, source_target_pairs={{0,16},{128,129},{1,17},{129,130},{2,18},{130,131},{3,19},{131,128... | collective-permute-start | bytes 786440 | tf_op jit(solution)/shard_map/ppermute | solution.py:188
  19.4 18.6 %copy-start.1 = (bf16[448,2048]{1,0:T(8,128)(2,1)S(1)}, bf16[448,2048]{1,0:T(8,128)(2,1)}, u32[]{:S(2)}) copy-start(bf16[448,2048]{1,0:T(8,128)(2,1)} %refs_0_.7) | copy-start | bytes 5505028
  19.4 18.6 %copy-start.2 = (bf16[448,2048]{1,0:T(8,128)(2,1)S(1)}, bf16[448,2048]{1,0:T(8,128)(2,1)}, u32[]{:S(2)}) copy-start(bf16[448,2048]{1,0:T(8,128)(2,1)} %refs_1_.3) | copy-start | bytes 5505028
  19.4 12.9 %collective-permute-start.6 = (bf16[64,2048]{1,0:T(8,128)(2,1)S(1)}, bf16[64,2048]{1,0:T(8,128)(2,1)S(1)}, u32[]{:S(2)}, u32[]{:S(2)}) collective-permute-start(bf16[64,2048]{1,0:T(8,128)(2,1)S(1)} %get-tuple-element.35.refs_0_), channel_id=1, source_target_pairs={{0,48},{128,131},{1,49},{129,128},{2,50},{130,129},{3,51},{131,130... | collective-permute-start | bytes 786440 | tf_op jit(solution)/shard_map/ppermute | solution.py:188
  21.5 10.9 %collective-permute-start.5 = (bf16[64,2048]{1,0:T(8,128)(2,1)S(1)}, bf16[64,2048]{1,0:T(8,128)(2,1)S(1)}, u32[]{:S(2)}, u32[]{:S(2)}) collective-permute-start(bf16[64,2048]{1,0:T(8,128)(2,1)S(1)} %get-tuple-element.35.refs_0_), channel_id=1, source_target_pairs={{0,32},{128,130},{1,33},{129,131},{2,34},{130,128},{3,35},{131,129... | collective-permute-start | bytes 786440 | tf_op jit(solution)/shard_map/ppermute | solution.py:188
  24.7 9.4 %collective-permute-start.4 = (bf16[64,2048]{1,0:T(8,128)(2,1)S(1)}, bf16[64,2048]{1,0:T(8,128)(2,1)S(1)}, u32[]{:S(2)}, u32[]{:S(2)}) collective-permute-start(bf16[64,2048]{1,0:T(8,128)(2,1)S(1)} %get-tuple-element.35.refs_0_), channel_id=1, source_target_pairs={{0,16},{128,129},{1,17},{129,130},{2,18},{130,131},{3,19},{131,128... | collective-permute-start | bytes 786440 | tf_op jit(solution)/shard_map/ppermute | solution.py:188
  28.4 9.6 %collective-permute-start.3 = (bf16[256,2048]{1,0:T(8,128)(2,1)S(1)}, bf16[256,2048]{1,0:T(8,128)(2,1)S(1)}, u32[]{:S(2)}, u32[]{:S(2)}) collective-permute-start(bf16[256,2048]{1,0:T(8,128)(2,1)S(1)} %stacked_of.2.own_ref.own_t), channel_id=1, source_target_pairs={{0,128},{128,0},{1,129},{129,1},{2,130},{130,2},{3,131},{131,3},{4... | collective-permute-start | bytes 3145736 | tf_op jit(solution)/shard_map/ppermute | solution.py:34
  34.2 6.1 %copy-start = (bf16[448,2048]{1,0:T(8,128)(2,1)S(1)}, bf16[448,2048]{1,0:T(8,128)(2,1)}, u32[]{:S(2)}) copy-start(bf16[448,2048]{1,0:T(8,128)(2,1)} %refs_0_.6) | copy-start | bytes 5505028
  34.2 6.1 %collective-permute-start.7 = (bf16[256,2048]{1,0:T(8,128)(2,1)S(1)}, bf16[256,2048]{1,0:T(8,128)(2,1)S(1)}, u32[]{:S(2)}, u32[]{:S(2)}) collective-permute-start(bf16[256,2048]{1,0:T(8,128)(2,1)S(1)} %stacked_of.3.own_ref.own_g), channel_id=1, source_target_pairs={{0,128},{128,0},{1,129},{129,1},{2,130},{130,2},{3,131},{131,3},{4... | collective-permute-start | bytes 3145736 | tf_op jit(solution)/shard_map/ppermute | solution.py:34
  41.6 20.3 %collective-permute-start.8 = (bf16[1344,128]{1,0:T(8,128)(2,1)S(1)}, bf16[1344,128]{1,0:T(8,128)(2,1)S(1)}, u32[]{:S(2)}, u32[]{:S(2)}) collective-permute-start(bf16[1344,128]{1,0:T(8,128)(2,1)S(1)} %get-tuple-element.36), channel_id=1, source_target_pairs={{0,4},{4,8},{8,12},{12,0},{1,5},{5,9},{9,13},{13,1},{2,6},{6,10},{... | collective-permute-start | bytes 1032200 | tf_op jit(solution)/shard_map/ppermute | solution.py:161
  44.6 19.2 %collective-permute-start.9 = (bf16[1344,128]{1,0:T(8,128)(2,1)S(1)}, bf16[1344,128]{1,0:T(8,128)(2,1)S(1)}, u32[]{:S(2)}, u32[]{:S(2)}) collective-permute-start(bf16[1344,128]{1,0:T(8,128)(2,1)S(1)} %get-tuple-element.37), channel_id=1, source_target_pairs={{0,12},{4,0},{8,4},{12,8},{1,13},{5,1},{9,5},{13,9},{2,14},{6,2},{... | collective-permute-start | bytes 1032200 | tf_op jit(solution)/shard_map/ppermute | solution.py:161
  61.9 10.1 %collective-permute-start.10 = (bf16[672,128]{1,0:T(8,128)(2,1)S(1)}, bf16[672,128]{1,0:T(8,128)(2,1)S(1)}, u32[]{:S(2)}, u32[]{:S(2)}) collective-permute-start(bf16[672,128]{1,0:T(8,128)(2,1)S(1)} %joined_of.2), channel_id=1, source_target_pairs={{0,4},{4,8},{8,12},{12,0},{1,5},{5,9},{9,13},{13,1},{2,6},{6,10},{... | collective-permute-start | bytes 516104 | tf_op jit(solution)/shard_map/ppermute | solution.py:161
  63.9 10.2 %collective-permute-start.11 = (bf16[672,128]{1,0:T(8,128)(2,1)S(1)}, bf16[672,128]{1,0:T(8,128)(2,1)S(1)}, u32[]{:S(2)}, u32[]{:S(2)}) collective-permute-start(bf16[672,128]{1,0:T(8,128)(2,1)S(1)} %joined_of.3), channel_id=1, source_target_pairs={{0,12},{4,0},{8,4},{12,8},{1,13},{5,1},{9,5},{13,9},{2,14},{6,2},{... | collective-permute-start | bytes 516104 | tf_op jit(solution)/shard_map/ppermute | solution.py:161
  74.3 12.6 %collective-permute-start.13 = (bf16[1344,128]{1,0:T(8,128)(2,1)S(1)}, bf16[1344,128]{1,0:T(8,128)(2,1)S(1)}, u32[]{:S(2)}, u32[]{:S(2)}) collective-permute-start(bf16[1344,128]{1,0:T(8,128)(2,1)S(1)} %activations_of.1.mine_ref), channel_id=1, source_target_pairs={{0,12},{4,0},{8,4},{12,8},{1,13},{5,1},{9,5},{13,9},{2,14},{6,2},{... | collective-permute-start | bytes 1032200 | tf_op jit(solution)/shard_map/ppermute | solution.py:161
  76.8 13.4 %collective-permute-start.12 = (bf16[1344,128]{1,0:T(8,128)(2,1)S(1)}, bf16[1344,128]{1,0:T(8,128)(2,1)S(1)}, u32[]{:S(2)}, u32[]{:S(2)}) collective-permute-start(bf16[1344,128]{1,0:T(8,128)(2,1)S(1)} %activations_of.1.mine_ref), channel_id=1, source_target_pairs={{0,4},{4,8},{8,12},{12,0},{1,5},{5,9},{9,13},{13,1},{2,6},{6,10},{... | collective-permute-start | bytes 1032200 | tf_op jit(solution)/shard_map/ppermute | solution.py:161
  86.9 10.7 %collective-permute-start.15 = (bf16[672,128]{1,0:T(8,128)(2,1)S(1)}, bf16[672,128]{1,0:T(8,128)(2,1)S(1)}, u32[]{:S(2)}, u32[]{:S(2)}) collective-permute-start(bf16[672,128]{1,0:T(8,128)(2,1)S(1)} %slice.9), channel_id=1, source_target_pairs={{0,12},{4,0},{8,4},{12,8},{1,13},{5,1},{9,5},{13,9},{2,14},{6,2},{... | collective-permute-start | bytes 516104 | tf_op jit(solution)/shard_map/ppermute | solution.py:161
  90.3 7.3 %collective-permute-start.14 = (bf16[672,128]{1,0:T(8,128)(2,1)S(1)}, bf16[672,128]{1,0:T(8,128)(2,1)S(1)}, u32[]{:S(2)}, u32[]{:S(2)}) collective-permute-start(bf16[672,128]{1,0:T(8,128)(2,1)S(1)} %slice.8), channel_id=1, source_target_pairs={{0,4},{4,8},{8,12},{12,0},{1,5},{5,9},{9,13},{13,1},{2,6},{6,10},{... | collective-permute-start | bytes 516104 | tf_op jit(solution)/shard_map/ppermute | solution.py:161
  99.8 5.7 %collective-permute-start.17 = (bf16[256,2048]{1,0:T(8,128)(2,1)S(1)}, bf16[256,2048]{1,0:T(8,128)(2,1)S(1)}, u32[]{:S(2)}, u32[]{:S(2)}) collective-permute-start(bf16[256,2048]{1,0:T(8,128)(2,1)S(1)} %row_sums_of.5), channel_id=1, source_target_pairs={{0,128},{128,0},{1,129},{129,1},{2,130},{130,2},{3,131},{131,3},{4... | collective-permute-start | bytes 3145736 | tf_op jit(solution)/shard_map/ppermute | solution.py:34
  103.2 4.3 %collective-permute-start.16 = (bf16[256,2048]{1,0:T(8,128)(2,1)S(1)}, bf16[256,2048]{1,0:T(8,128)(2,1)S(1)}, u32[]{:S(2)}, u32[]{:S(2)}) collective-permute-start(bf16[256,2048]{1,0:T(8,128)(2,1)S(1)} %row_sums_of.4), channel_id=1, source_target_pairs={{0,128},{128,0},{1,129},{129,1},{2,130},{130,2},{3,131},{131,3},{4... | collective-permute-start | bytes 3145736 | tf_op jit(solution)/shard_map/ppermute | solution.py:34
  105.6 5.6 %collective-permute-start.21 = (bf16[64,2048]{1,0:T(8,128)(2,1)S(1)}, bf16[64,2048]{1,0:T(8,128)(2,1)S(1)}, u32[]{:S(2)}, u32[]{:S(2)}) collective-permute-start(bf16[64,2048]{1,0:T(8,128)(2,1)S(1)} %get-tuple-element.47), channel_id=1, source_target_pairs={{0,48},{128,131},{1,49},{129,128},{2,50},{130,129},{3,51},{131,130... | collective-permute-start | bytes 786440 | tf_op jit(solution)/shard_map/ppermute | solution.py:188
  106.2 10.8 %collective-permute-start.22 = (bf16[64,2048]{1,0:T(8,128)(2,1)S(1)}, bf16[64,2048]{1,0:T(8,128)(2,1)S(1)}, u32[]{:S(2)}, u32[]{:S(2)}) collective-permute-start(bf16[64,2048]{1,0:T(8,128)(2,1)S(1)} %get-tuple-element.48), channel_id=1, source_target_pairs={{0,32},{128,130},{1,33},{129,131},{2,34},{130,128},{3,35},{131,129... | collective-permute-start | bytes 786440 | tf_op jit(solution)/shard_map/ppermute | solution.py:188
  107.5 9.5 %collective-permute-start.23 = (bf16[64,2048]{1,0:T(8,128)(2,1)S(1)}, bf16[64,2048]{1,0:T(8,128)(2,1)S(1)}, u32[]{:S(2)}, u32[]{:S(2)}) collective-permute-start(bf16[64,2048]{1,0:T(8,128)(2,1)S(1)} %get-tuple-element.49), channel_id=1, source_target_pairs={{0,16},{128,129},{1,17},{129,130},{2,18},{130,131},{3,19},{131,128... | collective-permute-start | bytes 786440 | tf_op jit(solution)/shard_map/ppermute | solution.py:188
  107.7 9.3 %collective-permute-start.18 = (bf16[64,2048]{1,0:T(8,128)(2,1)S(1)}, bf16[64,2048]{1,0:T(8,128)(2,1)S(1)}, u32[]{:S(2)}, u32[]{:S(2)}) collective-permute-start(bf16[64,2048]{1,0:T(8,128)(2,1)S(1)} %get-tuple-element.56), channel_id=1, source_target_pairs={{0,48},{128,131},{1,49},{129,128},{2,50},{130,129},{3,51},{131,130... | collective-permute-start | bytes 786440 | tf_op jit(solution)/shard_map/ppermute | solution.py:188
  110.4 8.5 %collective-permute-start.19 = (bf16[64,2048]{1,0:T(8,128)(2,1)S(1)}, bf16[64,2048]{1,0:T(8,128)(2,1)S(1)}, u32[]{:S(2)}, u32[]{:S(2)}) collective-permute-start(bf16[64,2048]{1,0:T(8,128)(2,1)S(1)} %get-tuple-element.57), channel_id=1, source_target_pairs={{0,32},{128,130},{1,33},{129,131},{2,34},{130,128},{3,35},{131,129... | collective-permute-start | bytes 786440 | tf_op jit(solution)/shard_map/ppermute | solution.py:188
  111.2 10.4 %collective-permute-start.20 = (bf16[64,2048]{1,0:T(8,128)(2,1)S(1)}, bf16[64,2048]{1,0:T(8,128)(2,1)S(1)}, u32[]{:S(2)}, u32[]{:S(2)}) collective-permute-start(bf16[64,2048]{1,0:T(8,128)(2,1)S(1)} %get-tuple-element.58), channel_id=1, source_target_pairs={{0,16},{128,129},{1,17},{129,130},{2,18},{130,131},{3,19},{131,128... | collective-permute-start | bytes 786440 | tf_op jit(solution)/shard_map/ppermute | solution.py:188

commit v4 on v3

v4 whole, which is shorter than its diff:
```python
import math

import jax
import jax.numpy as jnp
from jax import lax
from jax.experimental import pallas as pl
from jax.experimental.pallas import tpu as pltpu
from jax.sharding import PartitionSpec as P

BF16, F32 = jnp.bfloat16, jnp.float32
CUBE = ("dcn", "gx", "gz")
NEAR = 2
WIDTH = 512
WAYS = 4
SMEM = pl.BlockSpec(memory_space=pltpu.SMEM)
VMEM = pl.BlockSpec(memory_space=pltpu.VMEM)
PARAMS = pltpu.CompilerParams(vmem_limit_bytes=24 * 1024 * 1024)


def local(kernel, out_shape, *args, scratch=(), flops=1e6, moved=1e6):
    return pl.pallas_call(
        kernel,
        in_specs=[SMEM if a.dtype == jnp.int32 else VMEM for a in args],
        out_specs=[VMEM] * len(out_shape),
        out_shape=[jax.ShapeDtypeStruct(*s) for s in out_shape],
        scratch_shapes=list(scratch),
        compiler_params=PARAMS,
        cost_estimate=pl.CostEstimate(flops=int(flops), bytes_accessed=int(moved), transcendentals=0),
        name=kernel.__name__,
    )(*args)


def swapped(x):
    return lax.ppermute(x, "dcn", [(0, 1), (1, 0)])


def after(x, *others):
    return lax.optimization_barrier((x, *others))[0]


def copies(tokens, out_grad, peers):
    rows, width = tokens.shape

    def copies_of(t_hbm, g_hbm, out_ref, t_ref, g_ref, sems):
        moves = [
            pltpu.make_async_copy(t_hbm, t_ref, sems.at[0]),
            pltpu.make_async_copy(g_hbm, g_ref, sems.at[1]),
        ]
        for move in moves:
            move.start()
        for move in moves:
            move.wait()
        both = jnp.concatenate([t_ref[...].astype(F32), g_ref[...].astype(F32)]).astype(BF16)
        for p in range(peers):
            out_ref[p] = both

    in_hbm = pl.BlockSpec(memory_space=pltpu.HBM)
    return pl.pallas_call(
        copies_of,
        in_specs=[in_hbm] * 2,
        out_specs=VMEM,
        out_shape=jax.ShapeDtypeStruct((peers, 2 * rows, width), BF16),
        scratch_shapes=[pltpu.VMEM((rows, width), BF16)] * 2 + [pltpu.SemaphoreType.DMA((2,))],
        compiler_params=PARAMS,
        name="copies",
    )(*(pltpu.with_memory_space_constraint(x, pltpu.HBM) for x in (tokens, out_grad)))


def parted(rows_of_peers):
    peers, rows, width = rows_of_peers.shape
    half = rows // 2

    def parted_of(in_ref, t_ref, g_ref):
        for p in range(0, peers, 2):
            first, second = in_ref[p].astype(F32), in_ref[p + 1].astype(F32)
            to = slice(p * half, (p + 2) * half)
            t_ref[to] = jnp.concatenate([first[:half], second[:half]]).astype(BF16)
            g_ref[to] = jnp.concatenate([first[half:], second[half:]]).astype(BF16)

    return local(parted_of, [((peers * half, width), BF16)] * 2, rows_of_peers)


def stacked(*blocks):
    rows, width = blocks[0].shape

    def stacked_of(*refs):
        for k, ref in enumerate(refs[:-1]):
            refs[-1][k * rows : (k + 1) * rows] = ref[...]

    return local(stacked_of, [((len(blocks) * rows, width), BF16)], *blocks)[0]


def sums_into(held, first, w_ref, own_ref, other_ref):
    units, block = w_ref.shape[0], held.shape[-1]
    for half, rows_ref in enumerate((own_ref, other_ref)):
        sums = lax.dot_general(
            w_ref[...], rows_ref[...], (((1,), (1,)), ((), ())), preferred_element_type=F32
        )
        for c in range(2):
            held[2 * half + c, first : first + units] = sums[:, c * block : (c + 1) * block]


def ring_blocks(own, other, weights):
    count = len(weights)
    units, width = weights[0].shape
    rows = own.shape[0]
    block, part = rows // 2, count * units // 2

    def ring_blocks_of(own_ref, other_ref, *refs):
        w_refs = refs[:count]
        forth, back, next_, before, mine, held = refs[count:]
        for k, w_ref in enumerate(w_refs):
            sums_into(held, k * units, w_ref, own_ref, other_ref)
        me = lax.axis_index("gy")
        after_, far, last = (lax.rem(me + s, WAYS) for s in (1, 2, 3))
        forth[:part] = held[far, :part].astype(BF16)
        forth[part:] = held[after_, part:].astype(BF16)
        back[:part] = held[far, part:].astype(BF16)
        back[part:] = held[last, :part].astype(BF16)
        next_[...] = held[after_, :part]
        before[...] = held[last, part:]
        mine[...] = held[me]

    full = (2 * part, block)
    return local(
        ring_blocks_of,
        [(full, BF16)] * 2 + [((part, block), F32)] * 2 + [(full, F32)],
        own,
        other,
        *weights,
        scratch=[pltpu.VMEM((WAYS,) + full, F32)],
        flops=4 * count * units * width * rows,
    )


def shifted(x, by):
    n = lax.axis_size("gy")
    return lax.ppermute(x, "gy", [(i, (i + by) % n) for i in range(n)])


def plane():
    cores, ys, zs = lax.axis_size("dcn"), lax.axis_size("gx") // NEAR, lax.axis_size("gz")
    return cores, ys, zs, lambda d, n, y, z: ((d * NEAR + n) * ys + y) * zs + z


def first_groups():
    cores, ys, zs, place = plane()
    by_z = [[place(0, n, y, z) for n in range(NEAR) for z in range(zs)] for y in range(ys)]
    by_y = [[place(1, n, y, z) for n in range(NEAR) for y in range(ys)] for z in range(zs)]
    return by_z + by_y


def first_exchange(x):
    return lax.all_to_all(x, CUBE, 0, 0, axis_index_groups=first_groups(), tiled=True)


def turned(x, by_even, by_odd):
    cores, ys, zs, place = plane()
    ways = lax.axis_size("gy")
    pairs = []
    for n in range(NEAR):
        for y in range(ys):
            for z in range(zs):
                for g in range(ways):
                    by = by_odd if g % 2 else by_even
                    for d, to in ((0, ((y + by) % ys, z)), (1, (y, (z + by) % zs))):
                        places = place(d, n, y, z), place(d, n, *to)
                        pairs.append(tuple((p // zs * ways + g) * zs + p % zs for p in places))
    return lax.ppermute(x, ("dcn", "gx", "gy", "gz"), pairs)


def joined(here, there):
    part, block = here.shape

    def joined_of(here_ref, there_ref, out_ref):
        out_ref[...] = (here_ref[...] + there_ref[:part].astype(F32)).astype(BF16)

    return local(joined_of, [((part, block), BF16)], here, there)[0]


def block_sum(out, behind_ref, ahead_ref, low_ref, high_ref, mine_ref):
    part = low_ref.shape[0]
    out[:part] = mine_ref[:part] + low_ref[...].astype(F32) + ahead_ref[part:].astype(F32)
    out[part:] = mine_ref[part:] + high_ref[...].astype(F32) + behind_ref[part:].astype(F32)


def activations(*parts):
    rows, block = parts[-1].shape
    units = rows // 2

    def activations_of(behind, ahead, low, high, mine, hidden_ref, gate_ref, up_ref, total):
        block_sum(total, behind, ahead, low, high, mine)
        gate, up = total[:units], total[units:]
        sigmoid = jax.nn.sigmoid(gate)
        hidden_ref[...] = (gate * sigmoid * up).astype(BF16)
        gate_ref[...] = up * sigmoid * (1.0 + gate * (1.0 - sigmoid))
        up_ref[...] = gate * sigmoid

    one = ((units, block), F32)
    return local(
        activations_of,
        [((units, block), BF16), one, one],
        *parts,
        scratch=[pltpu.VMEM((rows, block), F32)],
    )


def deltas_from(hidden, gate_factor, up_factor, *parts):
    units, block = parts[-1].shape

    def deltas_of(hidden_ref, gate_ref, up_ref, behind, ahead, low, high, mine, out_ref, total):
        block_sum(total, behind, ahead, low, high, mine)
        out_ref[:units] = hidden_ref[...]
        out_ref[units : 2 * units] = (total[...] * gate_ref[...]).astype(BF16)
        out_ref[2 * units :] = (total[...] * up_ref[...]).astype(BF16)

    return local(
        deltas_of,
        [((3 * units, block), BF16)],
        hidden,
        gate_factor,
        up_factor,
        *parts,
        scratch=[pltpu.VMEM((units, block), F32)],
    )[0]


def placed(mine, behind, ahead, low, high):
    rows, block = mine.shape
    part = rows // 2

    def placed_of(mine_ref, behind_ref, ahead_ref, low_ref, high_ref, out_ref):
        me = lax.axis_index("gy")
        far = lax.rem(me + 2, WAYS)
        out_ref[me] = mine_ref[...]
        out_ref[lax.rem(me + 3, WAYS)] = behind_ref[...]
        out_ref[lax.rem(me + 1, WAYS)] = ahead_ref[...]
        out_ref[far, :part] = low_ref[...]
        out_ref[far, part:] = high_ref[...]

    return local(placed_of, [((WAYS, rows, block), BF16)], mine, behind, ahead, low, high)[0]


def both_ways(forth, back):
    return shifted(forth, 1), shifted(back, -1)


def early_chunk(me):
    return 3 - lax.rem(me, 2)


def rows_into(held, blocks, w_refs, store):
    gate, up, down = w_refs
    units, width = down.shape
    block = blocks[0].shape[-1]
    for k, ref in enumerate(blocks):
        for which in range(3):
            held[which, k * block : (k + 1) * block] = ref[which * units : (which + 1) * units].T
    for p in range(width // WIDTH):
        at = slice(p * WIDTH, (p + 1) * WIDTH)
        dot = lambda which, w: jnp.dot(held[which], w[:, at], preferred_element_type=F32)
        store(0, at, dot(0, down))
        store(1, at, dot(1, gate) + dot(2, up))


def near_rows(mine, behind, ahead, weights):
    rows, block = mine.shape
    units, width = weights[0].shape

    def near_rows_of(m_ref, b_ref, a_ref, w0, w1, w2, rows_ref, early_ref, held):
        me = lax.axis_index("gy")
        slots = [lax.rem(me + s, WAYS) for s in (0, 3, 1)]

        def store(kind, at, total):
            for k, slot in enumerate(slots):
                rows_ref[slot, kind, :, at] = total[k * block : (k + 1) * block]

        rows_into(held, (m_ref, b_ref, a_ref), (w0, w1, w2), store)
        early_ref[...] = rows_ref[early_chunk(me)].astype(BF16)

    return local(
        near_rows_of,
        [((WAYS, 2, block, width), F32), ((2, block, width), BF16)],
        mine,
        behind,
        ahead,
        *weights,
        scratch=[pltpu.VMEM((3, 3 * block, units), BF16)],
        flops=18 * block * units * width,
    )


def far_rows(low, high, weights, near):
    part, block = low.shape
    units, width = weights[0].shape

    def far_rows_of(low_ref, high_ref, w0, w1, w2, near_ref, rows_ref, late_ref, held, far_block):
        me = lax.axis_index("gy")
        far_block[:part] = low_ref[...]
        far_block[part:] = high_ref[...]

        def store(kind, at, total):
            rows_ref[kind, :, at] = total

        rows_into(held, (far_block,), (w0, w1, w2), store)

        @pl.when(me < 2)
        def _():
            late_ref[...] = rows_ref[...].astype(BF16)

        @pl.when(me >= 2)
        def _():
            late_ref[...] = near_ref[me].astype(BF16)

    return local(
        far_rows_of,
        [((2, block, width), F32), ((2, block, width), BF16)],
        low,
        high,
        *weights,
        near,
        scratch=[pltpu.VMEM((3, block, units), BF16), pltpu.VMEM((2 * part, block), BF16)],
        flops=6 * block * units * width,
    )


def early_quarter(near, early):
    _, _, block, width = near.shape
    each = 2 * block // WAYS

    def early_quarter_of(near_ref, early_ref, out_ref):
        me = lax.axis_index("gy")
        odd = lax.rem(me, 2)
        at = pl.ds(pl.multiple_of(odd * each, each), each)
        for kind in range(2):
            own = near_ref[early_chunk(me) - 2, kind, at]
            out_ref[kind] = (own + early_ref[kind, at].astype(F32)).astype(BF16)

    return local(early_quarter_of, [((2, each, width), BF16)], near, early)[0]


def late_quarters(near, far, early, late):
    _, _, block, width = near.shape
    each = 2 * block // WAYS

    def late_quarters_of(near_ref, far_ref, early_ref, late_ref, mine_ref, *out_refs):
        me = lax.axis_index("gy")
        odd = lax.rem(me, 2)

        def quarter(k, kind):
            chunk, first = k * each // block, k * each % block
            at = slice(first, first + each)
            is_far, is_early = lax.rem(me + 2, WAYS) == chunk, early_chunk(me) == chunk + 2
            own = jnp.where(is_far, far_ref[kind, at], near_ref[chunk, kind, at])
            other = jnp.where(is_early, early_ref[kind, at], late_ref[kind, at])
            return own + other.astype(F32)

        for kind in range(2):
            mine_ref[kind] = quarter(0, kind)

        @pl.when(odd == 1)
        def _():
            for kind in range(2):
                for out_ref, k in zip(out_refs, (2, 3)):
                    out_ref[kind] = quarter(k, kind).astype(BF16)

        @pl.when(odd == 0)
        def _():
            for kind in range(2):
                for out_ref, k in zip(out_refs, (3, 1)):
                    out_ref[kind] = quarter(k, kind).astype(BF16)

    shape = (2, each, width)
    return local(
        late_quarters_of,
        [(shape, F32), (shape, BF16), (shape, BF16)],
        near,
        far,
        early,
        late,
    )


def collected(parts, peers):
    _, rows, width = parts[0].shape
    each = rows // peers

    def collected_of(*refs):
        for p in range(0, peers, 2):
            at = slice(p * each, (p + 2) * each)
            out, grad = refs[0][0, at], refs[0][1, at]
            for ref in refs[1:WAYS]:
                out, grad = out + ref[0, at].astype(F32), grad + ref[1, at].astype(F32)
            refs[-1][p] = jnp.concatenate([out[:each], grad[:each]]).astype(BF16)
            refs[-1][p + 1] = jnp.concatenate([out[each:], grad[each:]]).astype(BF16)

    return local(collected_of, [((peers, 2 * each, width), BF16)], *parts)[0]


def totals(parts):
    peers, rows, width = parts.shape

    def totals_of(parts_ref, out_ref, grad_ref):
        for at in range(0, width, WIDTH):
            columns = slice(at, at + WIDTH)
            total = parts_ref[0, :, columns].astype(F32)
            for p in range(1, peers):
                total += parts_ref[p, :, columns].astype(F32)
            out_ref[:, columns] = total[: rows // 2].astype(BF16)
            grad_ref[:, columns] = total[rows // 2 :].astype(BF16)

    return local(totals_of, [((rows // 2, width), BF16)] * 2, parts)


def weight_grads(blocks, own_t, other_t, own_g, other_g, factor):
    _, rows, block = blocks.shape
    units, width = rows // 3, own_t.shape[1]

    def weight_grads_of(b_ref, own_t, other_t, own_g, other_g, gate_ref, up_ref, down_ref, held):
        @pl.when(pl.program_id(0) == 0)
        def _():
            for c in range(WAYS):
                held[:, c * block : (c + 1) * block] = b_ref[c]

        for k, out_ref in enumerate((down_ref, gate_ref, up_ref)):
            own_ref, other_ref = (own_t, other_t) if k else (own_g, other_g)
            at = slice(k * units, (k + 1) * units)
            total = jnp.dot(held[at, : 2 * block], own_ref[...], preferred_element_type=F32)
            total += jnp.dot(held[at, 2 * block :], other_ref[...], preferred_element_type=F32)
            out_ref[...] = (total * factor).astype(BF16)

    token_rows = pl.BlockSpec((2 * block, WIDTH), lambda i: (0, i))
    columns = pl.BlockSpec((units, WIDTH), lambda i: (0, i))
    return pl.pallas_call(
        weight_grads_of,
        grid=(width // WIDTH,),
        in_specs=[VMEM] + [token_rows] * 4,
        out_specs=[columns] * 3,
        out_shape=[jax.ShapeDtypeStruct((units, width), BF16)] * 3,
        scratch_shapes=[pltpu.VMEM((rows, WAYS * block), BF16)],
        compiler_params=PARAMS,
        cost_estimate=pl.CostEstimate(
            flops=8 * block * rows * width, bytes_accessed=2 * rows * width, transcendentals=0
        ),
        name="weight_grads",
    )(blocks, own_t, other_t, own_g, other_g)


def per_device(tokens, gate_weight, up_weight, down_weight, out_grad):
    rows, width = tokens.shape
    factor = 1.0 / math.sqrt(rows * math.prod(lax.axis_size(axis) for axis in CUBE))

    peers = NEAR * lax.axis_size("gz")
    by_peer = first_exchange(copies(tokens, out_grad, peers))
    t_rows, g_rows = parted(by_peer)
    t_rows = [t_rows] + [turned(t_rows, k, k) for k in (1, 2, 3)]
    g_rows = [g_rows] + [turned(g_rows, k, k) for k in (1, 2, 3)]
    own_t, own_g = stacked(*t_rows), stacked(*g_rows)
    other_t = swapped(own_t)
    *gate_up, gate_up_mine = ring_blocks(own_t, other_t, (gate_weight, up_weight))
    other_g = swapped(own_g)
    *hgrad, hgrad_mine = ring_blocks(own_g, other_g, (down_weight,))

    near = both_ways(*gate_up[:2])
    hgrad_near = both_ways(*hgrad[:2])
    gate_up[2], gate_up[3] = after((gate_up[2], gate_up[3]), hgrad)
    low = joined(gate_up[2], near[0])
    high = joined(gate_up[3], near[1])
    far = both_ways(low, high)
    hgrad_low = joined(after(hgrad[2], low, high), hgrad_near[0])
    hgrad_high = joined(after(hgrad[3], low, high), hgrad_near[1])
    hgrad_far = both_ways(hgrad_low, hgrad_high)
    gate_up_mine = after(gate_up_mine, hgrad_low, hgrad_high)
    hidden, *factors = activations(*near, *far, gate_up_mine)
    blocks = deltas_from(hidden, *factors, *hgrad_near, *hgrad_far, hgrad_mine)
    weights = (gate_weight, up_weight, down_weight)
    mine = blocks
    behind, ahead = both_ways(mine, mine)
    part = mine.shape[0] // 2
    far = both_ways(behind[:part], ahead[part:])
    near, early = near_rows(mine, behind, ahead, weights)
    early = swapped(early)
    first = turned(early_quarter(near, early), -2, -1)
    far_own, late = far_rows(*far, weights, near)
    sums = late_quarters(near, far_own, early, swapped(late))
    blocks = placed(after(mine, sums), behind, ahead, *far)
    sums = [sums[0], first, turned(sums[1], -3, -2), turned(sums[2], -1, -3)]
    gate_grad, up_grad, down_grad = weight_grads(blocks, own_t, other_t, own_g, other_g, factor)
    sums[0] = after(sums[0], gate_grad)
    parts = first_exchange(collected(sums, peers))
    output, tokens_grad = totals(parts)
    return output, tokens_grad, gate_grad, up_grad, down_grad


def solution(mesh):
    placed = P(("dcn", "gx", "gz"), "gy")
    return jax.shard_map(
        per_device,
        mesh=mesh,
        in_specs=(placed,) * 5,
        out_specs=(placed,) * 5,
        check_vma=False,
    )
```

time: 137 us -> 132 us (0.964)
  waiting for transfers between devices: 53.7 us -> 41.2 us
  starting transfers between devices: 38.5 us -> 47.5 us
  blocking collectives: 28.5 us -> 26.9 us
    ppermute x8 -> x12, waiting for transfers between devices: 41.5 us -> 27.4 us  [shifted(): return lax.ppermute(x, 'gy', [(i, (i + by) % n) for i in range(n)])]
    ppermute x8 -> x12, starting transfers between devices: 14.2 us -> 24.1 us  [shifted(): return lax.ppermute(x, 'gy', [(i, (i + by) % n) for i in range(n)])]
    ppermute x12 -> x9, starting transfers between devices: 13 us -> 10.2 us  [turned(): return lax.ppermute(x, ('dcn', 'gx', 'gy', 'gz'), pairs)]
    ppermute x4, starting transfers between devices: 11.2 us -> 13.2 us  [swapped(): return lax.ppermute(x, 'dcn', [(0, 1), (1, 0)])]
    all_to_all x2, blocking collectives: 28.5 us -> 26.9 us  [first_exchange(): lax.all_to_all(x, CUBE, 0, 0, axis_index_groups=first_groups(), tiled=True)]
    ppermute x4, waiting for transfers between devices: 0.34 us -> 1.79 us  [swapped(): return lax.ppermute(x, 'dcn', [(0, 1), (1, 0)])]
    pallas_call x17 -> x18, Pallas kernels: 9.22 us -> 9.78 us  [local(): pl.pallas_call(kernel, in_specs=[SMEM if a.dtype == jnp.int32 else VMEM f...]
    ppermute x12 -> x9, waiting for transfers between devices: 11.8 us -> 12 us  [turned(): return lax.ppermute(x, ('dcn', 'gx', 'gy', 'gz'), pairs)]
  transfers between devices with their start and end apart: 24 -> 25, of which waited for: 15 -> 14; matrix products, arithmetic and copies ran while one was open for 0% -> 0% of each run, Pallas kernels for 7% -> 11%
where the time goes in v4:
time: 132 us
  starting transfers between devices  47.5 us (36%)
  waiting for transfers between devices  41.2 us (31%)
  blocking collectives  26.9 us (20%)
  Pallas kernels  15.7 us (12%)
    ppermute x12, waiting for transfers between devices, shifted(): return lax.ppermute(x, 'gy', [(i, (i + by) % n) for i in range(n)])  27.4 us
    all_to_all x2, blocking collectives, first_exchange(): lax.all_to_all(x, CUBE, 0, 0, axis_index_groups=first_groups(), tiled=True)  26.9 us
    ppermute x12, starting transfers between devices, shifted(): return lax.ppermute(x, 'gy', [(i, (i + by) % n) for i in range(n)])  24.1 us
    ppermute x4, starting transfers between devices, swapped(): return lax.ppermute(x, 'dcn', [(0, 1), (1, 0)])  13.2 us
    ppermute x9, waiting for transfers between devices, turned(): return lax.ppermute(x, ('dcn', 'gx', 'gy', 'gz'), pairs)  12 us
    ppermute x9, starting transfers between devices, turned(): return lax.ppermute(x, ('dcn', 'gx', 'gy', 'gz'), pairs)  10.2 us
    pallas_call x18, Pallas kernels, local(): pl.pallas_call(kernel, in_specs=[SMEM if a.dtype == jnp.int32 else VMEM f...  9.78 us
    pallas_call x1, Pallas kernels, weight_grads(): pl.pallas_call(weight_grads_of, grid=(width // WIDTH,), in_specs=[VMEM] +...  5.13 us
  transfers between devices with their start and end apart: 25, of which 14 were waited for; matrix products, arithmetic and copies ran while one was open for 0% of the time, Pallas kernels for 11%

profile of v4, /device:TPU:1, one launch (start us, length us, event | category | flops | bytes accessed | tf_op | source)
XLA Modules:
  0.0 132.2 jit_solution(14176597306358860866)
XLA Ops:
  0.6 0.8 copies.1
  1.5 14.5 %all_to_all.10.in_ref = bf16[8,16,2048]{2,1,0:T(8,128)(2,1)S(1)} all-to-all(bf16[8,16,2048]{2,1,0:T(8,128)(2,1)S(1)} %copies.1), channel_id=1, replica_groups={{0,1,2,3,64,65,66,67},{16,17,18,19,80,81,82,83},{32,33,34,35,96,97,98,9..., dimensions={0} | all-to-all | bytes 1048576 | tf_op jit(solution)/shard_map/all_to_all | solution.py:154
  16.0 2.6 %collective-permute-start.2 = (bf16[64,2048]{1,0:T(8,128)(2,1)S(1)}, bf16[64,2048]{1,0:T(8,128)(2,1)S(1)}, u32[]{:S(2)}, u32[]{:S(2)}) collective-permute-start(bf16[64,2048]{1,0:T(8,128)(2,1)S(1)} %get-tuple-element.39.refs_0_), channel_id=1, source_target_pairs={{0,48},{128,131},{4,52},{132,135},{8,56},{136,139},{12,60},{140,14... | collective-permute-start | bytes 786440 | tf_op jit(solution)/shard_map/ppermute | solution.py:169
  18.6 0.2 collective-permute-start.1
  18.8 0.6 collective-permute-start
  19.4 2.0 %collective-permute-start.8 = (bf16[64,2048]{1,0:T(8,128)(2,1)S(1)}, bf16[64,2048]{1,0:T(8,128)(2,1)S(1)}, u32[]{:S(2)}, u32[]{:S(2)}) collective-permute-start(bf16[64,2048]{1,0:T(8,128)(2,1)S(1)} %get-tuple-element.44.refs_0_), channel_id=1, source_target_pairs={{0,48},{128,131},{4,52},{132,135},{8,56},{136,139},{12,60},{140,14... | collective-permute-start | bytes 786440 | tf_op jit(solution)/shard_map/ppermute | solution.py:169
  21.5 1.6 %collective-permute-start.7 = (bf16[64,2048]{1,0:T(8,128)(2,1)S(1)}, bf16[64,2048]{1,0:T(8,128)(2,1)S(1)}, u32[]{:S(2)}, u32[]{:S(2)}) collective-permute-start(bf16[64,2048]{1,0:T(8,128)(2,1)S(1)} %get-tuple-element.44.refs_0_), channel_id=1, source_target_pairs={{0,32},{128,130},{4,36},{132,134},{8,40},{136,138},{12,44},{140,14... | collective-permute-start | bytes 786440 | tf_op jit(solution)/shard_map/ppermute | solution.py:169
  23.0 1.7 %collective-permute-done.2.refs_3_ = bf16[64,2048]{1,0:T(8,128)(2,1)S(1)} collective-permute-done((bf16[64,2048]{1,0:T(8,128)(2,1)S(1)}, bf16[64,2048]{1,0:T(8,128)(2,1)S(1)}, u32[]{:S(2)}, u32[]{:S(2)}) %collective-permute-start.2) | collective-permute-done | bytes 262176 | tf_op jit(solution)/shard_map/ppermute | solution.py:169
  24.7 0.7 collective-permute-done.1.refs_2_
  25.4 2.9 %collective-permute-done.refs_1_ = bf16[64,2048]{1,0:T(8,128)(2,1)S(1)} collective-permute-done((bf16[64,2048]{1,0:T(8,128)(2,1)S(1)}, bf16[64,2048]{1,0:T(8,128)(2,1)S(1)}, u32[]{:S(2)}, u32[]{:S(2)}) %collective-permute-start) | collective-permute-done | bytes 262176 | tf_op jit(solution)/shard_map/ppermute | solution.py:169
  28.4 3.9 %collective-permute-start.3 = (bf16[256,2048]{1,0:T(8,128)(2,1)S(1)}, bf16[256,2048]{1,0:T(8,128)(2,1)S(1)}, u32[]{:S(2)}, u32[]{:S(2)}) collective-permute-start(bf16[256,2048]{1,0:T(8,128)(2,1)S(1)} %stacked_of.2.own_ref.own_t), channel_id=1, source_target_pairs={{0,128},{128,0},{1,129},{129,1},{2,130},{130,2},{3,131},{131,3},{4... | collective-permute-start | bytes 3145736 | tf_op jit(solution)/shard_map/ppermute | solution.py:34
  32.3 1.8 %collective-permute-done.6.refs_1_ = bf16[64,2048]{1,0:T(8,128)(2,1)S(1)} collective-permute-done((bf16[64,2048]{1,0:T(8,128)(2,1)S(1)}, bf16[64,2048]{1,0:T(8,128)(2,1)S(1)}, u32[]{:S(2)}, u32[]{:S(2)}) %collective-permute-start.6) | collective-permute-done | bytes 262176 | tf_op jit(solution)/shard_map/ppermute | solution.py:169
  34.2 3.8 %collective-permute-start.9 = (bf16[256,2048]{1,0:T(8,128)(2,1)S(1)}, bf16[256,2048]{1,0:T(8,128)(2,1)S(1)}, u32[]{:S(2)}, u32[]{:S(2)}) collective-permute-start(bf16[256,2048]{1,0:T(8,128)(2,1)S(1)} %stacked_of.3.own_ref.own_g), channel_id=1, source_target_pairs={{0,128},{128,0},{1,129},{129,1},{2,130},{130,2},{3,131},{131,3},{4... | collective-permute-start | bytes 3145736 | tf_op jit(solution)/shard_map/ppermute | solution.py:34
  38.0 2.4 %ring_blocks_of.2 = (bf16[896,128]{1,0:T(8,128)(2,1)S(1)}, bf16[896,128]{1,0:T(8,128)(2,1)S(1)}, f32[448,128]{1,0:T(8,128)S(1)}, f32[448,128]{1,0:T(8,128)S(1)}, f32[896,128]{1,0:T(8,128)S(1)}) custom-call(bf16[256,2048]{1,0:T(8,128)(2,1)S(1)} %stacked_of.2.own_ref.own_t, bf16[256,2048]{1,0:T(8,128)(2,1)S(1)} %collective-permute-done.3.other_ref.other_t, ...), custom_call_target="tpu_custom_call" | custom-call | flops 1879048192 | bytes 1000000 | tf_op jit(solution)/shard_map/ring_blocks_of/pallas_call | solution.py:21
  40.4 3.1 %collective-permute-start.4 = (bf16[896,128]{1,0:T(8,128)(2,1)S(1)}, bf16[896,128]{1,0:T(8,128)(2,1)S(1)}, u32[]{:S(2)}, u32[]{:S(2)}) collective-permute-start(bf16[896,128]{1,0:T(8,128)(2,1)S(1)} %get-tuple-element.40), channel_id=1, source_target_pairs={{0,4},{4,8},{8,12},{12,0},{1,5},{5,9},{9,13},{13,1},{2,6},{6,10},{... | collective-permute-start | bytes 688136 | tf_op jit(solution)/shard_map/ppermute | solution.py:138
  43.5 2.2 %collective-permute-start.5 = (bf16[896,128]{1,0:T(8,128)(2,1)S(1)}, bf16[896,128]{1,0:T(8,128)(2,1)S(1)}, u32[]{:S(2)}, u32[]{:S(2)}) collective-permute-start(bf16[896,128]{1,0:T(8,128)(2,1)S(1)} %get-tuple-element.41), channel_id=1, source_target_pairs={{0,12},{4,0},{8,4},{12,8},{1,13},{5,1},{9,5},{13,9},{2,14},{6,2},{... | collective-permute-start | bytes 688136 | tf_op jit(solution)/shard_map/ppermute | solution.py:138
  45.7 1.3 ring_blocks_of.3
  47.0 1.2 collective-permute-start.12
  48.2 2.5 %collective-permute-start.13 = (bf16[448,128]{1,0:T(8,128)(2,1)S(1)}, bf16[448,128]{1,0:T(8,128)(2,1)S(1)}, u32[]{:S(2)}, u32[]{:S(2)}) collective-permute-start(bf16[448,128]{1,0:T(8,128)(2,1)S(1)} %get-tuple-element.46), channel_id=1, source_target_pairs={{0,12},{4,0},{8,4},{12,8},{1,13},{5,1},{9,5},{13,9},{2,14},{6,2},{... | collective-permute-start | bytes 344072 | tf_op jit(solution)/shard_map/ppermute | solution.py:138
  50.6 4.9 %collective-permute-done.4.there_ref.behind = bf16[896,128]{1,0:T(8,128)(2,1)S(1)} collective-permute-done((bf16[896,128]{1,0:T(8,128)(2,1)S(1)}, bf16[896,128]{1,0:T(8,128)(2,1)S(1)}, u32[]{:S(2)}, u32[]{:S(2)}) %collective-permute-start.4) | collective-permute-done | bytes 229408 | tf_op jit(solution)/shard_map/ppermute | solution.py:138
  55.6 1.7 %collective-permute-start.10 = (bf16[448,128]{1,0:T(8,128)(2,1)S(1)}, bf16[448,128]{1,0:T(8,128)(2,1)S(1)}, u32[]{:S(2)}, u32[]{:S(2)}) collective-permute-start(bf16[448,128]{1,0:T(8,128)(2,1)S(1)} %joined_of.4), channel_id=1, source_target_pairs={{0,4},{4,8},{8,12},{12,0},{1,5},{5,9},{9,13},{13,1},{2,6},{6,10},{... | collective-permute-start | bytes 344072 | tf_op jit(solution)/shard_map/ppermute | solution.py:138
  57.2 3.1 %collective-permute-done.5.there_ref.ahead = bf16[896,128]{1,0:T(8,128)(2,1)S(1)} collective-permute-done((bf16[896,128]{1,0:T(8,128)(2,1)S(1)}, bf16[896,128]{1,0:T(8,128)(2,1)S(1)}, u32[]{:S(2)}, u32[]{:S(2)}) %collective-permute-start.5) | collective-permute-done | bytes 229408 | tf_op jit(solution)/shard_map/ppermute | solution.py:138
  60.3 2.5 %collective-permute-start.11 = (bf16[448,128]{1,0:T(8,128)(2,1)S(1)}, bf16[448,128]{1,0:T(8,128)(2,1)S(1)}, u32[]{:S(2)}, u32[]{:S(2)}) collective-permute-start(bf16[448,128]{1,0:T(8,128)(2,1)S(1)} %joined_of.5), channel_id=1, source_target_pairs={{0,12},{4,0},{8,4},{12,8},{1,13},{5,1},{9,5},{13,9},{2,14},{6,2},{... | collective-permute-start | bytes 344072 | tf_op jit(solution)/shard_map/ppermute | solution.py:138
  62.8 0.3 collective-permute-done.12.there_ref.behind
  63.1 1.0 collective-permute-start.14
  64.1 2.8 %collective-permute-start.15 = (bf16[224,128]{1,0:T(8,128)(2,1)S(1)}, bf16[224,128]{1,0:T(8,128)(2,1)S(1)}, u32[]{:S(2)}, u32[]{:S(2)}) collective-permute-start(bf16[224,128]{1,0:T(8,128)(2,1)S(1)} %joined_of.7), channel_id=1, source_target_pairs={{0,12},{4,0},{8,4},{12,8},{1,13},{5,1},{9,5},{13,9},{2,14},{6,2},{... | collective-permute-start | bytes 172040 | tf_op jit(solution)/shard_map/ppermute | solution.py:138
  66.9 0.4 collective-permute-done.10.low
  67.3 2.5 %collective-permute-done.11.high = bf16[448,128]{1,0:T(8,128)(2,1)S(1)} collective-permute-done((bf16[448,128]{1,0:T(8,128)(2,1)S(1)}, bf16[448,128]{1,0:T(8,128)(2,1)S(1)}, u32[]{:S(2)}, u32[]{:S(2)}) %collective-permute-start.11) | collective-permute-done | bytes 114720 | tf_op jit(solution)/shard_map/ppermute | solution.py:138
  69.8 0.2 activations_of.1
  69.9 1.4 %collective-permute-done.15.high = bf16[224,128]{1,0:T(8,128)(2,1)S(1)} collective-permute-done((bf16[224,128]{1,0:T(8,128)(2,1)S(1)}, bf16[224,128]{1,0:T(8,128)(2,1)S(1)}, u32[]{:S(2)}, u32[]{:S(2)}) %collective-permute-start.15) | collective-permute-done | bytes 57376 | tf_op jit(solution)/shard_map/ppermute | solution.py:138
  71.4 1.3 %collective-permute-start.17 = (bf16[1344,128]{1,0:T(8,128)(2,1)S(1)}, bf16[1344,128]{1,0:T(8,128)(2,1)S(1)}, u32[]{:S(2)}, u32[]{:S(2)}) collective-permute-start(bf16[1344,128]{1,0:T(8,128)(2,1)S(1)} %deltas_of.1.m_ref.mine_ref), channel_id=1, source_target_pairs={{0,12},{4,0},{8,4},{12,8},{1,13},{5,1},{9,5},{13,9},{2,14},{6,2},{... | collective-permute-start | bytes 1032200 | tf_op jit(solution)/shard_map/ppermute | solution.py:138
  72.7 1.4 %collective-permute-start.16 = (bf16[1344,128]{1,0:T(8,128)(2,1)S(1)}, bf16[1344,128]{1,0:T(8,128)(2,1)S(1)}, u32[]{:S(2)}, u32[]{:S(2)}) collective-permute-start(bf16[1344,128]{1,0:T(8,128)(2,1)S(1)} %deltas_of.1.m_ref.mine_ref), channel_id=1, source_target_pairs={{0,4},{4,8},{8,12},{12,0},{1,5},{5,9},{9,13},{13,1},{2,6},{6,10},{... | collective-permute-start | bytes 1032200 | tf_op jit(solution)/shard_map/ppermute | solution.py:138
  74.2 12.3 %collective-permute-done.17.a_ref.ahead_ref = bf16[1344,128]{1,0:T(8,128)(2,1)S(1)} collective-permute-done((bf16[1344,128]{1,0:T(8,128)(2,1)S(1)}, bf16[1344,128]{1,0:T(8,128)(2,1)S(1)}, u32[]{:S(2)}, u32[]{:S(2)}) %collective-permute-start.17) | collective-permute-done | bytes 344096 | tf_op jit(solution)/shard_map/ppermute | solution.py:138
  86.5 4.4 %collective-permute-start.19 = (bf16[672,128]{1,0:T(8,128)(2,1)S(1)}, bf16[672,128]{1,0:T(8,128)(2,1)S(1)}, u32[]{:S(2)}, u32[]{:S(2)}) collective-permute-start(bf16[672,128]{1,0:T(8,128)(2,1)S(1)} %slice.9), channel_id=1, source_target_pairs={{0,12},{4,0},{8,4},{12,8},{1,13},{5,1},{9,5},{13,9},{2,14},{6,2},{... | collective-permute-start | bytes 516104 | tf_op jit(solution)/shard_map/ppermute | solution.py:138
  91.0 3.0 %near_rows_of.1 = (f32[4,2,128,2048]{3,2,1,0:T(8,128)S(1)}, bf16[2,128,2048]{2,1,0:T(8,128)(2,1)S(1)}) custom-call(bf16[1344,128]{1,0:T(8,128)(2,1)S(1)} %deltas_of.1.m_ref.mine_ref, bf16[1344,128]{1,0:T(8,128)(2,1)S(1)} %collective-permute-done.16.b_ref.behind_ref, bf16[1344,128]{1,0:T(8,128)(2,1)S(1)} %collective-permute-done.17.a_ref.ahead_ref, ...), custom_call_target="tpu_custom_call" | custom-call | flops 2113929216 | bytes 1000000 | tf_op jit(solution)/shard_map/near_rows_of/pallas_call | solution.py:21
  93.9 3.3 %collective-permute-start.20 = (bf16[2,128,2048]{2,1,0:T(8,128)(2,1)S(1)}, bf16[2,128,2048]{2,1,0:T(8,128)(2,1)S(1)}, u32[]{:S(2)}, u32[]{:S(2)}) collective-permute-start(bf16[2,128,2048]{2,1,0:T(8,128)(2,1)S(1)} %get-tuple-element.61), channel_id=1, source_target_pairs={{0,128},{128,0},{1,129},{129,1},{2,130},{130,2},{3,131},{131,3},{4... | collective-permute-start | bytes 3145736 | tf_op jit(solution)/shard_map/ppermute | solution.py:34
  97.3 2.6 %collective-permute-done.18.low_ref = bf16[672,128]{1,0:T(8,128)(2,1)S(1)} collective-permute-done((bf16[672,128]{1,0:T(8,128)(2,1)S(1)}, bf16[672,128]{1,0:T(8,128)(2,1)S(1)}, u32[]{:S(2)}, u32[]{:S(2)}) %collective-permute-start.18) | collective-permute-done | bytes 172064 | tf_op jit(solution)/shard_map/ppermute | solution.py:138
  99.9 1.1 far_rows_of.1
  101.0 2.2 %collective-permute-start.21 = (bf16[2,128,2048]{2,1,0:T(8,128)(2,1)S(1)}, bf16[2,128,2048]{2,1,0:T(8,128)(2,1)S(1)}, u32[]{:S(2)}, u32[]{:S(2)}) collective-permute-start(bf16[2,128,2048]{2,1,0:T(8,128)(2,1)S(1)} %get-tuple-element.62), channel_id=1, source_target_pairs={{0,128},{128,0},{1,129},{129,1},{2,130},{130,2},{3,131},{131,3},{4... | collective-permute-start | bytes 3145736 | tf_op jit(solution)/shard_map/ppermute | solution.py:34
  103.3 0.4 collective-permute-start.22
  103.7 1.8 %collective-permute-done.21.late_ref = bf16[2,128,2048]{2,1,0:T(8,128)(2,1)S(1)} collective-permute-done((bf16[2,128,2048]{2,1,0:T(8,128)(2,1)S(1)}, bf16[2,128,2048]{2,1,0:T(8,128)(2,1)S(1)}, u32[]{:S(2)}, u32[]{:S(2)}) %collective-permute-start.21) | collective-permute-done | bytes 1048608 | tf_op jit(solution)/shard_map/ppermute | solution.py:34
  105.5 0.4 late_quarters_of.1
  106.0 2.7 %collective-permute-start.24 = (bf16[2,64,2048]{2,1,0:T(8,128)(2,1)S(1)}, bf16[2,64,2048]{2,1,0:T(8,128)(2,1)S(1)}, u32[]{:S(2)}, u32[]{:S(2)}) collective-permute-start(bf16[2,64,2048]{2,1,0:T(8,128)(2,1)S(1)} %get-tuple-element.65), channel_id=1, source_target_pairs={{0,48},{128,131},{4,20},{132,133},{8,56},{136,139},{12,28},{140,14... | collective-permute-start | bytes 1572872 | tf_op jit(solution)/shard_map/ppermute | solution.py:169
  108.8 5.1 %weight_grads.1 = (bf16[448,2048]{1,0:T(8,128)(2,1)}, bf16[448,2048]{1,0:T(8,128)(2,1)}, bf16[448,2048]{1,0:T(8,128)(2,1)}) custom-call(bf16[4,1344,128]{2,1,0:T(8,128)(2,1)S(1)} %placed_of.1.b_ref, bf16[256,2048]{1,0:T(8,128)(2,1)S(1)} %stacked_of.2.own_ref.own_t, bf16[256,2048]{1,0:T(8,128)(2,1)S(1)} %collective-permute-done.3.other_ref.other_t, ...), custom_call_target="tpu_custom_call" | custom-call | flops 2818572288 | bytes 5505024 | tf_op jit(solution)/shard_map/weight_grads/pallas_call | solution.py:434
  113.9 4.9 %collective-permute-done.23.refs_2_ = bf16[2,64,2048]{2,1,0:T(8,128)(2,1)S(1)} collective-permute-done((bf16[2,64,2048]{2,1,0:T(8,128)(2,1)S(1)}, bf16[2,64,2048]{2,1,0:T(8,128)(2,1)S(1)}, u32[]{:S(2)}, u32[]{:S(2)}) %collective-permute-start.23) | collective-permute-done | bytes 524320 | tf_op jit(solution)/shard_map/ppermute | solution.py:169
  118.9 0.2 collected_of.1
  119.1 12.4 %all_to_all.11.parts_ref = bf16[8,16,2048]{2,1,0:T(8,128)(2,1)S(1)} all-to-all(bf16[8,16,2048]{2,1,0:T(8,128)(2,1)S(1)} %collected_of.1), channel_id=1, replica_groups={{0,1,2,3,64,65,66,67},{16,17,18,19,80,81,82,83},{32,33,34,35,96,97,98,9..., dimensions={0} | all-to-all | bytes 1048576 | tf_op jit(solution)/shard_map/all_to_all | solution.py:154
  131.5 0.7 totals_of.1
  (32 shorter events, 0.7 us)
Async XLA Ops:
  16.0 8.8 %collective-permute-start.2 = (bf16[64,2048]{1,0:T(8,128)(2,1)S(1)}, bf16[64,2048]{1,0:T(8,128)(2,1)S(1)}, u32[]{:S(2)}, u32[]{:S(2)}) collective-permute-start(bf16[64,2048]{1,0:T(8,128)(2,1)S(1)} %get-tuple-element.39.refs_0_), channel_id=1, source_target_pairs={{0,48},{128,131},{4,52},{132,135},{8,56},{136,139},{12,60},{140,14... | collective-permute-start | bytes 786440 | tf_op jit(solution)/shard_map/ppermute | solution.py:169
  18.6 6.8 %collective-permute-start.1 = (bf16[64,2048]{1,0:T(8,128)(2,1)S(1)}, bf16[64,2048]{1,0:T(8,128)(2,1)S(1)}, u32[]{:S(2)}, u32[]{:S(2)}) collective-permute-start(bf16[64,2048]{1,0:T(8,128)(2,1)S(1)} %get-tuple-element.39.refs_0_), channel_id=1, source_target_pairs={{0,32},{128,130},{4,36},{132,134},{8,40},{136,138},{12,44},{140,14... | collective-permute-start | bytes 786440 | tf_op jit(solution)/shard_map/ppermute | solution.py:169
  18.8 9.5 %collective-permute-start = (bf16[64,2048]{1,0:T(8,128)(2,1)S(1)}, bf16[64,2048]{1,0:T(8,128)(2,1)S(1)}, u32[]{:S(2)}, u32[]{:S(2)}) collective-permute-start(bf16[64,2048]{1,0:T(8,128)(2,1)S(1)} %get-tuple-element.39.refs_0_), channel_id=1, source_target_pairs={{0,16},{128,129},{4,20},{132,133},{8,24},{136,137},{12,28},{140,14... | collective-permute-start | bytes 786440 | tf_op jit(solution)/shard_map/ppermute | solution.py:169
  19.4 18.6 %copy-start.1 = (bf16[448,2048]{1,0:T(8,128)(2,1)S(1)}, bf16[448,2048]{1,0:T(8,128)(2,1)}, u32[]{:S(2)}) copy-start(bf16[448,2048]{1,0:T(8,128)(2,1)} %w0.3) | copy-start | bytes 5505028
  19.4 18.6 %copy-start.2 = (bf16[448,2048]{1,0:T(8,128)(2,1)S(1)}, bf16[448,2048]{1,0:T(8,128)(2,1)}, u32[]{:S(2)}) copy-start(bf16[448,2048]{1,0:T(8,128)(2,1)} %w1.3) | copy-start | bytes 5505028
  19.4 12.9 %collective-permute-start.8 = (bf16[64,2048]{1,0:T(8,128)(2,1)S(1)}, bf16[64,2048]{1,0:T(8,128)(2,1)S(1)}, u32[]{:S(2)}, u32[]{:S(2)}) collective-permute-start(bf16[64,2048]{1,0:T(8,128)(2,1)S(1)} %get-tuple-element.44.refs_0_), channel_id=1, source_target_pairs={{0,48},{128,131},{4,52},{132,135},{8,56},{136,139},{12,60},{140,14... | collective-permute-start | bytes 786440 | tf_op jit(solution)/shard_map/ppermute | solution.py:169
  21.5 10.9 %collective-permute-start.7 = (bf16[64,2048]{1,0:T(8,128)(2,1)S(1)}, bf16[64,2048]{1,0:T(8,128)(2,1)S(1)}, u32[]{:S(2)}, u32[]{:S(2)}) collective-permute-start(bf16[64,2048]{1,0:T(8,128)(2,1)S(1)} %get-tuple-element.44.refs_0_), channel_id=1, source_target_pairs={{0,32},{128,130},{4,36},{132,134},{8,40},{136,138},{12,44},{140,14... | collective-permute-start | bytes 786440 | tf_op jit(solution)/shard_map/ppermute | solution.py:169
  24.7 9.4 %collective-permute-start.6 = (bf16[64,2048]{1,0:T(8,128)(2,1)S(1)}, bf16[64,2048]{1,0:T(8,128)(2,1)S(1)}, u32[]{:S(2)}, u32[]{:S(2)}) collective-permute-start(bf16[64,2048]{1,0:T(8,128)(2,1)S(1)} %get-tuple-element.44.refs_0_), channel_id=1, source_target_pairs={{0,16},{128,129},{4,20},{132,133},{8,24},{136,137},{12,28},{140,14... | collective-permute-start | bytes 786440 | tf_op jit(solution)/shard_map/ppermute | solution.py:169
  28.4 9.6 %collective-permute-start.3 = (bf16[256,2048]{1,0:T(8,128)(2,1)S(1)}, bf16[256,2048]{1,0:T(8,128)(2,1)S(1)}, u32[]{:S(2)}, u32[]{:S(2)}) collective-permute-start(bf16[256,2048]{1,0:T(8,128)(2,1)S(1)} %stacked_of.2.own_ref.own_t), channel_id=1, source_target_pairs={{0,128},{128,0},{1,129},{129,1},{2,130},{130,2},{3,131},{131,3},{4... | collective-permute-start | bytes 3145736 | tf_op jit(solution)/shard_map/ppermute | solution.py:34
  34.2 11.5 %copy-start = (bf16[448,2048]{1,0:T(8,128)(2,1)S(1)}, bf16[448,2048]{1,0:T(8,128)(2,1)}, u32[]{:S(2)}) copy-start(bf16[448,2048]{1,0:T(8,128)(2,1)} %w2.3) | copy-start | bytes 5505028
  34.2 11.5 %collective-permute-start.9 = (bf16[256,2048]{1,0:T(8,128)(2,1)S(1)}, bf16[256,2048]{1,0:T(8,128)(2,1)S(1)}, u32[]{:S(2)}, u32[]{:S(2)}) collective-permute-start(bf16[256,2048]{1,0:T(8,128)(2,1)S(1)} %stacked_of.3.own_ref.own_g), channel_id=1, source_target_pairs={{0,128},{128,0},{1,129},{129,1},{2,130},{130,2},{3,131},{131,3},{4... | collective-permute-start | bytes 3145736 | tf_op jit(solution)/shard_map/ppermute | solution.py:34
  40.4 15.1 %collective-permute-start.4 = (bf16[896,128]{1,0:T(8,128)(2,1)S(1)}, bf16[896,128]{1,0:T(8,128)(2,1)S(1)}, u32[]{:S(2)}, u32[]{:S(2)}) collective-permute-start(bf16[896,128]{1,0:T(8,128)(2,1)S(1)} %get-tuple-element.40), channel_id=1, source_target_pairs={{0,4},{4,8},{8,12},{12,0},{1,5},{5,9},{9,13},{13,1},{2,6},{6,10},{... | collective-permute-start | bytes 688136 | tf_op jit(solution)/shard_map/ppermute | solution.py:138
  43.5 16.8 %collective-permute-start.5 = (bf16[896,128]{1,0:T(8,128)(2,1)S(1)}, bf16[896,128]{1,0:T(8,128)(2,1)S(1)}, u32[]{:S(2)}, u32[]{:S(2)}) collective-permute-start(bf16[896,128]{1,0:T(8,128)(2,1)S(1)} %get-tuple-element.41), channel_id=1, source_target_pairs={{0,12},{4,0},{8,4},{12,8},{1,13},{5,1},{9,5},{13,9},{2,14},{6,2},{... | collective-permute-start | bytes 688136 | tf_op jit(solution)/shard_map/ppermute | solution.py:138
  47.0 16.1 %collective-permute-start.12 = (bf16[448,128]{1,0:T(8,128)(2,1)S(1)}, bf16[448,128]{1,0:T(8,128)(2,1)S(1)}, u32[]{:S(2)}, u32[]{:S(2)}) collective-permute-start(bf16[448,128]{1,0:T(8,128)(2,1)S(1)} %get-tuple-element.45), channel_id=1, source_target_pairs={{0,4},{4,8},{8,12},{12,0},{1,5},{5,9},{9,13},{13,1},{2,6},{6,10},{... | collective-permute-start | bytes 344072 | tf_op jit(solution)/shard_map/ppermute | solution.py:138
  48.2 15.9 %collective-permute-start.13 = (bf16[448,128]{1,0:T(8,128)(2,1)S(1)}, bf16[448,128]{1,0:T(8,128)(2,1)S(1)}, u32[]{:S(2)}, u32[]{:S(2)}) collective-permute-start(bf16[448,128]{1,0:T(8,128)(2,1)S(1)} %get-tuple-element.46), channel_id=1, source_target_pairs={{0,12},{4,0},{8,4},{12,8},{1,13},{5,1},{9,5},{13,9},{2,14},{6,2},{... | collective-permute-start | bytes 344072 | tf_op jit(solution)/shard_map/ppermute | solution.py:138
  55.6 11.7 %collective-permute-start.10 = (bf16[448,128]{1,0:T(8,128)(2,1)S(1)}, bf16[448,128]{1,0:T(8,128)(2,1)S(1)}, u32[]{:S(2)}, u32[]{:S(2)}) collective-permute-start(bf16[448,128]{1,0:T(8,128)(2,1)S(1)} %joined_of.4), channel_id=1, source_target_pairs={{0,4},{4,8},{8,12},{12,0},{1,5},{5,9},{9,13},{13,1},{2,6},{6,10},{... | collective-permute-start | bytes 344072 | tf_op jit(solution)/shard_map/ppermute | solution.py:138
  60.3 9.5 %collective-permute-start.11 = (bf16[448,128]{1,0:T(8,128)(2,1)S(1)}, bf16[448,128]{1,0:T(8,128)(2,1)S(1)}, u32[]{:S(2)}, u32[]{:S(2)}) collective-permute-start(bf16[448,128]{1,0:T(8,128)(2,1)S(1)} %joined_of.5), channel_id=1, source_target_pairs={{0,12},{4,0},{8,4},{12,8},{1,13},{5,1},{9,5},{13,9},{2,14},{6,2},{... | collective-permute-start | bytes 344072 | tf_op jit(solution)/shard_map/ppermute | solution.py:138
  63.1 6.8 %collective-permute-start.14 = (bf16[224,128]{1,0:T(8,128)(2,1)S(1)}, bf16[224,128]{1,0:T(8,128)(2,1)S(1)}, u32[]{:S(2)}, u32[]{:S(2)}) collective-permute-start(bf16[224,128]{1,0:T(8,128)(2,1)S(1)} %joined_of.6), channel_id=1, source_target_pairs={{0,4},{4,8},{8,12},{12,0},{1,5},{5,9},{9,13},{13,1},{2,6},{6,10},{... | collective-permute-start | bytes 172040 | tf_op jit(solution)/shard_map/ppermute | solution.py:138
  64.1 7.2 %collective-permute-start.15 = (bf16[224,128]{1,0:T(8,128)(2,1)S(1)}, bf16[224,128]{1,0:T(8,128)(2,1)S(1)}, u32[]{:S(2)}, u32[]{:S(2)}) collective-permute-start(bf16[224,128]{1,0:T(8,128)(2,1)S(1)} %joined_of.7), channel_id=1, source_target_pairs={{0,12},{4,0},{8,4},{12,8},{1,13},{5,1},{9,5},{13,9},{2,14},{6,2},{... | collective-permute-start | bytes 172040 | tf_op jit(solution)/shard_map/ppermute | solution.py:138
  71.4 15.0 %collective-permute-start.17 = (bf16[1344,128]{1,0:T(8,128)(2,1)S(1)}, bf16[1344,128]{1,0:T(8,128)(2,1)S(1)}, u32[]{:S(2)}, u32[]{:S(2)}) collective-permute-start(bf16[1344,128]{1,0:T(8,128)(2,1)S(1)} %deltas_of.1.m_ref.mine_ref), channel_id=1, source_target_pairs={{0,12},{4,0},{8,4},{12,8},{1,13},{5,1},{9,5},{13,9},{2,14},{6,2},{... | collective-permute-start | bytes 1032200 | tf_op jit(solution)/shard_map/ppermute | solution.py:138
  72.7 18.1 %collective-permute-start.16 = (bf16[1344,128]{1,0:T(8,128)(2,1)S(1)}, bf16[1344,128]{1,0:T(8,128)(2,1)S(1)}, u32[]{:S(2)}, u32[]{:S(2)}) collective-permute-start(bf16[1344,128]{1,0:T(8,128)(2,1)S(1)} %deltas_of.1.m_ref.mine_ref), channel_id=1, source_target_pairs={{0,4},{4,8},{8,12},{12,0},{1,5},{5,9},{9,13},{13,1},{2,6},{6,10},{... | collective-permute-start | bytes 1032200 | tf_op jit(solution)/shard_map/ppermute | solution.py:138
  86.5 10.8 %collective-permute-start.19 = (bf16[672,128]{1,0:T(8,128)(2,1)S(1)}, bf16[672,128]{1,0:T(8,128)(2,1)S(1)}, u32[]{:S(2)}, u32[]{:S(2)}) collective-permute-start(bf16[672,128]{1,0:T(8,128)(2,1)S(1)} %slice.9), channel_id=1, source_target_pairs={{0,12},{4,0},{8,4},{12,8},{1,13},{5,1},{9,5},{13,9},{2,14},{6,2},{... | collective-permute-start | bytes 516104 | tf_op jit(solution)/shard_map/ppermute | solution.py:138
  90.9 9.0 %collective-permute-start.18 = (bf16[672,128]{1,0:T(8,128)(2,1)S(1)}, bf16[672,128]{1,0:T(8,128)(2,1)S(1)}, u32[]{:S(2)}, u32[]{:S(2)}) collective-permute-start(bf16[672,128]{1,0:T(8,128)(2,1)S(1)} %slice.8), channel_id=1, source_target_pairs={{0,4},{4,8},{8,12},{12,0},{1,5},{5,9},{9,13},{13,1},{2,6},{6,10},{... | collective-permute-start | bytes 516104 | tf_op jit(solution)/shard_map/ppermute | solution.py:138
  93.9 9.3 %collective-permute-start.20 = (bf16[2,128,2048]{2,1,0:T(8,128)(2,1)S(1)}, bf16[2,128,2048]{2,1,0:T(8,128)(2,1)S(1)}, u32[]{:S(2)}, u32[]{:S(2)}) collective-permute-start(bf16[2,128,2048]{2,1,0:T(8,128)(2,1)S(1)} %get-tuple-element.61), channel_id=1, source_target_pairs={{0,128},{128,0},{1,129},{129,1},{2,130},{130,2},{3,131},{131,3},{4... | collective-permute-start | bytes 3145736 | tf_op jit(solution)/shard_map/ppermute | solution.py:34
  101.0 4.5 %collective-permute-start.21 = (bf16[2,128,2048]{2,1,0:T(8,128)(2,1)S(1)}, bf16[2,128,2048]{2,1,0:T(8,128)(2,1)S(1)}, u32[]{:S(2)}, u32[]{:S(2)}) collective-permute-start(bf16[2,128,2048]{2,1,0:T(8,128)(2,1)S(1)} %get-tuple-element.62), channel_id=1, source_target_pairs={{0,128},{128,0},{1,129},{129,1},{2,130},{130,2},{3,131},{131,3},{4... | collective-permute-start | bytes 3145736 | tf_op jit(solution)/shard_map/ppermute | solution.py:34
  103.3 10.6 %collective-permute-start.22 = (bf16[2,64,2048]{2,1,0:T(8,128)(2,1)S(1)}, bf16[2,64,2048]{2,1,0:T(8,128)(2,1)S(1)}, u32[]{:S(2)}, u32[]{:S(2)}) collective-permute-start(bf16[2,64,2048]{2,1,0:T(8,128)(2,1)S(1)} %early_quarter_of.1), channel_id=1, source_target_pairs={{0,32},{128,130},{4,52},{132,135},{8,40},{136,138},{12,60},{140,14... | collective-permute-start | bytes 1572872 | tf_op jit(solution)/shard_map/ppermute | solution.py:169
  105.9 12.9 %collective-permute-start.23 = (bf16[2,64,2048]{2,1,0:T(8,128)(2,1)S(1)}, bf16[2,64,2048]{2,1,0:T(8,128)(2,1)S(1)}, u32[]{:S(2)}, u32[]{:S(2)}) collective-permute-start(bf16[2,64,2048]{2,1,0:T(8,128)(2,1)S(1)} %get-tuple-element.64), channel_id=1, source_target_pairs={{0,16},{128,129},{4,36},{132,134},{8,24},{136,137},{12,44},{140,14... | collective-permute-start | bytes 1572872 | tf_op jit(solution)/shard_map/ppermute | solution.py:169
  106.0 12.8 %collective-permute-start.24 = (bf16[2,64,2048]{2,1,0:T(8,128)(2,1)S(1)}, bf16[2,64,2048]{2,1,0:T(8,128)(2,1)S(1)}, u32[]{:S(2)}, u32[]{:S(2)}) collective-permute-start(bf16[2,64,2048]{2,1,0:T(8,128)(2,1)S(1)} %get-tuple-element.65), channel_id=1, source_target_pairs={{0,48},{128,131},{4,20},{132,133},{8,56},{136,139},{12,28},{140,14... | collective-permute-start | bytes 1572872 | tf_op jit(solution)/shard_map/ppermute | solution.py:169

commit v5 on v4

--- a/solution.py
+++ b/solution.py
@@ -208,37 +208,37 @@
 def deltas_from(hidden, gate_factor, up_factor, *parts):
     units, block = parts[-1].shape
 
-    def deltas_of(hidden_ref, gate_ref, up_ref, behind, ahead, low, high, mine, out_ref, total):
+    def deltas_of(hidden_ref, gate_ref, up_ref, behind, ahead, low, high, mine, low_out, high_out, total):
         block_sum(total, behind, ahead, low, high, mine)
-        out_ref[:units] = hidden_ref[...]
-        out_ref[units : 2 * units] = (total[...] * gate_ref[...]).astype(BF16)
-        out_ref[2 * units :] = (total[...] * up_ref[...]).astype(BF16)
+        rest = units // 2
+        gate = (total[...] * gate_ref[...]).astype(BF16)
+        low_out[:units] = hidden_ref[...]
+        low_out[units:] = gate[:rest]
+        high_out[:rest] = gate[rest:]
+        high_out[rest:] = (total[...] * up_ref[...]).astype(BF16)
 
     return local(
         deltas_of,
-        [((3 * units, block), BF16)],
+        [((3 * units // 2, block), BF16)] * 2,
         hidden,
         gate_factor,
         up_factor,
         *parts,
         scratch=[pltpu.VMEM((units, block), F32)],
-    )[0]
-
-
-def placed(mine, behind, ahead, low, high):
-    rows, block = mine.shape
-    part = rows // 2
-
-    def placed_of(mine_ref, behind_ref, ahead_ref, low_ref, high_ref, out_ref):
-        me = lax.axis_index("gy")
-        far = lax.rem(me + 2, WAYS)
-        out_ref[me] = mine_ref[...]
-        out_ref[lax.rem(me + 3, WAYS)] = behind_ref[...]
-        out_ref[lax.rem(me + 1, WAYS)] = ahead_ref[...]
-        out_ref[far, :part] = low_ref[...]
-        out_ref[far, part:] = high_ref[...]
-
-    return local(placed_of, [((WAYS, rows, block), BF16)], mine, behind, ahead, low, high)[0]
+    )
+
+
+def placed(*halves):
+    part, block = halves[0].shape
+
+    def placed_of(*refs):
+        me, out_ref = lax.axis_index("gy"), refs[-1]
+        for k, step in enumerate((0, 3, 1, 2)):
+            slot = lax.rem(me + step, WAYS)
+            out_ref[slot, :part] = refs[2 * k][...]
+            out_ref[slot, part:] = refs[2 * k + 1][...]
+
+    return local(placed_of, [((WAYS, 2 * part, block), BF16)], *halves)[0]
 
 
 def both_ways(forth, back):
@@ -263,11 +263,15 @@
         store(1, at, dot(1, gate) + dot(2, up))
 
 
-def near_rows(mine, behind, ahead, weights):
-    rows, block = mine.shape
+def near_rows(halves, weights):
+    part, block = halves[0].shape
     units, width = weights[0].shape
 
-    def near_rows_of(m_ref, b_ref, a_ref, w0, w1, w2, rows_ref, early_ref, held):
+    def near_rows_of(*refs):
+        (w0, w1, w2, rows_ref, early_ref, held, *whole), halves_of = refs[6:], refs[:6]
+        for k, ref in enumerate(whole):
+            ref[:part] = halves_of[2 * k][...]
+            ref[part:] = halves_of[2 * k + 1][...]
         me = lax.axis_index("gy")
         slots = [lax.rem(me + s, WAYS) for s in (0, 3, 1)]
 
@@ -275,17 +279,15 @@
             for k, slot in enumerate(slots):
                 rows_ref[slot, kind, :, at] = total[k * block : (k + 1) * block]
 
-        rows_into(held, (m_ref, b_ref, a_ref), (w0, w1, w2), store)
+        rows_into(held, whole, (w0, w1, w2), store)
         early_ref[...] = rows_ref[early_chunk(me)].astype(BF16)
 
     return local(
         near_rows_of,
         [((WAYS, 2, block, width), F32), ((2, block, width), BF16)],
-        mine,
-        behind,
-        ahead,
+        *halves,
         *weights,
-        scratch=[pltpu.VMEM((3, 3 * block, units), BF16)],
+        scratch=[pltpu.VMEM((3, 3 * block, units), BF16)] + [pltpu.VMEM((2 * part, block), BF16)] * 3,
         flops=18 * block * units * width,
     )
 
@@ -474,16 +476,17 @@
     hidden, *factors = activations(*near, *far, gate_up_mine)
     blocks = deltas_from(hidden, *factors, *hgrad_near, *hgrad_far, hgrad_mine)
     weights = (gate_weight, up_weight, down_weight)
-    mine = blocks
-    behind, ahead = both_ways(mine, mine)
-    part = mine.shape[0] // 2
-    far = both_ways(behind[:part], ahead[part:])
-    near, early = near_rows(mine, behind, ahead, weights)
+    low, high = blocks
+    low_behind, high_ahead = both_ways(low, high)
+    high_behind, low_ahead = both_ways(high, low)
+    far = both_ways(low_behind, high_ahead)
+    near_halves = (low, high, low_behind, high_behind, low_ahead, high_ahead)
+    near, early = near_rows(near_halves, weights)
     early = swapped(early)
     first = turned(early_quarter(near, early), -2, -1)
     far_own, late = far_rows(*far, weights, near)
     sums = late_quarters(near, far_own, early, swapped(late))
-    blocks = placed(after(mine, sums), behind, ahead, *far)
+    blocks = placed(after(low, sums), *near_halves[1:], *far)
     sums = [sums[0], first, turned(sums[1], -3, -2), turned(sums[2], -1, -3)]
     gate_grad, up_grad, down_grad = weight_grads(blocks, own_t, other_t, own_g, other_g, factor)
     sums[0] = after(sums[0], gate_grad)

time: 132 us -> 130 us (0.985)
  waiting for transfers between devices: 41.2 us -> 35.6 us
  blocking collectives: 26.9 us -> 28.9 us
  starting transfers between devices: 47.5 us -> 49 us
    ppermute x12 -> x14, waiting for transfers between devices: 27.4 us -> 21.2 us  [shifted(): return lax.ppermute(x, 'gy', [(i, (i + by) % n) for i in range(n)])]
    all_to_all x2, blocking collectives: 26.9 us -> 28.9 us  [first_exchange(): lax.all_to_all(x, CUBE, 0, 0, axis_index_groups=first_groups(), tiled=True)]
    ppermute x12 -> x14, starting transfers between devices: 24.1 us -> 25.2 us  [shifted(): return lax.ppermute(x, 'gy', [(i, (i + by) % n) for i in range(n)])]
  transfers between devices with their start and end apart: 25 -> 27, of which waited for: 14 -> 17; matrix products, arithmetic and copies ran while one was open for 0% -> 0% of each run, Pallas kernels for 11% -> 11%
where the time goes in v5:
time: 130 us
  starting transfers between devices  49 us (38%)
  waiting for transfers between devices  35.6 us (27%)
  blocking collectives  28.9 us (22%)
  Pallas kernels  15.8 us (12%)
    all_to_all x2, blocking collectives, first_exchange(): lax.all_to_all(x, CUBE, 0, 0, axis_index_groups=first_groups(), tiled=True)  28.9 us
    ppermute x14, starting transfers between devices, shifted(): return lax.ppermute(x, 'gy', [(i, (i + by) % n) for i in range(n)])  25.2 us
    ppermute x14, waiting for transfers between devices, shifted(): return lax.ppermute(x, 'gy', [(i, (i + by) % n) for i in range(n)])  21.2 us
    ppermute x4, starting transfers between devices, swapped(): return lax.ppermute(x, 'dcn', [(0, 1), (1, 0)])  12.9 us
    ppermute x9, waiting for transfers between devices, turned(): return lax.ppermute(x, ('dcn', 'gx', 'gy', 'gz'), pairs)  12.9 us
    ppermute x9, starting transfers between devices, turned(): return lax.ppermute(x, ('dcn', 'gx', 'gy', 'gz'), pairs)  10.9 us
    pallas_call x18, Pallas kernels, local(): pl.pallas_call(kernel, in_specs=[SMEM if a.dtype == jnp.int32 else VMEM f...  9.85 us
    pallas_call x1, Pallas kernels, weight_grads(): pl.pallas_call(weight_grads_of, grid=(width // WIDTH,), in_specs=[VMEM] +...  5.12 us
  transfers between devices with their start and end apart: 27, of which 17 were waited for; matrix products, arithmetic and copies ran while one was open for 0% of the time, Pallas kernels for 11%

profile of v5, /device:TPU:1, one launch (start us, length us, event | category | flops | bytes accessed | tf_op | source)
XLA Modules:
  0.0 130.0 jit_solution(4707320134425887172)
XLA Ops:
  0.6 0.8 copies.1
  1.5 14.5 %all_to_all.10.in_ref = bf16[8,16,2048]{2,1,0:T(8,128)(2,1)S(1)} all-to-all(bf16[8,16,2048]{2,1,0:T(8,128)(2,1)S(1)} %copies.1), channel_id=1, replica_groups={{0,1,2,3,64,65,66,67},{16,17,18,19,80,81,82,83},{32,33,34,35,96,97,98,9..., dimensions={0} | all-to-all | bytes 1048576 | tf_op jit(solution)/shard_map/all_to_all | solution.py:154
  16.0 2.6 %collective-permute-start.2 = (bf16[64,2048]{1,0:T(8,128)(2,1)S(1)}, bf16[64,2048]{1,0:T(8,128)(2,1)S(1)}, u32[]{:S(2)}, u32[]{:S(2)}) collective-permute-start(bf16[64,2048]{1,0:T(8,128)(2,1)S(1)} %get-tuple-element.41.refs_0_), channel_id=1, source_target_pairs={{0,48},{128,131},{4,52},{132,135},{8,56},{136,139},{12,60},{140,14... | collective-permute-start | bytes 786440 | tf_op jit(solution)/shard_map/ppermute | solution.py:169
  18.8 0.6 collective-permute-start
  19.4 2.0 %collective-permute-start.8 = (bf16[64,2048]{1,0:T(8,128)(2,1)S(1)}, bf16[64,2048]{1,0:T(8,128)(2,1)S(1)}, u32[]{:S(2)}, u32[]{:S(2)}) collective-permute-start(bf16[64,2048]{1,0:T(8,128)(2,1)S(1)} %get-tuple-element.46.refs_0_), channel_id=1, source_target_pairs={{0,48},{128,131},{4,52},{132,135},{8,56},{136,139},{12,60},{140,14... | collective-permute-start | bytes 786440 | tf_op jit(solution)/shard_map/ppermute | solution.py:169
  21.5 1.6 %collective-permute-start.7 = (bf16[64,2048]{1,0:T(8,128)(2,1)S(1)}, bf16[64,2048]{1,0:T(8,128)(2,1)S(1)}, u32[]{:S(2)}, u32[]{:S(2)}) collective-permute-start(bf16[64,2048]{1,0:T(8,128)(2,1)S(1)} %get-tuple-element.46.refs_0_), channel_id=1, source_target_pairs={{0,32},{128,130},{4,36},{132,134},{8,40},{136,138},{12,44},{140,14... | collective-permute-start | bytes 786440 | tf_op jit(solution)/shard_map/ppermute | solution.py:169
  23.0 1.7 %collective-permute-done.2.refs_3_ = bf16[64,2048]{1,0:T(8,128)(2,1)S(1)} collective-permute-done((bf16[64,2048]{1,0:T(8,128)(2,1)S(1)}, bf16[64,2048]{1,0:T(8,128)(2,1)S(1)}, u32[]{:S(2)}, u32[]{:S(2)}) %collective-permute-start.2) | collective-permute-done | bytes 262176 | tf_op jit(solution)/shard_map/ppermute | solution.py:169
  24.7 0.7 collective-permute-done.1.refs_2_
  25.4 2.9 %collective-permute-done.refs_1_ = bf16[64,2048]{1,0:T(8,128)(2,1)S(1)} collective-permute-done((bf16[64,2048]{1,0:T(8,128)(2,1)S(1)}, bf16[64,2048]{1,0:T(8,128)(2,1)S(1)}, u32[]{:S(2)}, u32[]{:S(2)}) %collective-permute-start) | collective-permute-done | bytes 262176 | tf_op jit(solution)/shard_map/ppermute | solution.py:169
  28.4 3.9 %collective-permute-start.3 = (bf16[256,2048]{1,0:T(8,128)(2,1)S(1)}, bf16[256,2048]{1,0:T(8,128)(2,1)S(1)}, u32[]{:S(2)}, u32[]{:S(2)}) collective-permute-start(bf16[256,2048]{1,0:T(8,128)(2,1)S(1)} %stacked_of.2.own_ref.own_t), channel_id=1, source_target_pairs={{0,128},{128,0},{1,129},{129,1},{2,130},{130,2},{3,131},{131,3},{4... | collective-permute-start | bytes 3145736 | tf_op jit(solution)/shard_map/ppermute | solution.py:34
  32.3 1.8 %collective-permute-done.6.refs_1_ = bf16[64,2048]{1,0:T(8,128)(2,1)S(1)} collective-permute-done((bf16[64,2048]{1,0:T(8,128)(2,1)S(1)}, bf16[64,2048]{1,0:T(8,128)(2,1)S(1)}, u32[]{:S(2)}, u32[]{:S(2)}) %collective-permute-start.6) | collective-permute-done | bytes 262176 | tf_op jit(solution)/shard_map/ppermute | solution.py:169
  34.2 3.8 %collective-permute-start.9 = (bf16[256,2048]{1,0:T(8,128)(2,1)S(1)}, bf16[256,2048]{1,0:T(8,128)(2,1)S(1)}, u32[]{:S(2)}, u32[]{:S(2)}) collective-permute-start(bf16[256,2048]{1,0:T(8,128)(2,1)S(1)} %stacked_of.3.own_ref.own_g), channel_id=1, source_target_pairs={{0,128},{128,0},{1,129},{129,1},{2,130},{130,2},{3,131},{131,3},{4... | collective-permute-start | bytes 3145736 | tf_op jit(solution)/shard_map/ppermute | solution.py:34
  38.0 2.4 %ring_blocks_of.2 = (bf16[896,128]{1,0:T(8,128)(2,1)S(1)}, bf16[896,128]{1,0:T(8,128)(2,1)S(1)}, f32[448,128]{1,0:T(8,128)S(1)}, f32[448,128]{1,0:T(8,128)S(1)}, f32[896,128]{1,0:T(8,128)S(1)}) custom-call(bf16[256,2048]{1,0:T(8,128)(2,1)S(1)} %stacked_of.2.own_ref.own_t, bf16[256,2048]{1,0:T(8,128)(2,1)S(1)} %collective-permute-done.3.other_ref.other_t, ...), custom_call_target="tpu_custom_call" | custom-call | flops 1879048192 | bytes 1000000 | tf_op jit(solution)/shard_map/ring_blocks_of/pallas_call | solution.py:21
  40.4 3.1 %collective-permute-start.4 = (bf16[896,128]{1,0:T(8,128)(2,1)S(1)}, bf16[896,128]{1,0:T(8,128)(2,1)S(1)}, u32[]{:S(2)}, u32[]{:S(2)}) collective-permute-start(bf16[896,128]{1,0:T(8,128)(2,1)S(1)} %get-tuple-element.42), channel_id=1, source_target_pairs={{0,4},{4,8},{8,12},{12,0},{1,5},{5,9},{9,13},{13,1},{2,6},{6,10},{... | collective-permute-start | bytes 688136 | tf_op jit(solution)/shard_map/ppermute | solution.py:138
  43.5 2.2 %collective-permute-start.5 = (bf16[896,128]{1,0:T(8,128)(2,1)S(1)}, bf16[896,128]{1,0:T(8,128)(2,1)S(1)}, u32[]{:S(2)}, u32[]{:S(2)}) collective-permute-start(bf16[896,128]{1,0:T(8,128)(2,1)S(1)} %get-tuple-element.43), channel_id=1, source_target_pairs={{0,12},{4,0},{8,4},{12,8},{1,13},{5,1},{9,5},{13,9},{2,14},{6,2},{... | collective-permute-start | bytes 688136 | tf_op jit(solution)/shard_map/ppermute | solution.py:138
  45.7 1.3 ring_blocks_of.3
  47.0 1.2 collective-permute-start.12
  48.2 2.5 %collective-permute-start.13 = (bf16[448,128]{1,0:T(8,128)(2,1)S(1)}, bf16[448,128]{1,0:T(8,128)(2,1)S(1)}, u32[]{:S(2)}, u32[]{:S(2)}) collective-permute-start(bf16[448,128]{1,0:T(8,128)(2,1)S(1)} %get-tuple-element.48), channel_id=1, source_target_pairs={{0,12},{4,0},{8,4},{12,8},{1,13},{5,1},{9,5},{13,9},{2,14},{6,2},{... | collective-permute-start | bytes 344072 | tf_op jit(solution)/shard_map/ppermute | solution.py:138
  50.6 4.9 %collective-permute-done.4.there_ref.behind = bf16[896,128]{1,0:T(8,128)(2,1)S(1)} collective-permute-done((bf16[896,128]{1,0:T(8,128)(2,1)S(1)}, bf16[896,128]{1,0:T(8,128)(2,1)S(1)}, u32[]{:S(2)}, u32[]{:S(2)}) %collective-permute-start.4) | collective-permute-done | bytes 229408 | tf_op jit(solution)/shard_map/ppermute | solution.py:138
  55.6 1.7 %collective-permute-start.10 = (bf16[448,128]{1,0:T(8,128)(2,1)S(1)}, bf16[448,128]{1,0:T(8,128)(2,1)S(1)}, u32[]{:S(2)}, u32[]{:S(2)}) collective-permute-start(bf16[448,128]{1,0:T(8,128)(2,1)S(1)} %joined_of.4), channel_id=1, source_target_pairs={{0,4},{4,8},{8,12},{12,0},{1,5},{5,9},{9,13},{13,1},{2,6},{6,10},{... | collective-permute-start | bytes 344072 | tf_op jit(solution)/shard_map/ppermute | solution.py:138
  57.2 3.1 %collective-permute-done.5.there_ref.ahead = bf16[896,128]{1,0:T(8,128)(2,1)S(1)} collective-permute-done((bf16[896,128]{1,0:T(8,128)(2,1)S(1)}, bf16[896,128]{1,0:T(8,128)(2,1)S(1)}, u32[]{:S(2)}, u32[]{:S(2)}) %collective-permute-start.5) | collective-permute-done | bytes 229408 | tf_op jit(solution)/shard_map/ppermute | solution.py:138
  60.3 2.5 %collective-permute-start.11 = (bf16[448,128]{1,0:T(8,128)(2,1)S(1)}, bf16[448,128]{1,0:T(8,128)(2,1)S(1)}, u32[]{:S(2)}, u32[]{:S(2)}) collective-permute-start(bf16[448,128]{1,0:T(8,128)(2,1)S(1)} %joined_of.5), channel_id=1, source_target_pairs={{0,12},{4,0},{8,4},{12,8},{1,13},{5,1},{9,5},{13,9},{2,14},{6,2},{... | collective-permute-start | bytes 344072 | tf_op jit(solution)/shard_map/ppermute | solution.py:138
  62.8 0.3 collective-permute-done.12.there_ref.behind
  63.1 1.0 collective-permute-start.14
  64.1 2.8 %collective-permute-start.15 = (bf16[224,128]{1,0:T(8,128)(2,1)S(1)}, bf16[224,128]{1,0:T(8,128)(2,1)S(1)}, u32[]{:S(2)}, u32[]{:S(2)}) collective-permute-start(bf16[224,128]{1,0:T(8,128)(2,1)S(1)} %joined_of.7), channel_id=1, source_target_pairs={{0,12},{4,0},{8,4},{12,8},{1,13},{5,1},{9,5},{13,9},{2,14},{6,2},{... | collective-permute-start | bytes 172040 | tf_op jit(solution)/shard_map/ppermute | solution.py:138
  66.9 0.4 collective-permute-done.10.low
  67.3 2.5 %collective-permute-done.11.high = bf16[448,128]{1,0:T(8,128)(2,1)S(1)} collective-permute-done((bf16[448,128]{1,0:T(8,128)(2,1)S(1)}, bf16[448,128]{1,0:T(8,128)(2,1)S(1)}, u32[]{:S(2)}, u32[]{:S(2)}) %collective-permute-start.11) | collective-permute-done | bytes 114720 | tf_op jit(solution)/shard_map/ppermute | solution.py:138
  69.9 1.4 %collective-permute-done.15.high = bf16[224,128]{1,0:T(8,128)(2,1)S(1)} collective-permute-done((bf16[224,128]{1,0:T(8,128)(2,1)S(1)}, bf16[224,128]{1,0:T(8,128)(2,1)S(1)}, u32[]{:S(2)}, u32[]{:S(2)}) %collective-permute-start.15) | collective-permute-done | bytes 57376 | tf_op jit(solution)/shard_map/ppermute | solution.py:138
  71.4 2.7 %collective-permute-start.16 = (bf16[672,128]{1,0:T(8,128)(2,1)S(1)}, bf16[672,128]{1,0:T(8,128)(2,1)S(1)}, u32[]{:S(2)}, u32[]{:S(2)}) collective-permute-start(bf16[672,128]{1,0:T(8,128)(2,1)S(1)} %get-tuple-element.70.refs_0_), channel_id=1, source_target_pairs={{0,4},{4,8},{8,12},{12,0},{1,5},{5,9},{9,13},{13,1},{2,6},{6,10},{... | collective-permute-start | bytes 516104 | tf_op jit(solution)/shard_map/ppermute | solution.py:138
  74.1 1.0 collective-permute-start.19
  75.1 2.3 %collective-permute-start.17 = (bf16[672,128]{1,0:T(8,128)(2,1)S(1)}, bf16[672,128]{1,0:T(8,128)(2,1)S(1)}, u32[]{:S(2)}, u32[]{:S(2)}) collective-permute-start(bf16[672,128]{1,0:T(8,128)(2,1)S(1)} %get-tuple-element.62.refs_1_), channel_id=1, source_target_pairs={{0,4},{4,8},{8,12},{12,0},{1,5},{5,9},{9,13},{13,1},{2,6},{6,10},{... | collective-permute-start | bytes 516104 | tf_op jit(solution)/shard_map/ppermute | solution.py:138
  77.4 2.5 %collective-permute-done.16.refs_2_ = bf16[672,128]{1,0:T(8,128)(2,1)S(1)} collective-permute-done((bf16[672,128]{1,0:T(8,128)(2,1)S(1)}, bf16[672,128]{1,0:T(8,128)(2,1)S(1)}, u32[]{:S(2)}, u32[]{:S(2)}) %collective-permute-start.16) | collective-permute-done | bytes 172064 | tf_op jit(solution)/shard_map/ppermute | solution.py:138
  80.0 0.8 collective-permute-start.20
  80.8 1.3 collective-permute-done.19.refs_5_
  82.0 1.5 %collective-permute-start.21 = (bf16[672,128]{1,0:T(8,128)(2,1)S(1)}, bf16[672,128]{1,0:T(8,128)(2,1)S(1)}, u32[]{:S(2)}, u32[]{:S(2)}) collective-permute-start(bf16[672,128]{1,0:T(8,128)(2,1)S(1)} %collective-permute-done.19.refs_5_), channel_id=1, source_target_pairs={{0,12},{4,0},{8,4},{12,8},{1,13},{5,1},{9,5},{13,9},{2,14},{6,2},{... | collective-permute-start | bytes 516104 | tf_op jit(solution)/shard_map/ppermute | solution.py:138
  83.5 4.9 %collective-permute-done.18.refs_4_ = bf16[672,128]{1,0:T(8,128)(2,1)S(1)} collective-permute-done((bf16[672,128]{1,0:T(8,128)(2,1)S(1)}, bf16[672,128]{1,0:T(8,128)(2,1)S(1)}, u32[]{:S(2)}, u32[]{:S(2)}) %collective-permute-start.18) | collective-permute-done | bytes 172064 | tf_op jit(solution)/shard_map/ppermute | solution.py:138
  88.4 3.0 %near_rows_of.1 = (f32[4,2,128,2048]{3,2,1,0:T(8,128)S(1)}, bf16[2,128,2048]{2,1,0:T(8,128)(2,1)S(1)}) custom-call(bf16[672,128]{1,0:T(8,128)(2,1)S(1)} %get-tuple-element.70.refs_0_, bf16[672,128]{1,0:T(8,128)(2,1)S(1)} %get-tuple-element.62.refs_1_, bf16[672,128]{1,0:T(8,128)(2,1)S(1)} %collective-permute-done.16.refs_2_, ...), custom_call_target="tpu_custom_call" | custom-call | flops 2113929216 | bytes 1000000 | tf_op jit(solution)/shard_map/near_rows_of/pallas_call | solution.py:21
  91.5 5.1 %collective-permute-start.22 = (bf16[2,128,2048]{2,1,0:T(8,128)(2,1)S(1)}, bf16[2,128,2048]{2,1,0:T(8,128)(2,1)S(1)}, u32[]{:S(2)}, u32[]{:S(2)}) collective-permute-start(bf16[2,128,2048]{2,1,0:T(8,128)(2,1)S(1)} %get-tuple-element.65), channel_id=1, source_target_pairs={{0,128},{128,0},{1,129},{129,1},{2,130},{130,2},{3,131},{131,3},{4... | collective-permute-start | bytes 3145736 | tf_op jit(solution)/shard_map/ppermute | solution.py:34
  96.6 1.1 far_rows_of.1
  97.8 1.0 collective-permute-done.22.early_ref
  99.0 1.0 collective-permute-start.24
  100.0 0.5 collective-permute-done.23.late_ref
  100.5 0.4 late_quarters_of.1
  101.1 2.5 %collective-permute-start.26 = (bf16[2,64,2048]{2,1,0:T(8,128)(2,1)S(1)}, bf16[2,64,2048]{2,1,0:T(8,128)(2,1)S(1)}, u32[]{:S(2)}, u32[]{:S(2)}) collective-permute-start(bf16[2,64,2048]{2,1,0:T(8,128)(2,1)S(1)} %get-tuple-element.69), channel_id=1, source_target_pairs={{0,48},{128,131},{4,20},{132,133},{8,56},{136,139},{12,28},{140,14... | collective-permute-start | bytes 1572872 | tf_op jit(solution)/shard_map/ppermute | solution.py:169
  103.8 5.1 %weight_grads.1 = (bf16[448,2048]{1,0:T(8,128)(2,1)}, bf16[448,2048]{1,0:T(8,128)(2,1)}, bf16[448,2048]{1,0:T(8,128)(2,1)}) custom-call(bf16[4,1344,128]{2,1,0:T(8,128)(2,1)S(1)} %placed_of.1.b_ref, bf16[256,2048]{1,0:T(8,128)(2,1)S(1)} %stacked_of.2.own_ref.own_t, bf16[256,2048]{1,0:T(8,128)(2,1)S(1)} %collective-permute-done.3.other_ref.other_t, ...), custom_call_target="tpu_custom_call" | custom-call | flops 2818572288 | bytes 5505024 | tf_op jit(solution)/shard_map/weight_grads/pallas_call | solution.py:436
  109.1 5.6 %collective-permute-done.25.refs_2_ = bf16[2,64,2048]{2,1,0:T(8,128)(2,1)S(1)} collective-permute-done((bf16[2,64,2048]{2,1,0:T(8,128)(2,1)S(1)}, bf16[2,64,2048]{2,1,0:T(8,128)(2,1)S(1)}, u32[]{:S(2)}, u32[]{:S(2)}) %collective-permute-start.25) | collective-permute-done | bytes 524320 | tf_op jit(solution)/shard_map/ppermute | solution.py:169
  114.9 14.4 %all_to_all.11.parts_ref = bf16[8,16,2048]{2,1,0:T(8,128)(2,1)S(1)} all-to-all(bf16[8,16,2048]{2,1,0:T(8,128)(2,1)S(1)} %collected_of.1), channel_id=1, replica_groups={{0,1,2,3,64,65,66,67},{16,17,18,19,80,81,82,83},{32,33,34,35,96,97,98,9..., dimensions={0} | all-to-all | bytes 1048576 | tf_op jit(solution)/shard_map/all_to_all | solution.py:154
  129.4 0.7 totals_of.1
  (34 shorter events, 1.7 us)
Async XLA Ops:
  16.0 8.8 %collective-permute-start.2 = (bf16[64,2048]{1,0:T(8,128)(2,1)S(1)}, bf16[64,2048]{1,0:T(8,128)(2,1)S(1)}, u32[]{:S(2)}, u32[]{:S(2)}) collective-permute-start(bf16[64,2048]{1,0:T(8,128)(2,1)S(1)} %get-tuple-element.41.refs_0_), channel_id=1, source_target_pairs={{0,48},{128,131},{4,52},{132,135},{8,56},{136,139},{12,60},{140,14... | collective-permute-start | bytes 786440 | tf_op jit(solution)/shard_map/ppermute | solution.py:169
  18.6 6.8 %collective-permute-start.1 = (bf16[64,2048]{1,0:T(8,128)(2,1)S(1)}, bf16[64,2048]{1,0:T(8,128)(2,1)S(1)}, u32[]{:S(2)}, u32[]{:S(2)}) collective-permute-start(bf16[64,2048]{1,0:T(8,128)(2,1)S(1)} %get-tuple-element.41.refs_0_), channel_id=1, source_target_pairs={{0,32},{128,130},{4,36},{132,134},{8,40},{136,138},{12,44},{140,14... | collective-permute-start | bytes 786440 | tf_op jit(solution)/shard_map/ppermute | solution.py:169
  18.8 9.5 %collective-permute-start = (bf16[64,2048]{1,0:T(8,128)(2,1)S(1)}, bf16[64,2048]{1,0:T(8,128)(2,1)S(1)}, u32[]{:S(2)}, u32[]{:S(2)}) collective-permute-start(bf16[64,2048]{1,0:T(8,128)(2,1)S(1)} %get-tuple-element.41.refs_0_), channel_id=1, source_target_pairs={{0,16},{128,129},{4,20},{132,133},{8,24},{136,137},{12,28},{140,14... | collective-permute-start | bytes 786440 | tf_op jit(solution)/shard_map/ppermute | solution.py:169
  19.4 18.6 %copy-start.1 = (bf16[448,2048]{1,0:T(8,128)(2,1)S(1)}, bf16[448,2048]{1,0:T(8,128)(2,1)}, u32[]{:S(2)}) copy-start(bf16[448,2048]{1,0:T(8,128)(2,1)} %w0.1) | copy-start | bytes 5505028
  19.4 18.6 %copy-start.2 = (bf16[448,2048]{1,0:T(8,128)(2,1)S(1)}, bf16[448,2048]{1,0:T(8,128)(2,1)}, u32[]{:S(2)}) copy-start(bf16[448,2048]{1,0:T(8,128)(2,1)} %w1.1) | copy-start | bytes 5505028
  19.4 12.9 %collective-permute-start.8 = (bf16[64,2048]{1,0:T(8,128)(2,1)S(1)}, bf16[64,2048]{1,0:T(8,128)(2,1)S(1)}, u32[]{:S(2)}, u32[]{:S(2)}) collective-permute-start(bf16[64,2048]{1,0:T(8,128)(2,1)S(1)} %get-tuple-element.46.refs_0_), channel_id=1, source_target_pairs={{0,48},{128,131},{4,52},{132,135},{8,56},{136,139},{12,60},{140,14... | collective-permute-start | bytes 786440 | tf_op jit(solution)/shard_map/ppermute | solution.py:169
  21.5 10.9 %collective-permute-start.7 = (bf16[64,2048]{1,0:T(8,128)(2,1)S(1)}, bf16[64,2048]{1,0:T(8,128)(2,1)S(1)}, u32[]{:S(2)}, u32[]{:S(2)}) collective-permute-start(bf16[64,2048]{1,0:T(8,128)(2,1)S(1)} %get-tuple-element.46.refs_0_), channel_id=1, source_target_pairs={{0,32},{128,130},{4,36},{132,134},{8,40},{136,138},{12,44},{140,14... | collective-permute-start | bytes 786440 | tf_op jit(solution)/shard_map/ppermute | solution.py:169
  24.7 9.4 %collective-permute-start.6 = (bf16[64,2048]{1,0:T(8,128)(2,1)S(1)}, bf16[64,2048]{1,0:T(8,128)(2,1)S(1)}, u32[]{:S(2)}, u32[]{:S(2)}) collective-permute-start(bf16[64,2048]{1,0:T(8,128)(2,1)S(1)} %get-tuple-element.46.refs_0_), channel_id=1, source_target_pairs={{0,16},{128,129},{4,20},{132,133},{8,24},{136,137},{12,28},{140,14... | collective-permute-start | bytes 786440 | tf_op jit(solution)/shard_map/ppermute | solution.py:169
  28.4 9.6 %collective-permute-start.3 = (bf16[256,2048]{1,0:T(8,128)(2,1)S(1)}, bf16[256,2048]{1,0:T(8,128)(2,1)S(1)}, u32[]{:S(2)}, u32[]{:S(2)}) collective-permute-start(bf16[256,2048]{1,0:T(8,128)(2,1)S(1)} %stacked_of.2.own_ref.own_t), channel_id=1, source_target_pairs={{0,128},{128,0},{1,129},{129,1},{2,130},{130,2},{3,131},{131,3},{4... | collective-permute-start | bytes 3145736 | tf_op jit(solution)/shard_map/ppermute | solution.py:34
  34.2 11.5 %copy-start = (bf16[448,2048]{1,0:T(8,128)(2,1)S(1)}, bf16[448,2048]{1,0:T(8,128)(2,1)}, u32[]{:S(2)}) copy-start(bf16[448,2048]{1,0:T(8,128)(2,1)} %w2.1) | copy-start | bytes 5505028
  34.2 11.5 %collective-permute-start.9 = (bf16[256,2048]{1,0:T(8,128)(2,1)S(1)}, bf16[256,2048]{1,0:T(8,128)(2,1)S(1)}, u32[]{:S(2)}, u32[]{:S(2)}) collective-permute-start(bf16[256,2048]{1,0:T(8,128)(2,1)S(1)} %stacked_of.3.own_ref.own_g), channel_id=1, source_target_pairs={{0,128},{128,0},{1,129},{129,1},{2,130},{130,2},{3,131},{131,3},{4... | collective-permute-start | bytes 3145736 | tf_op jit(solution)/shard_map/ppermute | solution.py:34
  40.4 15.1 %collective-permute-start.4 = (bf16[896,128]{1,0:T(8,128)(2,1)S(1)}, bf16[896,128]{1,0:T(8,128)(2,1)S(1)}, u32[]{:S(2)}, u32[]{:S(2)}) collective-permute-start(bf16[896,128]{1,0:T(8,128)(2,1)S(1)} %get-tuple-element.42), channel_id=1, source_target_pairs={{0,4},{4,8},{8,12},{12,0},{1,5},{5,9},{9,13},{13,1},{2,6},{6,10},{... | collective-permute-start | bytes 688136 | tf_op jit(solution)/shard_map/ppermute | solution.py:138
  43.5 16.8 %collective-permute-start.5 = (bf16[896,128]{1,0:T(8,128)(2,1)S(1)}, bf16[896,128]{1,0:T(8,128)(2,1)S(1)}, u32[]{:S(2)}, u32[]{:S(2)}) collective-permute-start(bf16[896,128]{1,0:T(8,128)(2,1)S(1)} %get-tuple-element.43), channel_id=1, source_target_pairs={{0,12},{4,0},{8,4},{12,8},{1,13},{5,1},{9,5},{13,9},{2,14},{6,2},{... | collective-permute-start | bytes 688136 | tf_op jit(solution)/shard_map/ppermute | solution.py:138
  47.0 16.1 %collective-permute-start.12 = (bf16[448,128]{1,0:T(8,128)(2,1)S(1)}, bf16[448,128]{1,0:T(8,128)(2,1)S(1)}, u32[]{:S(2)}, u32[]{:S(2)}) collective-permute-start(bf16[448,128]{1,0:T(8,128)(2,1)S(1)} %get-tuple-element.47), channel_id=1, source_target_pairs={{0,4},{4,8},{8,12},{12,0},{1,5},{5,9},{9,13},{13,1},{2,6},{6,10},{... | collective-permute-start | bytes 344072 | tf_op jit(solution)/shard_map/ppermute | solution.py:138
  48.2 15.9 %collective-permute-start.13 = (bf16[448,128]{1,0:T(8,128)(2,1)S(1)}, bf16[448,128]{1,0:T(8,128)(2,1)S(1)}, u32[]{:S(2)}, u32[]{:S(2)}) collective-permute-start(bf16[448,128]{1,0:T(8,128)(2,1)S(1)} %get-tuple-element.48), channel_id=1, source_target_pairs={{0,12},{4,0},{8,4},{12,8},{1,13},{5,1},{9,5},{13,9},{2,14},{6,2},{... | collective-permute-start | bytes 344072 | tf_op jit(solution)/shard_map/ppermute | solution.py:138
  55.6 11.7 %collective-permute-start.10 = (bf16[448,128]{1,0:T(8,128)(2,1)S(1)}, bf16[448,128]{1,0:T(8,128)(2,1)S(1)}, u32[]{:S(2)}, u32[]{:S(2)}) collective-permute-start(bf16[448,128]{1,0:T(8,128)(2,1)S(1)} %joined_of.4), channel_id=1, source_target_pairs={{0,4},{4,8},{8,12},{12,0},{1,5},{5,9},{9,13},{13,1},{2,6},{6,10},{... | collective-permute-start | bytes 344072 | tf_op jit(solution)/shard_map/ppermute | solution.py:138
  60.3 9.5 %collective-permute-start.11 = (bf16[448,128]{1,0:T(8,128)(2,1)S(1)}, bf16[448,128]{1,0:T(8,128)(2,1)S(1)}, u32[]{:S(2)}, u32[]{:S(2)}) collective-permute-start(bf16[448,128]{1,0:T(8,128)(2,1)S(1)} %joined_of.5), channel_id=1, source_target_pairs={{0,12},{4,0},{8,4},{12,8},{1,13},{5,1},{9,5},{13,9},{2,14},{6,2},{... | collective-permute-start | bytes 344072 | tf_op jit(solution)/shard_map/ppermute | solution.py:138
  63.1 6.8 %collective-permute-start.14 = (bf16[224,128]{1,0:T(8,128)(2,1)S(1)}, bf16[224,128]{1,0:T(8,128)(2,1)S(1)}, u32[]{:S(2)}, u32[]{:S(2)}) collective-permute-start(bf16[224,128]{1,0:T(8,128)(2,1)S(1)} %joined_of.6), channel_id=1, source_target_pairs={{0,4},{4,8},{8,12},{12,0},{1,5},{5,9},{9,13},{13,1},{2,6},{6,10},{... | collective-permute-start | bytes 172040 | tf_op jit(solution)/shard_map/ppermute | solution.py:138
  64.1 7.2 %collective-permute-start.15 = (bf16[224,128]{1,0:T(8,128)(2,1)S(1)}, bf16[224,128]{1,0:T(8,128)(2,1)S(1)}, u32[]{:S(2)}, u32[]{:S(2)}) collective-permute-start(bf16[224,128]{1,0:T(8,128)(2,1)S(1)} %joined_of.7), channel_id=1, source_target_pairs={{0,12},{4,0},{8,4},{12,8},{1,13},{5,1},{9,5},{13,9},{2,14},{6,2},{... | collective-permute-start | bytes 172040 | tf_op jit(solution)/shard_map/ppermute | solution.py:138
  71.4 8.6 %collective-permute-start.16 = (bf16[672,128]{1,0:T(8,128)(2,1)S(1)}, bf16[672,128]{1,0:T(8,128)(2,1)S(1)}, u32[]{:S(2)}, u32[]{:S(2)}) collective-permute-start(bf16[672,128]{1,0:T(8,128)(2,1)S(1)} %get-tuple-element.70.refs_0_), channel_id=1, source_target_pairs={{0,4},{4,8},{8,12},{12,0},{1,5},{5,9},{9,13},{13,1},{2,6},{6,10},{... | collective-permute-start | bytes 516104 | tf_op jit(solution)/shard_map/ppermute | solution.py:138
  74.1 8.0 %collective-permute-start.19 = (bf16[672,128]{1,0:T(8,128)(2,1)S(1)}, bf16[672,128]{1,0:T(8,128)(2,1)S(1)}, u32[]{:S(2)}, u32[]{:S(2)}) collective-permute-start(bf16[672,128]{1,0:T(8,128)(2,1)S(1)} %get-tuple-element.62.refs_1_), channel_id=1, source_target_pairs={{0,12},{4,0},{8,4},{12,8},{1,13},{5,1},{9,5},{13,9},{2,14},{6,2},{... | collective-permute-start | bytes 516104 | tf_op jit(solution)/shard_map/ppermute | solution.py:138
  75.0 13.4 %collective-permute-start.18 = (bf16[672,128]{1,0:T(8,128)(2,1)S(1)}, bf16[672,128]{1,0:T(8,128)(2,1)S(1)}, u32[]{:S(2)}, u32[]{:S(2)}) collective-permute-start(bf16[672,128]{1,0:T(8,128)(2,1)S(1)} %get-tuple-element.70.refs_0_), channel_id=1, source_target_pairs={{0,12},{4,0},{8,4},{12,8},{1,13},{5,1},{9,5},{13,9},{2,14},{6,2},{... | collective-permute-start | bytes 516104 | tf_op jit(solution)/shard_map/ppermute | solution.py:138
  75.1 13.4 %collective-permute-start.17 = (bf16[672,128]{1,0:T(8,128)(2,1)S(1)}, bf16[672,128]{1,0:T(8,128)(2,1)S(1)}, u32[]{:S(2)}, u32[]{:S(2)}) collective-permute-start(bf16[672,128]{1,0:T(8,128)(2,1)S(1)} %get-tuple-element.62.refs_1_), channel_id=1, source_target_pairs={{0,4},{4,8},{8,12},{12,0},{1,5},{5,9},{9,13},{13,1},{2,6},{6,10},{... | collective-permute-start | bytes 516104 | tf_op jit(solution)/shard_map/ppermute | solution.py:138
  80.0 16.6 %collective-permute-start.20 = (bf16[672,128]{1,0:T(8,128)(2,1)S(1)}, bf16[672,128]{1,0:T(8,128)(2,1)S(1)}, u32[]{:S(2)}, u32[]{:S(2)}) collective-permute-start(bf16[672,128]{1,0:T(8,128)(2,1)S(1)} %collective-permute-done.16.refs_2_), channel_id=1, source_target_pairs={{0,4},{4,8},{8,12},{12,0},{1,5},{5,9},{9,13},{13,1},{2,6},{6,10},{... | collective-permute-start | bytes 516104 | tf_op jit(solution)/shard_map/ppermute | solution.py:138
  82.0 14.6 %collective-permute-start.21 = (bf16[672,128]{1,0:T(8,128)(2,1)S(1)}, bf16[672,128]{1,0:T(8,128)(2,1)S(1)}, u32[]{:S(2)}, u32[]{:S(2)}) collective-permute-start(bf16[672,128]{1,0:T(8,128)(2,1)S(1)} %collective-permute-done.19.refs_5_), channel_id=1, source_target_pairs={{0,12},{4,0},{8,4},{12,8},{1,13},{5,1},{9,5},{13,9},{2,14},{6,2},{... | collective-permute-start | bytes 516104 | tf_op jit(solution)/shard_map/ppermute | solution.py:138
  91.5 7.4 %collective-permute-start.22 = (bf16[2,128,2048]{2,1,0:T(8,128)(2,1)S(1)}, bf16[2,128,2048]{2,1,0:T(8,128)(2,1)S(1)}, u32[]{:S(2)}, u32[]{:S(2)}) collective-permute-start(bf16[2,128,2048]{2,1,0:T(8,128)(2,1)S(1)} %get-tuple-element.65), channel_id=1, source_target_pairs={{0,128},{128,0},{1,129},{129,1},{2,130},{130,2},{3,131},{131,3},{4... | collective-permute-start | bytes 3145736 | tf_op jit(solution)/shard_map/ppermute | solution.py:34
  97.7 2.7 %collective-permute-start.23 = (bf16[2,128,2048]{2,1,0:T(8,128)(2,1)S(1)}, bf16[2,128,2048]{2,1,0:T(8,128)(2,1)S(1)}, u32[]{:S(2)}, u32[]{:S(2)}) collective-permute-start(bf16[2,128,2048]{2,1,0:T(8,128)(2,1)S(1)} %get-tuple-element.66), channel_id=1, source_target_pairs={{0,128},{128,0},{1,129},{129,1},{2,130},{130,2},{3,131},{131,3},{4... | collective-permute-start | bytes 3145736 | tf_op jit(solution)/shard_map/ppermute | solution.py:34
  99.0 10.2 %collective-permute-start.24 = (bf16[2,64,2048]{2,1,0:T(8,128)(2,1)S(1)}, bf16[2,64,2048]{2,1,0:T(8,128)(2,1)S(1)}, u32[]{:S(2)}, u32[]{:S(2)}) collective-permute-start(bf16[2,64,2048]{2,1,0:T(8,128)(2,1)S(1)} %early_quarter_of.1), channel_id=1, source_target_pairs={{0,32},{128,130},{4,52},{132,135},{8,40},{136,138},{12,60},{140,14... | collective-permute-start | bytes 1572872 | tf_op jit(solution)/shard_map/ppermute | solution.py:169
  100.9 13.8 %collective-permute-start.25 = (bf16[2,64,2048]{2,1,0:T(8,128)(2,1)S(1)}, bf16[2,64,2048]{2,1,0:T(8,128)(2,1)S(1)}, u32[]{:S(2)}, u32[]{:S(2)}) collective-permute-start(bf16[2,64,2048]{2,1,0:T(8,128)(2,1)S(1)} %get-tuple-element.68), channel_id=1, source_target_pairs={{0,16},{128,129},{4,36},{132,134},{8,24},{136,137},{12,44},{140,14... | collective-permute-start | bytes 1572872 | tf_op jit(solution)/shard_map/ppermute | solution.py:169
  101.1 13.6 %collective-permute-start.26 = (bf16[2,64,2048]{2,1,0:T(8,128)(2,1)S(1)}, bf16[2,64,2048]{2,1,0:T(8,128)(2,1)S(1)}, u32[]{:S(2)}, u32[]{:S(2)}) collective-permute-start(bf16[2,64,2048]{2,1,0:T(8,128)(2,1)S(1)} %get-tuple-element.69), channel_id=1, source_target_pairs={{0,48},{128,131},{4,20},{132,133},{8,56},{136,139},{12,28},{140,14... | collective-permute-start | bytes 1572872 | tf_op jit(solution)/shard_map/ppermute | solution.py:169

commit v6 on v5

--- a/solution.py
+++ b/solution.py
@@ -100,34 +100,38 @@
             held[2 * half + c, first : first + units] = sums[:, c * block : (c + 1) * block]
 
 
-def ring_blocks(own, other, weights):
+def ring_blocks(own, other, weights, earlier=()):
     count = len(weights)
     units, width = weights[0].shape
     rows = own.shape[0]
     block, part = rows // 2, count * units // 2
+    first = earlier[0].shape[0] if earlier else 0
 
     def ring_blocks_of(own_ref, other_ref, *refs):
-        w_refs = refs[:count]
-        forth, back, next_, before, mine, held = refs[count:]
+        w_refs, e_refs = refs[:count], refs[count : count + len(earlier)]
+        low, high, forth, back, next_, before, mine, held = refs[count + len(earlier) :]
         for k, w_ref in enumerate(w_refs):
             sums_into(held, k * units, w_ref, own_ref, other_ref)
         me = lax.axis_index("gy")
         after_, far, last = (lax.rem(me + s, WAYS) for s in (1, 2, 3))
-        forth[:part] = held[far, :part].astype(BF16)
-        forth[part:] = held[after_, part:].astype(BF16)
-        back[:part] = held[far, part:].astype(BF16)
-        back[part:] = held[last, :part].astype(BF16)
+        low[...] = held[far, :part].astype(BF16)
+        high[...] = held[far, part:].astype(BF16)
+        for out, ref in zip((forth, back), e_refs):
+            out[:first] = ref[...]
+        forth[first:] = held[after_, part:].astype(BF16)
+        back[first:] = held[last, :part].astype(BF16)
         next_[...] = held[after_, :part]
         before[...] = held[last, part:]
         mine[...] = held[me]
 
-    full = (2 * part, block)
+    half, full = (part, block), (2 * part, block)
     return local(
         ring_blocks_of,
-        [(full, BF16)] * 2 + [((part, block), F32)] * 2 + [(full, F32)],
+        [(half, BF16)] * 2 + [((first + part, block), BF16)] * 2 + [(half, F32)] * 2 + [(full, F32)],
         own,
         other,
         *weights,
+        *earlier,
         scratch=[pltpu.VMEM((WAYS,) + full, F32)],
         flops=4 * count * units * width * rows,
     )
@@ -173,15 +177,16 @@
     part, block = here.shape
 
     def joined_of(here_ref, there_ref, out_ref):
-        out_ref[...] = (here_ref[...] + there_ref[:part].astype(F32)).astype(BF16)
+        out_ref[...] = (here_ref[...] + there_ref[...].astype(F32)).astype(BF16)
 
     return local(joined_of, [((part, block), BF16)], here, there)[0]
 
 
-def block_sum(out, behind_ref, ahead_ref, low_ref, high_ref, mine_ref):
+def block_sum(out, first, behind_ref, ahead_ref, low_ref, high_ref, mine_ref):
     part = low_ref.shape[0]
-    out[:part] = mine_ref[:part] + low_ref[...].astype(F32) + ahead_ref[part:].astype(F32)
-    out[part:] = mine_ref[part:] + high_ref[...].astype(F32) + behind_ref[part:].astype(F32)
+    direct = slice(first, first + part)
+    out[:part] = mine_ref[:part] + low_ref[...].astype(F32) + ahead_ref[direct].astype(F32)
+    out[part:] = mine_ref[part:] + high_ref[...].astype(F32) + behind_ref[direct].astype(F32)
 
 
 def activations(*parts):
@@ -189,7 +194,7 @@
     units = rows // 2
 
     def activations_of(behind, ahead, low, high, mine, hidden_ref, gate_ref, up_ref, total):
-        block_sum(total, behind, ahead, low, high, mine)
+        block_sum(total, 0, behind, ahead, low, high, mine)
         gate, up = total[:units], total[units:]
         sigmoid = jax.nn.sigmoid(gate)
         hidden_ref[...] = (gate * sigmoid * up).astype(BF16)
@@ -209,7 +214,7 @@
     units, block = parts[-1].shape
 
     def deltas_of(hidden_ref, gate_ref, up_ref, behind, ahead, low, high, mine, low_out, high_out, total):
-        block_sum(total, behind, ahead, low, high, mine)
+        block_sum(total, behind.shape[0] - units // 2, behind, ahead, low, high, mine)
         rest = units // 2
         gate = (total[...] * gate_ref[...]).astype(BF16)
         low_out[:units] = hidden_ref[...]
@@ -459,22 +464,21 @@
     g_rows = [g_rows] + [turned(g_rows, k, k) for k in (1, 2, 3)]
     own_t, own_g = stacked(*t_rows), stacked(*g_rows)
     other_t = swapped(own_t)
-    *gate_up, gate_up_mine = ring_blocks(own_t, other_t, (gate_weight, up_weight))
+    gate_up = ring_blocks(own_t, other_t, (gate_weight, up_weight))
+    near = both_ways(*gate_up[:2])
     other_g = swapped(own_g)
-    *hgrad, hgrad_mine = ring_blocks(own_g, other_g, (down_weight,))
-
-    near = both_ways(*gate_up[:2])
+    hgrad = ring_blocks(own_g, other_g, (down_weight,), gate_up[2:4])
     hgrad_near = both_ways(*hgrad[:2])
-    gate_up[2], gate_up[3] = after((gate_up[2], gate_up[3]), hgrad)
-    low = joined(gate_up[2], near[0])
-    high = joined(gate_up[3], near[1])
+    direct = both_ways(*hgrad[2:4])
+
+    following, before = after(tuple(gate_up[4:6]), hgrad)
+    low, high = joined(following, near[0]), joined(before, near[1])
     far = both_ways(low, high)
-    hgrad_low = joined(after(hgrad[2], low, high), hgrad_near[0])
-    hgrad_high = joined(after(hgrad[3], low, high), hgrad_near[1])
+    following, before = after(tuple(hgrad[4:6]), low, high)
+    hgrad_low, hgrad_high = joined(following, hgrad_near[0]), joined(before, hgrad_near[1])
     hgrad_far = both_ways(hgrad_low, hgrad_high)
-    gate_up_mine = after(gate_up_mine, hgrad_low, hgrad_high)
-    hidden, *factors = activations(*near, *far, gate_up_mine)
-    blocks = deltas_from(hidden, *factors, *hgrad_near, *hgrad_far, hgrad_mine)
+    hidden, *factors = activations(*direct, *far, gate_up[6])
+    blocks = deltas_from(hidden, *factors, *direct, *hgrad_far, hgrad[6])
     weights = (gate_weight, up_weight, down_weight)
     low, high = blocks
     low_behind, high_ahead = both_ways(low, high)

time: 130 us -> 130 us (level)
  waiting for transfers between devices: 35.6 us -> 25.4 us
  starting transfers between devices: 49 us -> 55.5 us
  blocking collectives: 28.9 us -> 31.6 us
    ppermute x14 -> x16, waiting for transfers between devices: 21.2 us -> 12 us  [shifted(): return lax.ppermute(x, 'gy', [(i, (i + by) % n) for i in range(n)])]
    ppermute x14 -> x16, starting transfers between devices: 25.2 us -> 29.1 us  [shifted(): return lax.ppermute(x, 'gy', [(i, (i + by) % n) for i in range(n)])]
    ppermute x4, starting transfers between devices: 12.9 us -> 15.8 us  [swapped(): return lax.ppermute(x, 'dcn', [(0, 1), (1, 0)])]
    all_to_all x2, blocking collectives: 28.9 us -> 31.6 us  [first_exchange(): lax.all_to_all(x, CUBE, 0, 0, axis_index_groups=first_groups(), tiled=True)]
  transfers between devices with their start and end apart: 27 -> 29, of which waited for: 17 -> 14; matrix products, arithmetic and copies ran while one was open for 0% -> 0% of each run, Pallas kernels for 11% -> 11%
where the time goes in v6:
time: 130 us; the launch traced here: 129 us
  starting transfers between devices  55.5 us (43%)
  blocking collectives  31.6 us (24%)
  waiting for transfers between devices  25.4 us (20%)
  Pallas kernels  16 us (12%)
    all_to_all x2, blocking collectives, first_exchange(): lax.all_to_all(x, CUBE, 0, 0, axis_index_groups=first_groups(), tiled=True)  31.6 us
    ppermute x16, starting transfers between devices, shifted(): return lax.ppermute(x, 'gy', [(i, (i + by) % n) for i in range(n)])  29.1 us
    ppermute x4, starting transfers between devices, swapped(): return lax.ppermute(x, 'dcn', [(0, 1), (1, 0)])  15.8 us
    ppermute x16, waiting for transfers between devices, shifted(): return lax.ppermute(x, 'gy', [(i, (i + by) % n) for i in range(n)])  12 us
    ppermute x9, waiting for transfers between devices, turned(): return lax.ppermute(x, ('dcn', 'gx', 'gy', 'gz'), pairs)  12 us
    ppermute x9, starting transfers between devices, turned(): return lax.ppermute(x, ('dcn', 'gx', 'gy', 'gz'), pairs)  10.6 us
    pallas_call x18, Pallas kernels, local(): pl.pallas_call(kernel, in_specs=[SMEM if a.dtype == jnp.int32 else VMEM f...  10.1 us
    pallas_call x1, Pallas kernels, weight_grads(): pl.pallas_call(weight_grads_of, grid=(width // WIDTH,), in_specs=[VMEM] +...  5.12 us
  transfers between devices with their start and end apart: 29, of which 14 were waited for; matrix products, arithmetic and copies ran while one was open for 0% of the time, Pallas kernels for 11%

profile of v6, /device:TPU:1, one launch (start us, length us, event | category | flops | bytes accessed | tf_op | source)
XLA Modules:
  0.0 129.3 jit_solution(2142946843214647201)
XLA Ops:
  0.6 0.8 copies.1
  1.5 14.5 %all_to_all.10.in_ref = bf16[8,16,2048]{2,1,0:T(8,128)(2,1)S(1)} all-to-all(bf16[8,16,2048]{2,1,0:T(8,128)(2,1)S(1)} %copies.1), channel_id=1, replica_groups={{0,1,2,3,64,65,66,67},{16,17,18,19,80,81,82,83},{32,33,34,35,96,97,98,9..., dimensions={0} | all-to-all | bytes 1048576 | tf_op jit(solution)/shard_map/all_to_all | solution.py:158
  16.0 2.6 %collective-permute-start.6 = (bf16[64,2048]{1,0:T(8,128)(2,1)S(1)}, bf16[64,2048]{1,0:T(8,128)(2,1)S(1)}, u32[]{:S(2)}, u32[]{:S(2)}) collective-permute-start(bf16[64,2048]{1,0:T(8,128)(2,1)S(1)} %get-tuple-element.45.refs_0_), channel_id=1, source_target_pairs={{0,48},{128,131},{4,52},{132,135},{8,56},{136,139},{12,60},{140,14... | collective-permute-start | bytes 786440 | tf_op jit(solution)/shard_map/ppermute | solution.py:173
  18.8 0.6 collective-permute-start.4
  19.4 2.0 %collective-permute-start.2 = (bf16[64,2048]{1,0:T(8,128)(2,1)S(1)}, bf16[64,2048]{1,0:T(8,128)(2,1)S(1)}, u32[]{:S(2)}, u32[]{:S(2)}) collective-permute-start(bf16[64,2048]{1,0:T(8,128)(2,1)S(1)} %get-tuple-element.44.refs_0_), channel_id=1, source_target_pairs={{0,48},{128,131},{4,52},{132,135},{8,56},{136,139},{12,60},{140,14... | collective-permute-start | bytes 786440 | tf_op jit(solution)/shard_map/ppermute | solution.py:173
  21.5 1.6 %collective-permute-start.1 = (bf16[64,2048]{1,0:T(8,128)(2,1)S(1)}, bf16[64,2048]{1,0:T(8,128)(2,1)S(1)}, u32[]{:S(2)}, u32[]{:S(2)}) collective-permute-start(bf16[64,2048]{1,0:T(8,128)(2,1)S(1)} %get-tuple-element.44.refs_0_), channel_id=1, source_target_pairs={{0,32},{128,130},{4,36},{132,134},{8,40},{136,138},{12,44},{140,14... | collective-permute-start | bytes 786440 | tf_op jit(solution)/shard_map/ppermute | solution.py:173
  23.0 1.7 %collective-permute-done.6.refs_3_ = bf16[64,2048]{1,0:T(8,128)(2,1)S(1)} collective-permute-done((bf16[64,2048]{1,0:T(8,128)(2,1)S(1)}, bf16[64,2048]{1,0:T(8,128)(2,1)S(1)}, u32[]{:S(2)}, u32[]{:S(2)}) %collective-permute-start.6) | collective-permute-done | bytes 262176 | tf_op jit(solution)/shard_map/ppermute | solution.py:173
  24.7 0.7 collective-permute-done.5.refs_2_
  25.4 2.9 %collective-permute-done.4.refs_1_ = bf16[64,2048]{1,0:T(8,128)(2,1)S(1)} collective-permute-done((bf16[64,2048]{1,0:T(8,128)(2,1)S(1)}, bf16[64,2048]{1,0:T(8,128)(2,1)S(1)}, u32[]{:S(2)}, u32[]{:S(2)}) %collective-permute-start.4) | collective-permute-done | bytes 262176 | tf_op jit(solution)/shard_map/ppermute | solution.py:173
  28.4 3.9 %collective-permute-start.7 = (bf16[256,2048]{1,0:T(8,128)(2,1)S(1)}, bf16[256,2048]{1,0:T(8,128)(2,1)S(1)}, u32[]{:S(2)}, u32[]{:S(2)}) collective-permute-start(bf16[256,2048]{1,0:T(8,128)(2,1)S(1)} %stacked_of.3.own_ref.own_t), channel_id=1, source_target_pairs={{0,128},{128,0},{1,129},{129,1},{2,130},{130,2},{3,131},{131,3},{4... | collective-permute-start | bytes 3145736 | tf_op jit(solution)/shard_map/ppermute | solution.py:34
  32.3 1.8 %collective-permute-done.refs_1_ = bf16[64,2048]{1,0:T(8,128)(2,1)S(1)} collective-permute-done((bf16[64,2048]{1,0:T(8,128)(2,1)S(1)}, bf16[64,2048]{1,0:T(8,128)(2,1)S(1)}, u32[]{:S(2)}, u32[]{:S(2)}) %collective-permute-start) | collective-permute-done | bytes 262176 | tf_op jit(solution)/shard_map/ppermute | solution.py:173
  34.2 3.8 %collective-permute-start.3 = (bf16[256,2048]{1,0:T(8,128)(2,1)S(1)}, bf16[256,2048]{1,0:T(8,128)(2,1)S(1)}, u32[]{:S(2)}, u32[]{:S(2)}) collective-permute-start(bf16[256,2048]{1,0:T(8,128)(2,1)S(1)} %stacked_of.2.own_ref.own_g), channel_id=1, source_target_pairs={{0,128},{128,0},{1,129},{129,1},{2,130},{130,2},{3,131},{131,3},{4... | collective-permute-start | bytes 3145736 | tf_op jit(solution)/shard_map/ppermute | solution.py:34
  38.0 2.4 %ring_blocks_of.2 = (bf16[448,128]{1,0:T(8,128)(2,1)S(1)}, bf16[448,128]{1,0:T(8,128)(2,1)S(1)}, bf16[448,128]{1,0:T(8,128)(2,1)S(1)}, bf16[448,128]{1,0:T(8,128...) custom-call(bf16[256,2048]{1,0:T(8,128)(2,1)S(1)} %stacked_of.3.own_ref.own_t, ...), custom_call_target="tpu_custom_call" | custom-call | flops 1879048192 | bytes 1000000 | tf_op jit(solution)/shard_map/ring_blocks_of/pallas_call | solution.py:21
  40.4 3.1 %collective-permute-start.10 = (bf16[448,128]{1,0:T(8,128)(2,1)S(1)}, bf16[448,128]{1,0:T(8,128)(2,1)S(1)}, u32[]{:S(2)}, u32[]{:S(2)}) collective-permute-start(bf16[448,128]{1,0:T(8,128)(2,1)S(1)} %get-tuple-element.58), channel_id=1, source_target_pairs={{0,4},{4,8},{8,12},{12,0},{1,5},{5,9},{9,13},{13,1},{2,6},{6,10},{... | collective-permute-start | bytes 344072 | tf_op jit(solution)/shard_map/ppermute | solution.py:142
  43.5 2.2 %collective-permute-start.12 = (bf16[448,128]{1,0:T(8,128)(2,1)S(1)}, bf16[448,128]{1,0:T(8,128)(2,1)S(1)}, u32[]{:S(2)}, u32[]{:S(2)}) collective-permute-start(bf16[448,128]{1,0:T(8,128)(2,1)S(1)} %get-tuple-element.60), channel_id=1, source_target_pairs={{0,12},{4,0},{8,4},{12,8},{1,13},{5,1},{9,5},{13,9},{2,14},{6,2},{... | collective-permute-start | bytes 344072 | tf_op jit(solution)/shard_map/ppermute | solution.py:142
  45.7 1.3 ring_blocks_of.3
  47.0 1.2 collective-permute-start.8
  48.2 2.5 %collective-permute-start.9 = (bf16[672,128]{1,0:T(8,128)(2,1)S(1)}, bf16[672,128]{1,0:T(8,128)(2,1)S(1)}, u32[]{:S(2)}, u32[]{:S(2)}) collective-permute-start(bf16[672,128]{1,0:T(8,128)(2,1)S(1)} %get-tuple-element.49), channel_id=1, source_target_pairs={{0,12},{4,0},{8,4},{12,8},{1,13},{5,1},{9,5},{13,9},{2,14},{6,2},{... | collective-permute-start | bytes 516104 | tf_op jit(solution)/shard_map/ppermute | solution.py:142
  50.6 1.1 collective-permute-start.14
  51.7 1.2 collective-permute-done.12.there_ref
  52.9 2.5 %collective-permute-start.16 = (bf16[224,128]{1,0:T(8,128)(2,1)S(1)}, bf16[224,128]{1,0:T(8,128)(2,1)S(1)}, u32[]{:S(2)}, u32[]{:S(2)}) collective-permute-start(bf16[224,128]{1,0:T(8,128)(2,1)S(1)} %get-tuple-element.53), channel_id=1, source_target_pairs={{0,12},{4,0},{8,4},{12,8},{1,13},{5,1},{9,5},{13,9},{2,14},{6,2},{... | collective-permute-start | bytes 172040 | tf_op jit(solution)/shard_map/ppermute | solution.py:142
  55.4 1.3 collective-permute-start.13
  56.7 3.1 %collective-permute-done.14.there_ref = bf16[224,128]{1,0:T(8,128)(2,1)S(1)} collective-permute-done((bf16[224,128]{1,0:T(8,128)(2,1)S(1)}, bf16[224,128]{1,0:T(8,128)(2,1)S(1)}, u32[]{:S(2)}, u32[]{:S(2)}) %collective-permute-start.14) | collective-permute-done | bytes 57376 | tf_op jit(solution)/shard_map/ppermute | solution.py:142
  59.8 1.2 collective-permute-start.11
  61.0 4.4 %collective-permute-start.15 = (bf16[224,128]{1,0:T(8,128)(2,1)S(1)}, bf16[224,128]{1,0:T(8,128)(2,1)S(1)}, u32[]{:S(2)}, u32[]{:S(2)}) collective-permute-start(bf16[224,128]{1,0:T(8,128)(2,1)S(1)} %joined_of.6), channel_id=1, source_target_pairs={{0,4},{4,8},{8,12},{12,0},{1,5},{5,9},{9,13},{13,1},{2,6},{6,10},{... | collective-permute-start | bytes 172040 | tf_op jit(solution)/shard_map/ppermute | solution.py:142
  65.6 2.7 %collective-permute-done.11.low = bf16[448,128]{1,0:T(8,128)(2,1)S(1)} collective-permute-done((bf16[448,128]{1,0:T(8,128)(2,1)S(1)}, bf16[448,128]{1,0:T(8,128)(2,1)S(1)}, u32[]{:S(2)}, u32[]{:S(2)}) %collective-permute-start.11) | collective-permute-done | bytes 114720 | tf_op jit(solution)/shard_map/ppermute | solution.py:142
  68.5 1.1 collective-permute-done.15.low
  69.5 0.8 collective-permute-done.17.high
  70.4 1.5 %collective-permute-start.18 = (bf16[672,128]{1,0:T(8,128)(2,1)S(1)}, bf16[672,128]{1,0:T(8,128)(2,1)S(1)}, u32[]{:S(2)}, u32[]{:S(2)}) collective-permute-start(bf16[672,128]{1,0:T(8,128)(2,1)S(1)} %get-tuple-element.76.refs_0_), channel_id=1, source_target_pairs={{0,4},{4,8},{8,12},{12,0},{1,5},{5,9},{9,13},{13,1},{2,6},{6,10},{... | collective-permute-start | bytes 516104 | tf_op jit(solution)/shard_map/ppermute | solution.py:142
  71.9 2.1 %collective-permute-start.21 = (bf16[672,128]{1,0:T(8,128)(2,1)S(1)}, bf16[672,128]{1,0:T(8,128)(2,1)S(1)}, u32[]{:S(2)}, u32[]{:S(2)}) collective-permute-start(bf16[672,128]{1,0:T(8,128)(2,1)S(1)} %get-tuple-element.68.refs_1_), channel_id=1, source_target_pairs={{0,12},{4,0},{8,4},{12,8},{1,13},{5,1},{9,5},{13,9},{2,14},{6,2},{... | collective-permute-start | bytes 516104 | tf_op jit(solution)/shard_map/ppermute | solution.py:142
  74.1 2.3 %collective-permute-start.19 = (bf16[672,128]{1,0:T(8,128)(2,1)S(1)}, bf16[672,128]{1,0:T(8,128)(2,1)S(1)}, u32[]{:S(2)}, u32[]{:S(2)}) collective-permute-start(bf16[672,128]{1,0:T(8,128)(2,1)S(1)} %get-tuple-element.68.refs_1_), channel_id=1, source_target_pairs={{0,4},{4,8},{8,12},{12,0},{1,5},{5,9},{9,13},{13,1},{2,6},{6,10},{... | collective-permute-start | bytes 516104 | tf_op jit(solution)/shard_map/ppermute | solution.py:142
  76.4 0.7 collective-permute-done.18.refs_2_
  77.1 0.7 collective-permute-start.22
  77.9 2.9 %collective-permute-start.23 = (bf16[672,128]{1,0:T(8,128)(2,1)S(1)}, bf16[672,128]{1,0:T(8,128)(2,1)S(1)}, u32[]{:S(2)}, u32[]{:S(2)}) collective-permute-start(bf16[672,128]{1,0:T(8,128)(2,1)S(1)} %collective-permute-done.21.refs_5_), channel_id=1, source_target_pairs={{0,12},{4,0},{8,4},{12,8},{1,13},{5,1},{9,5},{13,9},{2,14},{6,2},{... | collective-permute-start | bytes 516104 | tf_op jit(solution)/shard_map/ppermute | solution.py:142
  80.7 0.7 collective-permute-done.20.refs_4_
  81.4 1.8 %collective-permute-done.19.refs_3_ = bf16[672,128]{1,0:T(8,128)(2,1)S(1)} collective-permute-done((bf16[672,128]{1,0:T(8,128)(2,1)S(1)}, bf16[672,128]{1,0:T(8,128)(2,1)S(1)}, u32[]{:S(2)}, u32[]{:S(2)}) %collective-permute-start.19) | collective-permute-done | bytes 172064 | tf_op jit(solution)/shard_map/ppermute | solution.py:142
  83.2 3.0 %near_rows_of.1 = (f32[4,2,128,2048]{3,2,1,0:T(8,128)S(1)}, bf16[2,128,2048]{2,1,0:T(8,128)(2,1)S(1)}) custom-call(bf16[672,128]{1,0:T(8,128)(2,1)S(1)} %get-tuple-element.76.refs_0_, bf16[672,128]{1,0:T(8,128)(2,1)S(1)} %get-tuple-element.68.refs_1_, bf16[672,128]{1,0:T(8,128)(2,1)S(1)} %collective-permute-done.18.refs_2_, ...), custom_call_target="tpu_custom_call" | custom-call | flops 2113929216 | bytes 1000000 | tf_op jit(solution)/shard_map/near_rows_of/pallas_call | solution.py:21
  86.2 4.5 %collective-permute-start.24 = (bf16[2,128,2048]{2,1,0:T(8,128)(2,1)S(1)}, bf16[2,128,2048]{2,1,0:T(8,128)(2,1)S(1)}, u32[]{:S(2)}, u32[]{:S(2)}) collective-permute-start(bf16[2,128,2048]{2,1,0:T(8,128)(2,1)S(1)} %get-tuple-element.71), channel_id=1, source_target_pairs={{0,128},{128,0},{1,129},{129,1},{2,130},{130,2},{3,131},{131,3},{4... | collective-permute-start | bytes 3145736 | tf_op jit(solution)/shard_map/ppermute | solution.py:34
  90.7 1.3 %far_rows_of.1 = (f32[2,128,2048]{2,1,0:T(8,128)S(1)}, bf16[2,128,2048]{2,1,0:T(8,128)(2,1)S(1)}) custom-call(bf16[672,128]{1,0:T(8,128)(2,1)S(1)} %collective-permute-done.22.low_ref.refs_6_, bf16[672,128]{1,0:T(8,128)(2,1)S(1)} %collective-permute-done.23.high_ref.refs_7_, bf16[448,2048]{1,0:T(8,128)(2,1)S(1)} %copy-done.1, ...), custom_call_target="tpu_custom_call" | custom-call | flops 704643072 | bytes 1000000 | tf_op jit(solution)/shard_map/far_rows_of/pallas_call | solution.py:21
  92.0 3.6 %collective-permute-start.25 = (bf16[2,128,2048]{2,1,0:T(8,128)(2,1)S(1)}, bf16[2,128,2048]{2,1,0:T(8,128)(2,1)S(1)}, u32[]{:S(2)}, u32[]{:S(2)}) collective-permute-start(bf16[2,128,2048]{2,1,0:T(8,128)(2,1)S(1)} %get-tuple-element.72), channel_id=1, source_target_pairs={{0,128},{128,0},{1,129},{129,1},{2,130},{130,2},{3,131},{131,3},{4... | collective-permute-start | bytes 3145736 | tf_op jit(solution)/shard_map/ppermute | solution.py:34
  95.7 0.8 collective-permute-start.26
  96.5 1.4 %collective-permute-done.25.late_ref = bf16[2,128,2048]{2,1,0:T(8,128)(2,1)S(1)} collective-permute-done((bf16[2,128,2048]{2,1,0:T(8,128)(2,1)S(1)}, bf16[2,128,2048]{2,1,0:T(8,128)(2,1)S(1)}, u32[]{:S(2)}, u32[]{:S(2)}) %collective-permute-start.25) | collective-permute-done | bytes 1048608 | tf_op jit(solution)/shard_map/ppermute | solution.py:34
  97.9 0.4 late_quarters_of.1
  98.4 2.7 %collective-permute-start.28 = (bf16[2,64,2048]{2,1,0:T(8,128)(2,1)S(1)}, bf16[2,64,2048]{2,1,0:T(8,128)(2,1)S(1)}, u32[]{:S(2)}, u32[]{:S(2)}) collective-permute-start(bf16[2,64,2048]{2,1,0:T(8,128)(2,1)S(1)} %get-tuple-element.75), channel_id=1, source_target_pairs={{0,48},{128,131},{4,20},{132,133},{8,56},{136,139},{12,28},{140,14... | collective-permute-start | bytes 1572872 | tf_op jit(solution)/shard_map/ppermute | solution.py:173
  101.2 5.1 %weight_grads.1 = (bf16[448,2048]{1,0:T(8,128)(2,1)}, bf16[448,2048]{1,0:T(8,128)(2,1)}, bf16[448,2048]{1,0:T(8,128)(2,1)}) custom-call(bf16[4,1344,128]{2,1,0:T(8,128)(2,1)S(1)} %placed_of.1.b_ref, bf16[256,2048]{1,0:T(8,128)(2,1)S(1)} %stacked_of.3.own_ref.own_t, bf16[256,2048]{1,0:T(8,128)(2,1)S(1)} %collective-permute-done.7.other_ref.other_t, ...), custom_call_target="tpu_custom_call" | custom-call | flops 2818572288 | bytes 5505024 | tf_op jit(solution)/shard_map/weight_grads/pallas_call | solution.py:441
  106.3 4.9 %collective-permute-done.27.refs_2_ = bf16[2,64,2048]{2,1,0:T(8,128)(2,1)S(1)} collective-permute-done((bf16[2,64,2048]{2,1,0:T(8,128)(2,1)S(1)}, bf16[2,64,2048]{2,1,0:T(8,128)(2,1)S(1)}, u32[]{:S(2)}, u32[]{:S(2)}) %collective-permute-start.27) | collective-permute-done | bytes 524320 | tf_op jit(solution)/shard_map/ppermute | solution.py:173
  111.5 17.2 %all_to_all.11.parts_ref = bf16[8,16,2048]{2,1,0:T(8,128)(2,1)S(1)} all-to-all(bf16[8,16,2048]{2,1,0:T(8,128)(2,1)S(1)} %collected_of.1), channel_id=1, replica_groups={{0,1,2,3,64,65,66,67},{16,17,18,19,80,81,82,83},{32,33,34,35,96,97,98,9..., dimensions={0} | all-to-all | bytes 1048576 | tf_op jit(solution)/shard_map/all_to_all | solution.py:158
  128.7 0.7 totals_of.1
  (38 shorter events, 1.4 us)
Async XLA Ops:
  16.0 8.8 %collective-permute-start.6 = (bf16[64,2048]{1,0:T(8,128)(2,1)S(1)}, bf16[64,2048]{1,0:T(8,128)(2,1)S(1)}, u32[]{:S(2)}, u32[]{:S(2)}) collective-permute-start(bf16[64,2048]{1,0:T(8,128)(2,1)S(1)} %get-tuple-element.45.refs_0_), channel_id=1, source_target_pairs={{0,48},{128,131},{4,52},{132,135},{8,56},{136,139},{12,60},{140,14... | collective-permute-start | bytes 786440 | tf_op jit(solution)/shard_map/ppermute | solution.py:173
  18.6 6.8 %collective-permute-start.5 = (bf16[64,2048]{1,0:T(8,128)(2,1)S(1)}, bf16[64,2048]{1,0:T(8,128)(2,1)S(1)}, u32[]{:S(2)}, u32[]{:S(2)}) collective-permute-start(bf16[64,2048]{1,0:T(8,128)(2,1)S(1)} %get-tuple-element.45.refs_0_), channel_id=1, source_target_pairs={{0,32},{128,130},{4,36},{132,134},{8,40},{136,138},{12,44},{140,14... | collective-permute-start | bytes 786440 | tf_op jit(solution)/shard_map/ppermute | solution.py:173
  18.8 9.5 %collective-permute-start.4 = (bf16[64,2048]{1,0:T(8,128)(2,1)S(1)}, bf16[64,2048]{1,0:T(8,128)(2,1)S(1)}, u32[]{:S(2)}, u32[]{:S(2)}) collective-permute-start(bf16[64,2048]{1,0:T(8,128)(2,1)S(1)} %get-tuple-element.45.refs_0_), channel_id=1, source_target_pairs={{0,16},{128,129},{4,20},{132,133},{8,24},{136,137},{12,28},{140,14... | collective-permute-start | bytes 786440 | tf_op jit(solution)/shard_map/ppermute | solution.py:173
  19.4 18.6 %copy-start.1 = (bf16[448,2048]{1,0:T(8,128)(2,1)S(1)}, bf16[448,2048]{1,0:T(8,128)(2,1)}, u32[]{:S(2)}) copy-start(bf16[448,2048]{1,0:T(8,128)(2,1)} %w0.1) | copy-start | bytes 5505028
  19.4 18.6 %copy-start.2 = (bf16[448,2048]{1,0:T(8,128)(2,1)S(1)}, bf16[448,2048]{1,0:T(8,128)(2,1)}, u32[]{:S(2)}) copy-start(bf16[448,2048]{1,0:T(8,128)(2,1)} %w1.1) | copy-start | bytes 5505028
  19.4 12.9 %collective-permute-start.2 = (bf16[64,2048]{1,0:T(8,128)(2,1)S(1)}, bf16[64,2048]{1,0:T(8,128)(2,1)S(1)}, u32[]{:S(2)}, u32[]{:S(2)}) collective-permute-start(bf16[64,2048]{1,0:T(8,128)(2,1)S(1)} %get-tuple-element.44.refs_0_), channel_id=1, source_target_pairs={{0,48},{128,131},{4,52},{132,135},{8,56},{136,139},{12,60},{140,14... | collective-permute-start | bytes 786440 | tf_op jit(solution)/shard_map/ppermute | solution.py:173
  21.5 10.9 %collective-permute-start.1 = (bf16[64,2048]{1,0:T(8,128)(2,1)S(1)}, bf16[64,2048]{1,0:T(8,128)(2,1)S(1)}, u32[]{:S(2)}, u32[]{:S(2)}) collective-permute-start(bf16[64,2048]{1,0:T(8,128)(2,1)S(1)} %get-tuple-element.44.refs_0_), channel_id=1, source_target_pairs={{0,32},{128,130},{4,36},{132,134},{8,40},{136,138},{12,44},{140,14... | collective-permute-start | bytes 786440 | tf_op jit(solution)/shard_map/ppermute | solution.py:173
  24.7 9.4 %collective-permute-start = (bf16[64,2048]{1,0:T(8,128)(2,1)S(1)}, bf16[64,2048]{1,0:T(8,128)(2,1)S(1)}, u32[]{:S(2)}, u32[]{:S(2)}) collective-permute-start(bf16[64,2048]{1,0:T(8,128)(2,1)S(1)} %get-tuple-element.44.refs_0_), channel_id=1, source_target_pairs={{0,16},{128,129},{4,20},{132,133},{8,24},{136,137},{12,28},{140,14... | collective-permute-start | bytes 786440 | tf_op jit(solution)/shard_map/ppermute | solution.py:173
  28.4 9.6 %collective-permute-start.7 = (bf16[256,2048]{1,0:T(8,128)(2,1)S(1)}, bf16[256,2048]{1,0:T(8,128)(2,1)S(1)}, u32[]{:S(2)}, u32[]{:S(2)}) collective-permute-start(bf16[256,2048]{1,0:T(8,128)(2,1)S(1)} %stacked_of.3.own_ref.own_t), channel_id=1, source_target_pairs={{0,128},{128,0},{1,129},{129,1},{2,130},{130,2},{3,131},{131,3},{4... | collective-permute-start | bytes 3145736 | tf_op jit(solution)/shard_map/ppermute | solution.py:34
  34.2 11.5 %copy-start = (bf16[448,2048]{1,0:T(8,128)(2,1)S(1)}, bf16[448,2048]{1,0:T(8,128)(2,1)}, u32[]{:S(2)}) copy-start(bf16[448,2048]{1,0:T(8,128)(2,1)} %w2.1) | copy-start | bytes 5505028
  34.2 11.5 %collective-permute-start.3 = (bf16[256,2048]{1,0:T(8,128)(2,1)S(1)}, bf16[256,2048]{1,0:T(8,128)(2,1)S(1)}, u32[]{:S(2)}, u32[]{:S(2)}) collective-permute-start(bf16[256,2048]{1,0:T(8,128)(2,1)S(1)} %stacked_of.2.own_ref.own_g), channel_id=1, source_target_pairs={{0,128},{128,0},{1,129},{129,1},{2,130},{130,2},{3,131},{131,3},{4... | collective-permute-start | bytes 3145736 | tf_op jit(solution)/shard_map/ppermute | solution.py:34
  40.4 15.0 %collective-permute-start.10 = (bf16[448,128]{1,0:T(8,128)(2,1)S(1)}, bf16[448,128]{1,0:T(8,128)(2,1)S(1)}, u32[]{:S(2)}, u32[]{:S(2)}) collective-permute-start(bf16[448,128]{1,0:T(8,128)(2,1)S(1)} %get-tuple-element.58), channel_id=1, source_target_pairs={{0,4},{4,8},{8,12},{12,0},{1,5},{5,9},{9,13},{13,1},{2,6},{6,10},{... | collective-permute-start | bytes 344072 | tf_op jit(solution)/shard_map/ppermute | solution.py:142
  43.5 9.4 %collective-permute-start.12 = (bf16[448,128]{1,0:T(8,128)(2,1)S(1)}, bf16[448,128]{1,0:T(8,128)(2,1)S(1)}, u32[]{:S(2)}, u32[]{:S(2)}) collective-permute-start(bf16[448,128]{1,0:T(8,128)(2,1)S(1)} %get-tuple-element.60), channel_id=1, source_target_pairs={{0,12},{4,0},{8,4},{12,8},{1,13},{5,1},{9,5},{13,9},{2,14},{6,2},{... | collective-permute-start | bytes 344072 | tf_op jit(solution)/shard_map/ppermute | solution.py:142
  47.0 18.4 %collective-permute-start.8 = (bf16[672,128]{1,0:T(8,128)(2,1)S(1)}, bf16[672,128]{1,0:T(8,128)(2,1)S(1)}, u32[]{:S(2)}, u32[]{:S(2)}) collective-permute-start(bf16[672,128]{1,0:T(8,128)(2,1)S(1)} %get-tuple-element.48), channel_id=1, source_target_pairs={{0,4},{4,8},{8,12},{12,0},{1,5},{5,9},{9,13},{13,1},{2,6},{6,10},{... | collective-permute-start | bytes 516104 | tf_op jit(solution)/shard_map/ppermute | solution.py:142
  48.2 17.4 %collective-permute-start.9 = (bf16[672,128]{1,0:T(8,128)(2,1)S(1)}, bf16[672,128]{1,0:T(8,128)(2,1)S(1)}, u32[]{:S(2)}, u32[]{:S(2)}) collective-permute-start(bf16[672,128]{1,0:T(8,128)(2,1)S(1)} %get-tuple-element.49), channel_id=1, source_target_pairs={{0,12},{4,0},{8,4},{12,8},{1,13},{5,1},{9,5},{13,9},{2,14},{6,2},{... | collective-permute-start | bytes 516104 | tf_op jit(solution)/shard_map/ppermute | solution.py:142
  50.6 9.1 %collective-permute-start.14 = (bf16[224,128]{1,0:T(8,128)(2,1)S(1)}, bf16[224,128]{1,0:T(8,128)(2,1)S(1)}, u32[]{:S(2)}, u32[]{:S(2)}) collective-permute-start(bf16[224,128]{1,0:T(8,128)(2,1)S(1)} %get-tuple-element.52), channel_id=1, source_target_pairs={{0,4},{4,8},{8,12},{12,0},{1,5},{5,9},{9,13},{13,1},{2,6},{6,10},{... | collective-permute-start | bytes 172040 | tf_op jit(solution)/shard_map/ppermute | solution.py:142
  52.9 8.1 %collective-permute-start.16 = (bf16[224,128]{1,0:T(8,128)(2,1)S(1)}, bf16[224,128]{1,0:T(8,128)(2,1)S(1)}, u32[]{:S(2)}, u32[]{:S(2)}) collective-permute-start(bf16[224,128]{1,0:T(8,128)(2,1)S(1)} %get-tuple-element.53), channel_id=1, source_target_pairs={{0,12},{4,0},{8,4},{12,8},{1,13},{5,1},{9,5},{13,9},{2,14},{6,2},{... | collective-permute-start | bytes 172040 | tf_op jit(solution)/shard_map/ppermute | solution.py:142
  55.4 10.1 %collective-permute-start.13 = (bf16[448,128]{1,0:T(8,128)(2,1)S(1)}, bf16[448,128]{1,0:T(8,128)(2,1)S(1)}, u32[]{:S(2)}, u32[]{:S(2)}) collective-permute-start(bf16[448,128]{1,0:T(8,128)(2,1)S(1)} %joined_of.5), channel_id=1, source_target_pairs={{0,12},{4,0},{8,4},{12,8},{1,13},{5,1},{9,5},{13,9},{2,14},{6,2},{... | collective-permute-start | bytes 344072 | tf_op jit(solution)/shard_map/ppermute | solution.py:142
  59.8 8.5 %collective-permute-start.11 = (bf16[448,128]{1,0:T(8,128)(2,1)S(1)}, bf16[448,128]{1,0:T(8,128)(2,1)S(1)}, u32[]{:S(2)}, u32[]{:S(2)}) collective-permute-start(bf16[448,128]{1,0:T(8,128)(2,1)S(1)} %joined_of.4), channel_id=1, source_target_pairs={{0,4},{4,8},{8,12},{12,0},{1,5},{5,9},{9,13},{13,1},{2,6},{6,10},{... | collective-permute-start | bytes 344072 | tf_op jit(solution)/shard_map/ppermute | solution.py:142
  61.0 8.5 %collective-permute-start.15 = (bf16[224,128]{1,0:T(8,128)(2,1)S(1)}, bf16[224,128]{1,0:T(8,128)(2,1)S(1)}, u32[]{:S(2)}, u32[]{:S(2)}) collective-permute-start(bf16[224,128]{1,0:T(8,128)(2,1)S(1)} %joined_of.6), channel_id=1, source_target_pairs={{0,4},{4,8},{8,12},{12,0},{1,5},{5,9},{9,13},{13,1},{2,6},{6,10},{... | collective-permute-start | bytes 172040 | tf_op jit(solution)/shard_map/ppermute | solution.py:142
  65.5 4.8 %collective-permute-start.17 = (bf16[224,128]{1,0:T(8,128)(2,1)S(1)}, bf16[224,128]{1,0:T(8,128)(2,1)S(1)}, u32[]{:S(2)}, u32[]{:S(2)}) collective-permute-start(bf16[224,128]{1,0:T(8,128)(2,1)S(1)} %joined_of.7), channel_id=1, source_target_pairs={{0,12},{4,0},{8,4},{12,8},{1,13},{5,1},{9,5},{13,9},{2,14},{6,2},{... | collective-permute-start | bytes 172040 | tf_op jit(solution)/shard_map/ppermute | solution.py:142
  70.4 6.8 %collective-permute-start.18 = (bf16[672,128]{1,0:T(8,128)(2,1)S(1)}, bf16[672,128]{1,0:T(8,128)(2,1)S(1)}, u32[]{:S(2)}, u32[]{:S(2)}) collective-permute-start(bf16[672,128]{1,0:T(8,128)(2,1)S(1)} %get-tuple-element.76.refs_0_), channel_id=1, source_target_pairs={{0,4},{4,8},{8,12},{12,0},{1,5},{5,9},{9,13},{13,1},{2,6},{6,10},{... | collective-permute-start | bytes 516104 | tf_op jit(solution)/shard_map/ppermute | solution.py:142
  71.9 5.9 %collective-permute-start.21 = (bf16[672,128]{1,0:T(8,128)(2,1)S(1)}, bf16[672,128]{1,0:T(8,128)(2,1)S(1)}, u32[]{:S(2)}, u32[]{:S(2)}) collective-permute-start(bf16[672,128]{1,0:T(8,128)(2,1)S(1)} %get-tuple-element.68.refs_1_), channel_id=1, source_target_pairs={{0,12},{4,0},{8,4},{12,8},{1,13},{5,1},{9,5},{13,9},{2,14},{6,2},{... | collective-permute-start | bytes 516104 | tf_op jit(solution)/shard_map/ppermute | solution.py:142
  74.0 7.3 %collective-permute-start.20 = (bf16[672,128]{1,0:T(8,128)(2,1)S(1)}, bf16[672,128]{1,0:T(8,128)(2,1)S(1)}, u32[]{:S(2)}, u32[]{:S(2)}) collective-permute-start(bf16[672,128]{1,0:T(8,128)(2,1)S(1)} %get-tuple-element.76.refs_0_), channel_id=1, source_target_pairs={{0,12},{4,0},{8,4},{12,8},{1,13},{5,1},{9,5},{13,9},{2,14},{6,2},{... | collective-permute-start | bytes 516104 | tf_op jit(solution)/shard_map/ppermute | solution.py:142
  74.1 9.0 %collective-permute-start.19 = (bf16[672,128]{1,0:T(8,128)(2,1)S(1)}, bf16[672,128]{1,0:T(8,128)(2,1)S(1)}, u32[]{:S(2)}, u32[]{:S(2)}) collective-permute-start(bf16[672,128]{1,0:T(8,128)(2,1)S(1)} %get-tuple-element.68.refs_1_), channel_id=1, source_target_pairs={{0,4},{4,8},{8,12},{12,0},{1,5},{5,9},{9,13},{13,1},{2,6},{6,10},{... | collective-permute-start | bytes 516104 | tf_op jit(solution)/shard_map/ppermute | solution.py:142
  77.1 13.6 %collective-permute-start.22 = (bf16[672,128]{1,0:T(8,128)(2,1)S(1)}, bf16[672,128]{1,0:T(8,128)(2,1)S(1)}, u32[]{:S(2)}, u32[]{:S(2)}) collective-permute-start(bf16[672,128]{1,0:T(8,128)(2,1)S(1)} %collective-permute-done.18.refs_2_), channel_id=1, source_target_pairs={{0,4},{4,8},{8,12},{12,0},{1,5},{5,9},{9,13},{13,1},{2,6},{6,10},{... | collective-permute-start | bytes 516104 | tf_op jit(solution)/shard_map/ppermute | solution.py:142
  77.9 12.8 %collective-permute-start.23 = (bf16[672,128]{1,0:T(8,128)(2,1)S(1)}, bf16[672,128]{1,0:T(8,128)(2,1)S(1)}, u32[]{:S(2)}, u32[]{:S(2)}) collective-permute-start(bf16[672,128]{1,0:T(8,128)(2,1)S(1)} %collective-permute-done.21.refs_5_), channel_id=1, source_target_pairs={{0,12},{4,0},{8,4},{12,8},{1,13},{5,1},{9,5},{13,9},{2,14},{6,2},{... | collective-permute-start | bytes 516104 | tf_op jit(solution)/shard_map/ppermute | solution.py:142
  86.2 9.4 %collective-permute-start.24 = (bf16[2,128,2048]{2,1,0:T(8,128)(2,1)S(1)}, bf16[2,128,2048]{2,1,0:T(8,128)(2,1)S(1)}, u32[]{:S(2)}, u32[]{:S(2)}) collective-permute-start(bf16[2,128,2048]{2,1,0:T(8,128)(2,1)S(1)} %get-tuple-element.71), channel_id=1, source_target_pairs={{0,128},{128,0},{1,129},{129,1},{2,130},{130,2},{3,131},{131,3},{4... | collective-permute-start | bytes 3145736 | tf_op jit(solution)/shard_map/ppermute | solution.py:34
  92.0 5.9 %collective-permute-start.25 = (bf16[2,128,2048]{2,1,0:T(8,128)(2,1)S(1)}, bf16[2,128,2048]{2,1,0:T(8,128)(2,1)S(1)}, u32[]{:S(2)}, u32[]{:S(2)}) collective-permute-start(bf16[2,128,2048]{2,1,0:T(8,128)(2,1)S(1)} %get-tuple-element.72), channel_id=1, source_target_pairs={{0,128},{128,0},{1,129},{129,1},{2,130},{130,2},{3,131},{131,3},{4... | collective-permute-start | bytes 3145736 | tf_op jit(solution)/shard_map/ppermute | solution.py:34
  95.7 10.6 %collective-permute-start.26 = (bf16[2,64,2048]{2,1,0:T(8,128)(2,1)S(1)}, bf16[2,64,2048]{2,1,0:T(8,128)(2,1)S(1)}, u32[]{:S(2)}, u32[]{:S(2)}) collective-permute-start(bf16[2,64,2048]{2,1,0:T(8,128)(2,1)S(1)} %early_quarter_of.1), channel_id=1, source_target_pairs={{0,32},{128,130},{4,52},{132,135},{8,40},{136,138},{12,60},{140,14... | collective-permute-start | bytes 1572872 | tf_op jit(solution)/shard_map/ppermute | solution.py:173
  98.3 12.9 %collective-permute-start.27 = (bf16[2,64,2048]{2,1,0:T(8,128)(2,1)S(1)}, bf16[2,64,2048]{2,1,0:T(8,128)(2,1)S(1)}, u32[]{:S(2)}, u32[]{:S(2)}) collective-permute-start(bf16[2,64,2048]{2,1,0:T(8,128)(2,1)S(1)} %get-tuple-element.74), channel_id=1, source_target_pairs={{0,16},{128,129},{4,36},{132,134},{8,24},{136,137},{12,44},{140,14... | collective-permute-start | bytes 1572872 | tf_op jit(solution)/shard_map/ppermute | solution.py:173
  98.4 12.8 %collective-permute-start.28 = (bf16[2,64,2048]{2,1,0:T(8,128)(2,1)S(1)}, bf16[2,64,2048]{2,1,0:T(8,128)(2,1)S(1)}, u32[]{:S(2)}, u32[]{:S(2)}) collective-permute-start(bf16[2,64,2048]{2,1,0:T(8,128)(2,1)S(1)} %get-tuple-element.75), channel_id=1, source_target_pairs={{0,48},{128,131},{4,20},{132,133},{8,56},{136,139},{12,28},{140,14... | collective-permute-start | bytes 1572872 | tf_op jit(solution)/shard_map/ppermute | solution.py:173
